TPU v7x, 256 devices: a whole 4x4x8 slice. The times are simulated.
256 devices in a mesh: dp: 16 (over z, core), seq: 16 (over y, x).
Axes of the slice: x: 4, y: 4, z: 8, core: 2. Of those that a mesh axis runs over, the one named last changes fastest.
Arguments:
- queries: bfloat16 [65536, 3584], P(('dp', 'seq')), may hold values from -25 to 25
- key_states: bfloat16 [65536, 512], P(('dp', 'seq')), may hold values from -6 to 6
- value_vectors: bfloat16 [65536, 512], P(('dp', 'seq')), may hold values from -6 to 6
- segment_ids: int32 [65536], P(('dp', 'seq')), may hold values from 0 to 156, as said below
Outputs:
- attended: bfloat16 [65536, 3584], P(('dp', 'seq'))
Inputs may be any that keep to these rules, and one draw needn't show every extreme that they name: `segment_ids`: segment ids never fall along the token order and take every value from min to max; the tokens of one segment lie within 9 consecutive blocks of 256 tokens, and in every draw some segment spans exactly 9 such blocks.
All inputs are finite; a program needn't handle non-finite values.
Results may differ from a plain program's by a relative error of at most 0.0031.
Values may be sent and summed in bfloat16 or wider, within the bound.
No kernel may reach another device: no remote copies, remote signals or barrier semaphores. Data moves between devices by JAX's collectives and lax.ppermute only.
A program may use at most 192 MiB of HBM per device.

v0:
```python
import jax
import jax.numpy as jnp
from jax import lax
from jax.sharding import PartitionSpec as P

QUERY_HEAD_COUNT = 28
KEY_VALUE_HEADS = 4
HEAD_WIDTH = 128
REACH = 8


def passed_along(value, axis, steps):
    count = lax.axis_size(axis)
    initial, last = (max(0, -steps), min(count, count - steps))
    return lax.ppermute(value, axis, [(source, source + steps) for source in range(initial, last)])


def attend_heads(queries, key_window, value_window, allowed):
    queries_per_group = QUERY_HEAD_COUNT // KEY_VALUE_HEADS
    row_count = queries.shape[0]
    scaling = 1.0 / HEAD_WIDTH**0.5
    outputs = []
    for current_head in range(KEY_VALUE_HEADS):
        query_heads = queries[
            :,
            current_head
            * queries_per_group
            * HEAD_WIDTH : (current_head + 1)
            * queries_per_group
            * HEAD_WIDTH,
        ]
        query_heads = query_heads.reshape(row_count, queries_per_group, HEAD_WIDTH)
        key_head = key_window[:, current_head * HEAD_WIDTH : (current_head + 1) * HEAD_WIDTH]
        value_head = value_window[:, current_head * HEAD_WIDTH : (current_head + 1) * HEAD_WIDTH]
        scores = (
            jnp.einsum("tgd,sd->gts", query_heads, key_head, preferred_element_type=jnp.float32)
            * scaling
        )
        scores = jnp.where(allowed[None], scores, -jnp.inf)
        largest = jnp.max(scores, axis=2, keepdims=True)
        weights = jnp.exp(scores - largest)
        totals = jnp.sum(weights, axis=2, keepdims=True)
        mixture = jnp.einsum(
            "gts,sd->tgd",
            weights.astype(jnp.bfloat16),
            value_head,
            preferred_element_type=jnp.float32,
        )
        mixture = mixture / jnp.transpose(totals, (1, 0, 2))
        outputs.append(mixture.reshape(row_count, queries_per_group * HEAD_WIDTH))
    return jnp.concatenate(outputs, axis=1).astype(jnp.bfloat16)


def per_device(queries, key_states, value_vectors, segment_ids):
    row_count = queries.shape[0]
    local_block = (key_states, value_vectors, segment_ids)
    shifted_all = [local_block]
    for distance in range(1, REACH + 1):
        shifted_all.insert(
            0,
            passed_along((local_block[0], local_block[1], local_block[2]), ("dp", "seq"), distance),
        )
    window = tuple(
        (
            jnp.concatenate([shifted[member] for shifted in shifted_all], axis=0)
            for member in range(3)
        )
    )
    key_window, value_window, segment_window = window
    device = lax.axis_index(("dp", "seq"))
    first_row = device * row_count
    query_place = first_row + jnp.arange(row_count, dtype=jnp.int32)
    window_place = (
        first_row - REACH * row_count + jnp.arange((REACH + 1) * row_count, dtype=jnp.int32)
    )
    allowed = (
        (segment_ids[:, None] == segment_window[None, :])
        & (window_place[None, :] <= query_place[:, None])
        & (window_place[None, :] >= 0)
    )
    return attend_heads(queries, key_window, value_window, allowed)


def solution(mesh):
    in_specs = (
        P(("dp", "seq"), None),
        P(("dp", "seq"), None),
        P(("dp", "seq"), None),
        P(("dp", "seq")),
    )
    out_specs = P(("dp", "seq"), None)
    return jax.shard_map(
        per_device, mesh=mesh, in_specs=in_specs, out_specs=out_specs, check_vma=False
    )
```

profile of v0, /device:TPU:97, one launch (start us, length us, event | category | flops | bytes accessed | tf_op | source)
XLA Modules:
  0.0 270.7 jit_solution(5630485090679978028)
XLA Ops:
  0.0 4.8 %collective-permute-start.14 = (s32[256]{0:T(256)}, s32[256]{0:T(256)S(1)}, u32[]{:S(2)}, u32[]{:S(2)}) collective-permute-start(s32[256]{0:T(256)} %param.7), channel_id=1, source_target_pairs={{0,2},{1,3},{2,4},{3,5},{4,6},{5,7},{6,8},{7,9},{8,10},{9,11},{10,... | collective-permute-start | bytes 3080 | tf_op jit(solution)/shard_map/ppermute | solution.py:15
  4.8 3.8 %collective-permute-start.13 = (s32[256]{0:T(256)}, s32[256]{0:T(256)S(1)}, u32[]{:S(2)}, u32[]{:S(2)}) collective-permute-start(s32[256]{0:T(256)} %param.7), channel_id=1, source_target_pairs={{0,3},{1,4},{2,5},{3,6},{4,7},{5,8},{6,9},{7,10},{8,11},{9,12},{10... | collective-permute-start | bytes 3080 | tf_op jit(solution)/shard_map/ppermute | solution.py:15
  8.6 3.2 %collective-permute-start.12 = (s32[256]{0:T(256)}, s32[256]{0:T(256)S(1)}, u32[]{:S(2)}, u32[]{:S(2)}) collective-permute-start(s32[256]{0:T(256)} %param.7), channel_id=1, source_target_pairs={{0,4},{1,5},{2,6},{3,7},{4,8},{5,9},{6,10},{7,11},{8,12},{9,13},{1... | collective-permute-start | bytes 3080 | tf_op jit(solution)/shard_map/ppermute | solution.py:15
  11.8 3.2 %collective-permute-start.11 = (s32[256]{0:T(256)}, s32[256]{0:T(256)S(1)}, u32[]{:S(2)}, u32[]{:S(2)}) collective-permute-start(s32[256]{0:T(256)} %param.7), channel_id=1, source_target_pairs={{0,5},{1,6},{2,7},{3,8},{4,9},{5,10},{6,11},{7,12},{8,13},{9,14},{... | collective-permute-start | bytes 3080 | tf_op jit(solution)/shard_map/ppermute | solution.py:15
  15.0 7.2 %collective-permute-start.8 = (s32[256]{0:T(256)}, s32[256]{0:T(256)S(1)}, u32[]{:S(2)}, u32[]{:S(2)}) collective-permute-start(s32[256]{0:T(256)} %param.7), channel_id=1, source_target_pairs={{0,8},{1,9},{2,10},{3,11},{4,12},{5,13},{6,14},{7,15},{8,16},{9,17... | collective-permute-start | bytes 3080 | tf_op jit(solution)/shard_map/ppermute | solution.py:15
  22.2 1.6 fusion.72
  23.8 1.1 copy.22
  24.9 0.2 copy.57
  25.1 0.2 copy.56
  25.4 0.2 copy.55
  25.6 0.2 copy.58
  25.8 0.0 collective-permute-done.8
  25.8 5.4 %collective-permute-start.9 = (s32[256]{0:T(256)S(1)}, s32[256]{0:T(256)S(1)}, u32[]{:S(2)}, u32[]{:S(2)}) collective-permute-start(s32[256]{0:T(256)S(1)} %copy-done.2), channel_id=1, source_target_pairs={{0,7},{1,8},{2,9},{3,10},{4,11},{5,12},{6,13},{7,14},{8,15},{9,16}... | collective-permute-start | bytes 3080 | tf_op jit(solution)/shard_map/ppermute | solution.py:15
  31.2 1.9 collective-permute-done.9
  33.1 3.5 %collective-permute-start.10 = (s32[256]{0:T(256)S(1)}, s32[256]{0:T(256)S(1)}, u32[]{:S(2)}, u32[]{:S(2)}) collective-permute-start(s32[256]{0:T(256)S(1)} %copy-done.2), channel_id=1, source_target_pairs={{0,6},{1,7},{2,8},{3,9},{4,10},{5,11},{6,12},{7,13},{8,14},{9,15},... | collective-permute-start | bytes 3080 | tf_op jit(solution)/shard_map/ppermute | solution.py:15
  36.7 5.2 %collective-permute-done.10 = s32[256]{0:T(256)S(1)} collective-permute-done((s32[256]{0:T(256)S(1)}, s32[256]{0:T(256)S(1)}, u32[]{:S(2)}, u32[]{:S(2)}) %collective-permute-start.10) | collective-permute-done | bytes 1056 | tf_op jit(solution)/shard_map/ppermute | solution.py:15
  41.9 2.2 collective-permute-start.15
  44.1 0.0 collective-permute-done.11
  44.1 2.2 collective-permute-start.7
  46.4 0.0 collective-permute-done.12
  46.4 5.9 %collective-permute-start.6 = (bf16[256,512]{0,1:T(8,128)(2,1)S(1)}, bf16[256,512]{0,1:T(8,128)(2,1)S(1)}, u32[]{:S(2)}, u32[]{:S(2)}) collective-permute-start(bf16[256,512]{0,1:T(8,128)(2,1)S(1)} %copy.22), channel_id=1, source_target_pairs={{0,2},{1,3},{2,4},{3,5},{4,6},{5,7},{6,8},{7,9},{8,10},{9,11},{10,... | collective-permute-start | bytes 786440 | tf_op jit(solution)/shard_map/ppermute | solution.py:15
  52.3 0.0 collective-permute-done.13
  52.3 2.8 %collective-permute-start.18 = (bf16[256,512]{1,0:T(8,128)(2,1)S(1)}, bf16[256,512]{1,0:T(8,128)(2,1)S(1)}, u32[]{:S(2)}, u32[]{:S(2)}) collective-permute-start(bf16[256,512]{1,0:T(8,128)(2,1)S(1)} %copy-done), channel_id=1, source_target_pairs={{0,6},{1,7},{2,8},{3,9},{4,10},{5,11},{6,12},{7,13},{8,14},{9,15},... | collective-permute-start | bytes 786440 | tf_op jit(solution)/shard_map/ppermute | solution.py:15
  55.2 11.4 %collective-permute-start.17 = (bf16[256,512]{1,0:T(8,128)(2,1)S(1)}, bf16[256,512]{1,0:T(8,128)(2,1)S(1)}, u32[]{:S(2)}, u32[]{:S(2)}) collective-permute-start(bf16[256,512]{1,0:T(8,128)(2,1)S(1)} %copy-done), channel_id=1, source_target_pairs={{0,7},{1,8},{2,9},{3,10},{4,11},{5,12},{6,13},{7,14},{8,15},{9,16}... | collective-permute-start | bytes 786440 | tf_op jit(solution)/shard_map/ppermute | solution.py:15
  66.6 0.0 collective-permute-done.15
  66.6 3.1 %collective-permute-start.16 = (bf16[256,512]{1,0:T(8,128)(2,1)S(1)}, bf16[256,512]{1,0:T(8,128)(2,1)S(1)}, u32[]{:S(2)}, u32[]{:S(2)}) collective-permute-start(bf16[256,512]{1,0:T(8,128)(2,1)S(1)} %copy-done), channel_id=1, source_target_pairs={{0,8},{1,9},{2,10},{3,11},{4,12},{5,13},{6,14},{7,15},{8,16},{9,17... | collective-permute-start | bytes 786440 | tf_op jit(solution)/shard_map/ppermute | solution.py:15
  69.8 2.2 and_and_fusion
  72.0 9.7 %collective-permute-done.16 = bf16[256,512]{1,0:T(8,128)(2,1)S(1)} collective-permute-done((bf16[256,512]{1,0:T(8,128)(2,1)S(1)}, bf16[256,512]{1,0:T(8,128)(2,1)S(1)}, u32[]{:S(2)}, u32[]{:S(2)}) %collective-permute-start.16) | collective-permute-done | bytes 262176 | tf_op jit(solution)/shard_map/ppermute | solution.py:15
  81.6 1.9 collective-permute-start.19
  83.6 0.0 collective-permute-done.17
  83.6 1.9 collective-permute-start.20
  85.6 4.9 %collective-permute-start.21 = (bf16[256,512]{1,0:T(8,128)(2,1)S(1)}, bf16[256,512]{1,0:T(8,128)(2,1)S(1)}, u32[]{:S(2)}, u32[]{:S(2)}) collective-permute-start(bf16[256,512]{1,0:T(8,128)(2,1)S(1)} %copy-done), channel_id=1, source_target_pairs={{0,3},{1,4},{2,5},{3,6},{4,7},{5,8},{6,9},{7,10},{8,11},{9,12},{10... | collective-permute-start | bytes 786440 | tf_op jit(solution)/shard_map/ppermute | solution.py:15
  90.5 7.3 %collective-permute-done.19 = bf16[256,512]{1,0:T(8,128)(2,1)S(1)} collective-permute-done((bf16[256,512]{1,0:T(8,128)(2,1)S(1)}, bf16[256,512]{1,0:T(8,128)(2,1)S(1)}, u32[]{:S(2)}, u32[]{:S(2)}) %collective-permute-start.19) | collective-permute-done | bytes 262176 | tf_op jit(solution)/shard_map/ppermute | solution.py:15
  97.8 1.9 collective-permute-start.22
  99.7 9.2 %collective-permute-done.20 = bf16[256,512]{1,0:T(8,128)(2,1)S(1)} collective-permute-done((bf16[256,512]{1,0:T(8,128)(2,1)S(1)}, bf16[256,512]{1,0:T(8,128)(2,1)S(1)}, u32[]{:S(2)}, u32[]{:S(2)}) %collective-permute-start.20) | collective-permute-done | bytes 262176 | tf_op jit(solution)/shard_map/ppermute | solution.py:15
  108.9 1.9 collective-permute-start.23
  110.8 0.0 collective-permute-done.21
  110.8 1.9 collective-permute-start.2
  112.8 0.0 collective-permute-done.22
  112.8 1.9 collective-permute-start
  114.8 13.4 %collective-permute-done.23 = bf16[256,512]{1,0:T(8,128)(2,1)S(1)} collective-permute-done((bf16[256,512]{1,0:T(8,128)(2,1)S(1)}, bf16[256,512]{1,0:T(8,128)(2,1)S(1)}, u32[]{:S(2)}, u32[]{:S(2)}) %collective-permute-start.23) | collective-permute-done | bytes 262176 | tf_op jit(solution)/shard_map/ppermute | solution.py:15
  128.2 1.9 collective-permute-start.1
  130.2 11.1 %collective-permute-done = bf16[256,512]{0,1:T(8,128)(2,1)S(1)} collective-permute-done((bf16[256,512]{0,1:T(8,128)(2,1)S(1)}, bf16[256,512]{0,1:T(8,128)(2,1)S(1)}, u32[]{:S(2)}, u32[]{:S(2)}) %collective-permute-start) | collective-permute-done | bytes 262176 | tf_op jit(solution)/shard_map/ppermute | solution.py:15
  141.3 1.9 collective-permute-start.3
  143.2 3.5 %collective-permute-start.4 = (bf16[256,512]{0,1:T(8,128)(2,1)S(1)}, bf16[256,512]{0,1:T(8,128)(2,1)S(1)}, u32[]{:S(2)}, u32[]{:S(2)}) collective-permute-start(bf16[256,512]{0,1:T(8,128)(2,1)S(1)} %copy.22), channel_id=1, source_target_pairs={{0,4},{1,5},{2,6},{3,7},{4,8},{5,9},{6,10},{7,11},{8,12},{9,13},{1... | collective-permute-start | bytes 786440 | tf_op jit(solution)/shard_map/ppermute | solution.py:15
  146.8 4.0 %collective-permute-start.5 = (bf16[256,512]{0,1:T(8,128)(2,1)S(1)}, bf16[256,512]{0,1:T(8,128)(2,1)S(1)}, u32[]{:S(2)}, u32[]{:S(2)}) collective-permute-start(bf16[256,512]{0,1:T(8,128)(2,1)S(1)} %copy.22), channel_id=1, source_target_pairs={{0,3},{1,4},{2,5},{3,6},{4,7},{5,8},{6,9},{7,10},{8,11},{9,12},{10... | collective-permute-start | bytes 786440 | tf_op jit(solution)/shard_map/ppermute | solution.py:15
  150.8 5.0 %collective-permute-done.3 = bf16[256,512]{0,1:T(8,128)(2,1)S(1)} collective-permute-done((bf16[256,512]{0,1:T(8,128)(2,1)S(1)}, bf16[256,512]{0,1:T(8,128)(2,1)S(1)}, u32[]{:S(2)}, u32[]{:S(2)}) %collective-permute-start.3) | collective-permute-done | bytes 262176 | tf_op jit(solution)/shard_map/ppermute | solution.py:15
  155.7 7.4 %collective-permute-done.4 = bf16[256,512]{0,1:T(8,128)(2,1)S(1)} collective-permute-done((bf16[256,512]{0,1:T(8,128)(2,1)S(1)}, bf16[256,512]{0,1:T(8,128)(2,1)S(1)}, u32[]{:S(2)}, u32[]{:S(2)}) %collective-permute-start.4) | collective-permute-done | bytes 262176 | tf_op jit(solution)/shard_map/ppermute | solution.py:15
  163.2 0.0 collective-permute-done.6
  163.2 0.0 collective-permute-done.7
  163.3 8.0 %fusion.60 = f32[2304,256,7]{1,0,2:T(8,128)} fusion(bf16[256,7,128]{0,2,1:T(8,128)(2,1)S(1)} %bitcast.146, bf16[2304,512]{1,0:T(8,128)(2,1)S(1)} %constant_dynamic-update-slice_fusion.10), kind=kOutput, calls=%fused_computation.43 | convolution fusion | flops 1056964608 | bytes 17563648 | tf_op jit(solution)/shard_map/tgd,sd->gts/dot_general | solution.py:36
  171.2 7.9 %fusion.61 = f32[2304,256,7]{1,0,2:T(8,128)} fusion(bf16[256,7,128]{0,2,1:T(8,128)(2,1)S(1)} %bitcast.145, bf16[2304,512]{1,0:T(8,128)(2,1)S(1)} %constant_dynamic-update-slice_fusion.10), kind=kOutput, calls=%fused_computation.46 | convolution fusion | flops 1056964608 | bytes 17563648 | tf_op jit(solution)/shard_map/tgd,sd->gts/dot_general | solution.py:36
  179.2 7.0 %fusion.8 = (f32[7,256]{1,0:T(8,128)S(1)}, f32[2304,256,7]{1,0,2:T(8,128)}) fusion(pred[256,2304]{0,1:T(8,128)(4,1)S(1)} %and_and_fusion, bf16[256,7,128]{0,2,1:T(8,128)(2,1)S(1)} %bitcast.144, bf16[2304,512]{1,0:T(8,128)(2,1)S(1)} %constant_dynamic-update-slice_fusion.10), kind=kOutput, calls=%fused_computation.16 | convolution fusion | flops 1069349120 | bytes 18160640 | tf_op jit(solution)/shard_map/tgd,sd->gts/dot_general | solution.py:36
  186.2 24.8 %fusion = (f32[7,256]{1,0:T(8,128)S(1)}, f32[7,256]{1,0:T(8,128)S(1)}, f32[7,256]{1,0:T(8,128)S(1)}, f32[7,256]{1,0:T(8,128)S(1)}, f32[2304,256,7]{1,0,2:T(8,128)}) fusion(f32[2304,256,7]{1,0,2:T(8,128)} %get-tuple-element.17, f32[7,256]{1,0:T(8,128)S(1)} %get-tuple-element.16, pred[256,2304]{0,1:T(8,128)(4,1)S(1)} %and_and_fusion, ...), kind=kOutput, calls=%fused_computation.8 | convolution fusion | flops 1110631424 | bytes 67735552 | tf_op jit(solution)/shard_map/tgd,sd->gts/dot_general | solution.py:36
  211.1 8.1 %fusion.57 = bf16[256,7,128]{0,2,1:T(8,128)(2,1)S(1)} fusion(f32[2304,256,7]{1,0,2:T(8,128)} %get-tuple-element.17, f32[7,256]{1,0:T(8,128)S(1)} %get-tuple-element.16, pred[256,2304]{0,1:T(8,128)(4,1)S(1)} %and_and_fusion, bf16[2304,512]{0,1:T(8,128)(2,1)S(1)} %constant_dynamic-update-slice_fusion, f32[256,7]{0,1:T(8,128)S(1)} %bitcast.155), kind=kOutput, calls=%fused_computation.41 | convolution fusion | flops 1073938432 | bytes 18169856 | tf_op jit(solution)/shard_map/gts,sd->tgd/dot_general | solution.py:43
  219.2 0.2 copy.43
  219.4 18.5 %fusion.2 = (f32[7,256]{1,0:T(8,128)S(1)}, f32[7,256]{1,0:T(8,128)S(1)}, f32[7,256]{1,0:T(8,128)S(1)}) fusion(f32[2304,256,7]{1,0,2:T(8,128)} %get-tuple-element.18, f32[7,256]{1,0:T(8,128)S(1)} %get-tuple-element.6, pred[256,2304]{0,1:T(8,128)(4,1)S(1)} %and_and_fusion, f32[7,256]{1,0:T(8,128)S(1)} %get-tuple-element.7, f32[2304,256,7]{1,0,2:T(8,128)} %fusion.61, ...), kind=kLoop, calls=%fused_computation.10 | loop fusion | flops 49539840 | bytes 50178048 | tf_op jit(solution)/shard_map/reduce_sum | solution.py:42
  237.9 10.2 %fusion.39 = bf16[256,7,128]{0,2,1:T(8,128)(2,1)S(1)} fusion(f32[2304,256,7]{1,0,2:T(8,128)} %fusion.60, f32[7,256]{1,0:T(8,128)S(1)} %get-tuple-element.8, pred[256,2304]{0,1:T(8,128)(4,1)S(1)} %and_and_fusion, bf16[2304,512]{0,1:T(8,128)(2,1)} %copy-done.1, f32[256,7]{0,1:T(8,128)S(1)} %bitcast.154), kind=kOutput, calls=%fused_computation.35 | convolution fusion | flops 1073938432 | bytes 18167808 | tf_op jit(solution)/shard_map/gts,sd->tgd/dot_general | solution.py:43
  248.1 0.2 copy.46
  248.3 10.2 %fusion.51 = bf16[256,7,128]{0,2,1:T(8,128)(2,1)S(1)} fusion(f32[2304,256,7]{1,0,2:T(8,128)} %get-tuple-element.18, f32[7,256]{1,0:T(8,128)S(1)} %get-tuple-element.6, pred[256,2304]{0,1:T(8,128)(4,1)S(1)} %and_and_fusion, bf16[2304,512]{0,1:T(8,128)(2,1)} %copy-done.1, f32[256,7]{0,1:T(8,128)S(1)} %bitcast.153), kind=kOutput, calls=%fused_computation.39 | convolution fusion | flops 1073938432 | bytes 18167808 | tf_op jit(solution)/shard_map/gts,sd->tgd/dot_general | solution.py:43
  258.6 0.2 copy.44
  258.8 10.2 %fusion.45 = bf16[256,7,128]{0,2,1:T(8,128)(2,1)S(1)} fusion(f32[2304,256,7]{1,0,2:T(8,128)} %fusion.61, f32[7,256]{1,0:T(8,128)S(1)} %get-tuple-element.7, pred[256,2304]{0,1:T(8,128)(4,1)S(1)} %and_and_fusion, bf16[2304,512]{0,1:T(8,128)(2,1)} %copy-done.1, f32[256,7]{0,1:T(8,128)S(1)} %bitcast.152), kind=kOutput, calls=%fused_computation.37 | convolution fusion | flops 1073938432 | bytes 18167808 | tf_op jit(solution)/shard_map/gts,sd->tgd/dot_general | solution.py:43
  269.0 0.2 copy.45
  269.3 1.4 pad_maximum_fusion
  (42 shorter events, 0.4 us)
Async XLA Ops:
  0.0 25.8 %copy-start.2 = (s32[256]{0:T(256)S(1)}, s32[256]{0:T(256)}, u32[]{:S(2)}) copy-start(s32[256]{0:T(256)} %param.7) | copy-start | bytes 3076
  0.0 52.3 %copy-start = (bf16[256,512]{1,0:T(8,128)(2,1)S(1)}, bf16[256,512]{1,0:T(8,128)(2,1)}, u32[]{:S(2)}) copy-start(bf16[256,512]{1,0:T(8,128)(2,1)} %param.5) | copy-start | bytes 786436
  0.0 55.1 %collective-permute-start.14 = (s32[256]{0:T(256)}, s32[256]{0:T(256)S(1)}, u32[]{:S(2)}, u32[]{:S(2)}) collective-permute-start(s32[256]{0:T(256)} %param.7), channel_id=1, source_target_pairs={{0,2},{1,3},{2,4},{3,5},{4,6},{5,7},{6,8},{7,9},{8,10},{9,11},{10,... | collective-permute-start | bytes 3080 | tf_op jit(solution)/shard_map/ppermute | solution.py:15
  4.8 47.5 %collective-permute-start.13 = (s32[256]{0:T(256)}, s32[256]{0:T(256)S(1)}, u32[]{:S(2)}, u32[]{:S(2)}) collective-permute-start(s32[256]{0:T(256)} %param.7), channel_id=1, source_target_pairs={{0,3},{1,4},{2,5},{3,6},{4,7},{5,8},{6,9},{7,10},{8,11},{9,12},{10... | collective-permute-start | bytes 3080 | tf_op jit(solution)/shard_map/ppermute | solution.py:15
  8.6 37.8 %collective-permute-start.12 = (s32[256]{0:T(256)}, s32[256]{0:T(256)S(1)}, u32[]{:S(2)}, u32[]{:S(2)}) collective-permute-start(s32[256]{0:T(256)} %param.7), channel_id=1, source_target_pairs={{0,4},{1,5},{2,6},{3,7},{4,8},{5,9},{6,10},{7,11},{8,12},{9,13},{1... | collective-permute-start | bytes 3080 | tf_op jit(solution)/shard_map/ppermute | solution.py:15
  11.8 32.3 %collective-permute-start.11 = (s32[256]{0:T(256)}, s32[256]{0:T(256)S(1)}, u32[]{:S(2)}, u32[]{:S(2)}) collective-permute-start(s32[256]{0:T(256)} %param.7), channel_id=1, source_target_pairs={{0,5},{1,6},{2,7},{3,8},{4,9},{5,10},{6,11},{7,12},{8,13},{9,14},{... | collective-permute-start | bytes 3080 | tf_op jit(solution)/shard_map/ppermute | solution.py:15
  15.0 10.8 %collective-permute-start.8 = (s32[256]{0:T(256)}, s32[256]{0:T(256)S(1)}, u32[]{:S(2)}, u32[]{:S(2)}) collective-permute-start(s32[256]{0:T(256)} %param.7), channel_id=1, source_target_pairs={{0,8},{1,9},{2,10},{3,11},{4,12},{5,13},{6,14},{7,15},{8,16},{9,17... | collective-permute-start | bytes 3080 | tf_op jit(solution)/shard_map/ppermute | solution.py:15
  25.8 7.3 %collective-permute-start.9 = (s32[256]{0:T(256)S(1)}, s32[256]{0:T(256)S(1)}, u32[]{:S(2)}, u32[]{:S(2)}) collective-permute-start(s32[256]{0:T(256)S(1)} %copy-done.2), channel_id=1, source_target_pairs={{0,7},{1,8},{2,9},{3,10},{4,11},{5,12},{6,13},{7,14},{8,15},{9,16}... | collective-permute-start | bytes 3080 | tf_op jit(solution)/shard_map/ppermute | solution.py:15
  33.1 8.8 %collective-permute-start.10 = (s32[256]{0:T(256)S(1)}, s32[256]{0:T(256)S(1)}, u32[]{:S(2)}, u32[]{:S(2)}) collective-permute-start(s32[256]{0:T(256)S(1)} %copy-done.2), channel_id=1, source_target_pairs={{0,6},{1,7},{2,8},{3,9},{4,10},{5,11},{6,12},{7,13},{8,14},{9,15},... | collective-permute-start | bytes 3080 | tf_op jit(solution)/shard_map/ppermute | solution.py:15
  41.9 24.7 %collective-permute-start.15 = (s32[256]{0:T(256)S(1)}, s32[256]{0:T(256)S(1)}, u32[]{:S(2)}, u32[]{:S(2)}) collective-permute-start(s32[256]{0:T(256)S(1)} %copy-done.2), channel_id=1, source_target_pairs={{0,1},{1,2},{2,3},{3,4},{4,5},{5,6},{6,7},{7,8},{8,9},{9,10},{10,1... | collective-permute-start | bytes 3080 | tf_op jit(solution)/shard_map/ppermute | solution.py:15
  44.1 119.1 %collective-permute-start.7 = (bf16[256,512]{0,1:T(8,128)(2,1)S(1)}, bf16[256,512]{0,1:T(8,128)(2,1)S(1)}, u32[]{:S(2)}, u32[]{:S(2)}) collective-permute-start(bf16[256,512]{0,1:T(8,128)(2,1)S(1)} %copy.22), channel_id=1, source_target_pairs={{0,1},{1,2},{2,3},{3,4},{4,5},{5,6},{6,7},{7,8},{8,9},{9,10},{10,1... | collective-permute-start | bytes 786440 | tf_op jit(solution)/shard_map/ppermute | solution.py:15
  46.4 116.8 %collective-permute-start.6 = (bf16[256,512]{0,1:T(8,128)(2,1)S(1)}, bf16[256,512]{0,1:T(8,128)(2,1)S(1)}, u32[]{:S(2)}, u32[]{:S(2)}) collective-permute-start(bf16[256,512]{0,1:T(8,128)(2,1)S(1)} %copy.22), channel_id=1, source_target_pairs={{0,2},{1,3},{2,4},{3,5},{4,6},{5,7},{6,8},{7,9},{8,10},{9,11},{10,... | collective-permute-start | bytes 786440 | tf_op jit(solution)/shard_map/ppermute | solution.py:15
  52.3 33.3 %collective-permute-start.18 = (bf16[256,512]{1,0:T(8,128)(2,1)S(1)}, bf16[256,512]{1,0:T(8,128)(2,1)S(1)}, u32[]{:S(2)}, u32[]{:S(2)}) collective-permute-start(bf16[256,512]{1,0:T(8,128)(2,1)S(1)} %copy-done), channel_id=1, source_target_pairs={{0,6},{1,7},{2,8},{3,9},{4,10},{5,11},{6,12},{7,13},{8,14},{9,15},... | collective-permute-start | bytes 786440 | tf_op jit(solution)/shard_map/ppermute | solution.py:15
  55.2 28.4 %collective-permute-start.17 = (bf16[256,512]{1,0:T(8,128)(2,1)S(1)}, bf16[256,512]{1,0:T(8,128)(2,1)S(1)}, u32[]{:S(2)}, u32[]{:S(2)}) collective-permute-start(bf16[256,512]{1,0:T(8,128)(2,1)S(1)} %copy-done), channel_id=1, source_target_pairs={{0,7},{1,8},{2,9},{3,10},{4,11},{5,12},{6,13},{7,14},{8,15},{9,16}... | collective-permute-start | bytes 786440 | tf_op jit(solution)/shard_map/ppermute | solution.py:15
  66.6 15.0 %collective-permute-start.16 = (bf16[256,512]{1,0:T(8,128)(2,1)S(1)}, bf16[256,512]{1,0:T(8,128)(2,1)S(1)}, u32[]{:S(2)}, u32[]{:S(2)}) collective-permute-start(bf16[256,512]{1,0:T(8,128)(2,1)S(1)} %copy-done), channel_id=1, source_target_pairs={{0,8},{1,9},{2,10},{3,11},{4,12},{5,13},{6,14},{7,15},{8,16},{9,17... | collective-permute-start | bytes 786440 | tf_op jit(solution)/shard_map/ppermute | solution.py:15
  81.6 16.1 %collective-permute-start.19 = (bf16[256,512]{1,0:T(8,128)(2,1)S(1)}, bf16[256,512]{1,0:T(8,128)(2,1)S(1)}, u32[]{:S(2)}, u32[]{:S(2)}) collective-permute-start(bf16[256,512]{1,0:T(8,128)(2,1)S(1)} %copy-done), channel_id=1, source_target_pairs={{0,5},{1,6},{2,7},{3,8},{4,9},{5,10},{6,11},{7,12},{8,13},{9,14},{... | collective-permute-start | bytes 786440 | tf_op jit(solution)/shard_map/ppermute | solution.py:15
  83.6 25.3 %collective-permute-start.20 = (bf16[256,512]{1,0:T(8,128)(2,1)S(1)}, bf16[256,512]{1,0:T(8,128)(2,1)S(1)}, u32[]{:S(2)}, u32[]{:S(2)}) collective-permute-start(bf16[256,512]{1,0:T(8,128)(2,1)S(1)} %copy-done), channel_id=1, source_target_pairs={{0,4},{1,5},{2,6},{3,7},{4,8},{5,9},{6,10},{7,11},{8,12},{9,13},{1... | collective-permute-start | bytes 786440 | tf_op jit(solution)/shard_map/ppermute | solution.py:15
  85.6 25.3 %collective-permute-start.21 = (bf16[256,512]{1,0:T(8,128)(2,1)S(1)}, bf16[256,512]{1,0:T(8,128)(2,1)S(1)}, u32[]{:S(2)}, u32[]{:S(2)}) collective-permute-start(bf16[256,512]{1,0:T(8,128)(2,1)S(1)} %copy-done), channel_id=1, source_target_pairs={{0,3},{1,4},{2,5},{3,6},{4,7},{5,8},{6,9},{7,10},{8,11},{9,12},{10... | collective-permute-start | bytes 786440 | tf_op jit(solution)/shard_map/ppermute | solution.py:15
  97.8 15.0 %collective-permute-start.22 = (bf16[256,512]{1,0:T(8,128)(2,1)S(1)}, bf16[256,512]{1,0:T(8,128)(2,1)S(1)}, u32[]{:S(2)}, u32[]{:S(2)}) collective-permute-start(bf16[256,512]{1,0:T(8,128)(2,1)S(1)} %copy-done), channel_id=1, source_target_pairs={{0,2},{1,3},{2,4},{3,5},{4,6},{5,7},{6,8},{7,9},{8,10},{9,11},{10,... | collective-permute-start | bytes 786440 | tf_op jit(solution)/shard_map/ppermute | solution.py:15
  108.9 19.3 %collective-permute-start.23 = (bf16[256,512]{1,0:T(8,128)(2,1)S(1)}, bf16[256,512]{1,0:T(8,128)(2,1)S(1)}, u32[]{:S(2)}, u32[]{:S(2)}) collective-permute-start(bf16[256,512]{1,0:T(8,128)(2,1)S(1)} %copy-done), channel_id=1, source_target_pairs={{0,1},{1,2},{2,3},{3,4},{4,5},{5,6},{6,7},{7,8},{8,9},{9,10},{10,1... | collective-permute-start | bytes 786440 | tf_op jit(solution)/shard_map/ppermute | solution.py:15
  110.8 35.9 %collective-permute-start.2 = (bf16[256,512]{0,1:T(8,128)(2,1)S(1)}, bf16[256,512]{0,1:T(8,128)(2,1)S(1)}, u32[]{:S(2)}, u32[]{:S(2)}) collective-permute-start(bf16[256,512]{0,1:T(8,128)(2,1)S(1)} %copy.22), channel_id=1, source_target_pairs={{0,6},{1,7},{2,8},{3,9},{4,10},{5,11},{6,12},{7,13},{8,14},{9,15},... | collective-permute-start | bytes 786440 | tf_op jit(solution)/shard_map/ppermute | solution.py:15
  112.8 28.5 %collective-permute-start = (bf16[256,512]{0,1:T(8,128)(2,1)S(1)}, bf16[256,512]{0,1:T(8,128)(2,1)S(1)}, u32[]{:S(2)}, u32[]{:S(2)}) collective-permute-start(bf16[256,512]{0,1:T(8,128)(2,1)S(1)} %copy.22), channel_id=1, source_target_pairs={{0,8},{1,9},{2,10},{3,11},{4,12},{5,13},{6,14},{7,15},{8,16},{9,17... | collective-permute-start | bytes 786440 | tf_op jit(solution)/shard_map/ppermute | solution.py:15
  128.2 15.0 %collective-permute-start.1 = (bf16[256,512]{0,1:T(8,128)(2,1)S(1)}, bf16[256,512]{0,1:T(8,128)(2,1)S(1)}, u32[]{:S(2)}, u32[]{:S(2)}) collective-permute-start(bf16[256,512]{0,1:T(8,128)(2,1)S(1)} %copy.22), channel_id=1, source_target_pairs={{0,7},{1,8},{2,9},{3,10},{4,11},{5,12},{6,13},{7,14},{8,15},{9,16}... | collective-permute-start | bytes 786440 | tf_op jit(solution)/shard_map/ppermute | solution.py:15
  141.3 14.4 %collective-permute-start.3 = (bf16[256,512]{0,1:T(8,128)(2,1)S(1)}, bf16[256,512]{0,1:T(8,128)(2,1)S(1)}, u32[]{:S(2)}, u32[]{:S(2)}) collective-permute-start(bf16[256,512]{0,1:T(8,128)(2,1)S(1)} %copy.22), channel_id=1, source_target_pairs={{0,5},{1,6},{2,7},{3,8},{4,9},{5,10},{6,11},{7,12},{8,13},{9,14},{... | collective-permute-start | bytes 786440 | tf_op jit(solution)/shard_map/ppermute | solution.py:15
  143.2 19.9 %collective-permute-start.4 = (bf16[256,512]{0,1:T(8,128)(2,1)S(1)}, bf16[256,512]{0,1:T(8,128)(2,1)S(1)}, u32[]{:S(2)}, u32[]{:S(2)}) collective-permute-start(bf16[256,512]{0,1:T(8,128)(2,1)S(1)} %copy.22), channel_id=1, source_target_pairs={{0,4},{1,5},{2,6},{3,7},{4,8},{5,9},{6,10},{7,11},{8,12},{9,13},{1... | collective-permute-start | bytes 786440 | tf_op jit(solution)/shard_map/ppermute | solution.py:15
  146.8 16.4 %collective-permute-start.5 = (bf16[256,512]{0,1:T(8,128)(2,1)S(1)}, bf16[256,512]{0,1:T(8,128)(2,1)S(1)}, u32[]{:S(2)}, u32[]{:S(2)}) collective-permute-start(bf16[256,512]{0,1:T(8,128)(2,1)S(1)} %copy.22), channel_id=1, source_target_pairs={{0,3},{1,4},{2,5},{3,6},{4,7},{5,8},{6,9},{7,10},{8,11},{9,12},{10... | collective-permute-start | bytes 786440 | tf_op jit(solution)/shard_map/ppermute | solution.py:15
  163.3 47.8 %copy-start.1 = (bf16[2304,512]{0,1:T(8,128)(2,1)}, bf16[2304,512]{0,1:T(8,128)(2,1)S(1)}, u32[]{:S(2)}) copy-start(bf16[2304,512]{0,1:T(8,128)(2,1)S(1)} %constant_dynamic-update-slice_fusion) | copy-start | bytes 7077892
where the time goes:
time: 271 us
  matrix products  86.5 us (32%)
  starting transfers between devices  86.4 us (32%)
  waiting for transfers between devices  70.2 us (26%)
  other arithmetic  22 us (8%)
  local copies, waits for them, and re-layouts  4.92 us (2%)
    ppermute x24, starting transfers between devices, passed_along(): lax.ppermute(value, axis, [(source, source + steps) for source in range(i...  86.4 us
    ppermute x24, waiting for transfers between devices, passed_along(): lax.ppermute(value, axis, [(source, source + steps) for source in range(i...  70.2 us
    dot_general x4, matrix products, attend_heads(): jnp.einsum('tgd,sd->gts', query_heads, key_head, preferred_element_type=j...  47.8 us
    dot_general x4, matrix products, attend_heads(): jnp.einsum('gts,sd->tgd', weights.astype(jnp.bfloat16), value_head, prefe...  38.7 us
    reduce_sum x1, other arithmetic, attend_heads(): totals = jnp.sum(weights, axis=2, keepdims=True)  18.5 us
  transfers between devices with their start and end apart: 24, of which 9 were waited for; matrix products, arithmetic and copies ran while one was open for 2% of the time, Pallas kernels for 0%

commit v1 on v0

v1 whole, which is shorter than its diff:
```python
import functools

import jax
import jax.numpy as jnp
from jax import lax
from jax.experimental import pallas as pl
from jax.experimental.pallas import tpu as pltpu
from jax.sharding import PartitionSpec as P

KEY_VALUE_HEADS = 4
GROUP = 7
WIDTH = 128
TOKENS = 256
EXTRA = 16
ROWS = 2 * TOKENS + EXTRA
AXES = ("dp", "seq")
SCALE = 1.4426950408889634 / WIDTH**0.5
LOW, HIGH = 1e-25, 1e30
NT = (((1,), (1,)), ((), ()))
NN = (((1,), (0,)), ((), ()))


def rank_of(plane, y, x):
    return (plane * 4 + y) * 4 + x


def turned_along_x(value, steps):
    pairs = [
        (rank_of(plane, y, x), rank_of(plane, y, (x + steps) % 4))
        for plane in range(16)
        for y in range(4)
        for x in range(4)
    ]
    return lax.ppermute(value, AXES, pairs)


def shifted(value, steps):
    return lax.ppermute(value, AXES, [(r, r + steps) for r in range(256 - steps)])


def ids_down(rows):
    halves = [
        jnp.transpose(jnp.broadcast_to(rows[i : i + 1], (WIDTH, WIDTH))) for i in range(2)
    ]
    return jnp.concatenate(halves, axis=0)


def ids_across(rows, count):
    halves = [jnp.broadcast_to(rows[i : i + 1], (count, WIDTH)) for i in range(2)]
    return jnp.concatenate(halves, axis=1)


def ids_of(block):
    return block[2 * TOKENS : ROWS, :].astype(jnp.float32)[0:2]


def general_head(head, whole, q_ref, o_ref, held, top, total, mix, sem):
    count = len(whole)
    for b in range(count):
        columns = pl.ds(pl.multiple_of(head * WIDTH, WIDTH), WIDTH)
        copy = pltpu.make_async_copy(whole[b].at[:, columns], held.at[b], sem)
        copy.start()
        copy.wait()
    mine = ids_down(ids_of(held[count - 1]))
    mine = jnp.concatenate([mine, mine], axis=1)
    later = lax.broadcasted_iota(jnp.int32, (TOKENS, TOKENS), 1) > lax.broadcasted_iota(
        jnp.int32, (TOKENS, TOKENS), 0
    )

    @pl.loop(0, GROUP)
    def _(g):
        columns = pl.ds(pl.multiple_of(g * WIDTH, WIDTH), WIDTH)
        top[...] = jnp.full((TOKENS, WIDTH), -1e30, jnp.float32)
        total[...] = jnp.zeros((TOKENS, WIDTH), jnp.float32)
        mix[...] = jnp.zeros((TOKENS, WIDTH), jnp.float32)

        @pl.loop(0, count)
        def _(b):
            s = lax.dot_general(
                q_ref[:, columns], held[b, 0:TOKENS, :], NT, preferred_element_type=jnp.float32
            )
            s = s * SCALE
            theirs = ids_across(
                held[b, 2 * TOKENS : ROWS, :].astype(jnp.float32)[0:2], TOKENS
            )
            allowed = (mine == theirs) & ~(later & (b == count - 1))
            s = jnp.where(allowed, s, -1e30)
            now = jnp.maximum(top[:, 0:1], jnp.max(s, axis=1, keepdims=True))
            p = jnp.where(allowed, jnp.exp2(s - now), 0.0)
            keep = jnp.exp2(top[:, 0:1] - now)
            total[...] = total[...] * keep + jnp.sum(p, axis=1, keepdims=True)
            mix[...] = mix[...] * keep + lax.dot_general(
                p.astype(jnp.bfloat16),
                held[b, TOKENS : 2 * TOKENS, :],
                NN,
                preferred_element_type=jnp.float32,
            )
            top[...] = jnp.broadcast_to(now, (TOKENS, WIDTH))

        o_ref[:, columns] = (mix[...] / total[...]).astype(jnp.bfloat16)


def attend(count, q_ref, *refs):
    blocks = refs[:count]
    whole = refs[count : 2 * count]
    o_ref = refs[2 * count]
    mixed, picked, causal, rows_in, held, top, total, mix, sem = refs[2 * count + 1 :]
    head = pl.program_id(0)
    own = blocks[-1]

    @pl.when(head == 0)
    def _():
        ids = ids_of(own)
        down = ids_down(ids)
        first = ids[0:1, 0:1]
        rows_in[...] = jnp.where(down == first, 1.0, 0.0)
        down = jnp.concatenate([down, down], axis=1)
        row = lax.broadcasted_iota(jnp.int32, (TOKENS, TOKENS), 0)
        column = lax.broadcasted_iota(jnp.int32, (TOKENS, TOKENS), 1)
        causal[...] = jnp.where((down == ids_across(ids, TOKENS)) & (column <= row), 1.0, 0.0)
        for b in range(count - 1):
            picked[b] = ids_down(jnp.where(ids_of(blocks[b]) == first, 1.0, 0.0)).astype(
                jnp.bfloat16
            )

    for b in range(count):
        mask = picked[b] if b < count - 1 else jnp.ones((TOKENS, WIDTH), jnp.bfloat16)
        values = blocks[b][TOKENS : 2 * TOKENS, :]
        mixed[b, :, 0:WIDTH] = values * mask if b < count - 1 else values
        mixed[b, :, WIDTH:] = mask

    good = None
    for g in range(GROUP):
        columns = slice(g * WIDTH, (g + 1) * WIDTH)
        q = q_ref[:, columns]
        sums = None
        for b in range(count):
            s = lax.dot_general(
                q, blocks[b][0:TOKENS, :], NT, preferred_element_type=jnp.float32
            )
            p = jnp.exp2(s * SCALE)
            if b == count - 1:
                p = p * causal[...]
                inside = rows_in[...] > 0.5
                sums = jnp.where(jnp.concatenate([inside, inside], axis=1), sums, 0.0)
            term = lax.dot_general(
                p.astype(jnp.bfloat16), mixed[b], NN, preferred_element_type=jnp.float32
            )
            sums = term if b == 0 else sums + term
        weight = sums[:, WIDTH:]
        o_ref[:, columns] = (sums[:, :WIDTH] / weight).astype(jnp.bfloat16)
        fine = jnp.where((weight > LOW) & (weight < HIGH), 1.0, 0.0)
        good = fine if good is None else jnp.minimum(good, fine)

    @pl.when(jnp.min(good) < 0.5)
    def _():
        general_head(head, whole, q_ref, o_ref, held, top, total, mix, sem)


def attention(queries, blocks):
    count = len(blocks)
    by_head = lambda rows, columns: pl.BlockSpec((rows, columns), lambda h: (0, h))
    return pl.pallas_call(
        functools.partial(attend, count),
        grid=(KEY_VALUE_HEADS,),
        in_specs=[by_head(TOKENS, GROUP * WIDTH)]
        + [by_head(ROWS, WIDTH)] * count
        + [pl.BlockSpec(memory_space=pl.ANY)] * count,
        out_specs=by_head(TOKENS, GROUP * WIDTH),
        out_shape=jax.ShapeDtypeStruct(queries.shape, jnp.bfloat16),
        scratch_shapes=[
            pltpu.VMEM((count, TOKENS, 2 * WIDTH), jnp.bfloat16),
            pltpu.VMEM((count - 1, TOKENS, WIDTH), jnp.bfloat16),
            pltpu.VMEM((TOKENS, TOKENS), jnp.float32),
            pltpu.VMEM((TOKENS, WIDTH), jnp.float32),
            pltpu.VMEM((count, ROWS, WIDTH), jnp.bfloat16),
            pltpu.VMEM((TOKENS, WIDTH), jnp.float32),
            pltpu.VMEM((TOKENS, WIDTH), jnp.float32),
            pltpu.VMEM((TOKENS, WIDTH), jnp.float32),
            pltpu.SemaphoreType.DMA,
        ],
        compiler_params=pltpu.CompilerParams(vmem_limit_bytes=56 * 1024 * 1024),
        cost_estimate=pl.CostEstimate(
            flops=28 * 256 * 256 * count * 512,
            bytes_accessed=4_000_000 + count * 540_000,
            transcendentals=28 * 256 * 256 * count,
        ),
    )(queries, *blocks, *blocks)


def per_device(queries, key_states, value_vectors, segment_ids):
    ids = (segment_ids + 1).astype(jnp.bfloat16).reshape(2, WIDTH)
    ids = jnp.pad(jnp.tile(ids, (1, KEY_VALUE_HEADS)), ((0, EXTRA - 2), (0, 0)))
    own = jnp.concatenate([key_states, value_vectors, ids], axis=0)
    x = lax.axis_index("seq") % 4
    four = shifted(own, 4)
    eight = shifted(own, 8)
    middle = [turned_along_x(four, a) for a in (1, 3)]
    ends = [turned_along_x(jnp.where(x + a < 4, own, eight), a) for a in (1, 3)]
    two = turned_along_x(jnp.where(x < 2, own, four), 2)
    six = shifted(two, 4)
    return attention(queries, [four, eight, *middle, *ends, two, six, own])


def solution(mesh):
    rows = P(AXES, None)
    return jax.shard_map(
        per_device,
        mesh=mesh,
        in_specs=(rows, rows, rows, P(AXES)),
        out_specs=rows,
        check_vma=False,
    )
```

time: 271 us -> 275 us (1.015)
  Pallas kernels: 0 us -> 201 us
  matrix products: 86.5 us -> 0 us
  starting transfers between devices: 86.4 us -> 14.8 us
  other arithmetic: 22 us -> 2.1 us
  waiting for transfers between devices: 70.2 us -> 53.6 us
  local copies, waits for them, and re-layouts: 4.92 us -> 2.1 us
    pallas_call x0 -> x1, Pallas kernels: none -> 201 us  [attention(): pl.pallas_call(functools.partial(attend, count), grid=(KEY_VALUE_HEADS,),...]
    dot_general x8 -> x0, matrix products: 86.5 us -> none  [the longest x4 47.8 us: attend_heads(): jnp.einsum('tgd,sd->gts', query_heads, key_head, preferred_element_type=j...]
    ppermute x24 -> x8, starting transfers between devices: 86.4 us -> 14.8 us  [the longest x3 9.04 us: shifted(): lax.ppermute(value, AXES, [(r, r + steps) for r in range(256 - steps)])]
    reduce_sum x1 -> x0, other arithmetic: 18.5 us -> none  [attend_heads(): totals = jnp.sum(weights, axis=2, keepdims=True)]
    ppermute x24 -> x8, waiting for transfers between devices: 70.2 us -> 53.6 us  [the longest x5 31 us: turned_along_x(): return lax.ppermute(value, AXES, pairs)]
  transfers between devices with their start and end apart: 24 -> 8, of which waited for: 9 -> 4; matrix products, arithmetic and copies ran while one was open for 2% -> 0% of each run, Pallas kernels for 0% -> 0%
where the time goes in v1:
time: 275 us; the launch traced here: 274 us
  Pallas kernels  201 us (73%)
  waiting for transfers between devices  53.6 us (19%)
  starting transfers between devices  14.8 us (5%)
    pallas_call x1, Pallas kernels, attention(): pl.pallas_call(functools.partial(attend, count), grid=(KEY_VALUE_HEADS,),...  201 us
    ppermute x5, waiting for transfers between devices, turned_along_x(): return lax.ppermute(value, AXES, pairs)  31 us
    ppermute x3, waiting for transfers between devices, shifted(): lax.ppermute(value, AXES, [(r, r + steps) for r in range(256 - steps)])  22.6 us
    ppermute x3, starting transfers between devices, shifted(): lax.ppermute(value, AXES, [(r, r + steps) for r in range(256 - steps)])  9.04 us
    ppermute x5, starting transfers between devices, turned_along_x(): return lax.ppermute(value, AXES, pairs)  5.76 us
  transfers between devices with their start and end apart: 8, of which 4 were waited for; matrix products, arithmetic and copies ran while one was open for 0% of the time, Pallas kernels for 0%

profile of v1, /device:TPU:97, one launch (start us, length us, event | category | flops | bytes accessed | tf_op | source)
XLA Modules:
  0.0 274.1 jit_solution(6184210795085670505)
XLA Ops:
  0.0 0.0 copy-start
  0.0 0.0 copy-start.1
  0.0 0.7 fusion.2
  0.8 1.1 fusion.1.refs_8_.refs_17_
  1.8 0.0 copy-start.2
  1.8 4.8 %collective-permute-start.1 = (bf16[528,512]{1,0:T(8,128)(2,1)S(1)}, bf16[528,512]{1,0:T(8,128)(2,1)S(1)}, u32[]{:S(2)}, u32[]{:S(2)}) collective-permute-start(bf16[528,512]{1,0:T(8,128)(2,1)S(1)} %fusion.1.refs_8_.refs_17_), channel_id=1, source_target_pairs={{0,8},{1,9},{2,10},{3,11},{4,12},{5,13},{6,14},{7,15},{8,16},{9,17... | collective-permute-start | bytes 1622024 | tf_op jit(solution)/shard_map/ppermute | solution.py:38
  6.7 2.3 collective-permute-start
  9.0 17.1 %collective-permute-done.1.refs_1_.refs_10_ = bf16[528,512]{1,0:T(8,128)(2,1)S(1)} collective-permute-done((bf16[528,512]{1,0:T(8,128)(2,1)S(1)}, bf16[528,512]{1,0:T(8,128)(2,1)S(1)}, u32[]{:S(2)}, u32[]{:S(2)}) %collective-permute-start.1) | collective-permute-done | bytes 540704 | tf_op jit(solution)/shard_map/ppermute | solution.py:38
  26.1 0.0 copy-start.3
  26.1 5.6 %collective-permute-done.refs_0_.refs_9_ = bf16[528,512]{1,0:T(8,128)(2,1)S(1)} collective-permute-done((bf16[528,512]{1,0:T(8,128)(2,1)S(1)}, bf16[528,512]{1,0:T(8,128)(2,1)S(1)}, u32[]{:S(2)}, u32[]{:S(2)}) %collective-permute-start) | collective-permute-done | bytes 540704 | tf_op jit(solution)/shard_map/ppermute | solution.py:38
  31.6 0.0 copy-done
  31.6 0.0 copy-done.1
  31.6 0.0 copy-start.4
  31.6 0.3 broadcast_select_fusion.1
  31.9 0.0 copy-done.2
  32.0 0.0 copy-done.3
  32.0 2.8 %collective-permute-start.6 = (bf16[528,512]{1,0:T(8,128)(2,1)S(1)}, bf16[528,512]{1,0:T(8,128)(2,1)S(1)}, u32[]{:S(2)}, u32[]{:S(2)}) collective-permute-start(bf16[528,512]{1,0:T(8,128)(2,1)S(1)} %get-tuple-element.7), channel_id=1, source_target_pairs={{0,2},{1,3},{2,0},{3,1},{4,6},{5,7},{6,4},{7,5},{8,10},{9,11},{10,... | collective-permute-start | bytes 1622024 | tf_op jit(solution)/shard_map/ppermute | solution.py:34
  34.8 0.9 collective-permute-start.5
  35.7 0.0 collective-permute-start.3
  35.7 0.0 copy-done.4
  35.7 1.4 collective-permute-start.2
  37.1 0.6 collective-permute-start.4
  37.7 9.8 %collective-permute-done.6.refs_6_.refs_15_ = bf16[528,512]{1,0:T(8,128)(2,1)S(1)} collective-permute-done((bf16[528,512]{1,0:T(8,128)(2,1)S(1)}, bf16[528,512]{1,0:T(8,128)(2,1)S(1)}, u32[]{:S(2)}, u32[]{:S(2)}) %collective-permute-start.6) | collective-permute-done | bytes 540704 | tf_op jit(solution)/shard_map/ppermute | solution.py:34
  47.5 0.0 copy-start.5
  47.5 1.9 collective-permute-start.7
  49.4 21.2 %collective-permute-done.3.refs_3_.refs_12_ = bf16[528,512]{1,0:T(8,128)(2,1)S(1)} collective-permute-done((bf16[528,512]{1,0:T(8,128)(2,1)S(1)}, bf16[528,512]{1,0:T(8,128)(2,1)S(1)}, u32[]{:S(2)}, u32[]{:S(2)}) %collective-permute-start.3) | collective-permute-done | bytes 540704 | tf_op jit(solution)/shard_map/ppermute | solution.py:34
  70.6 0.0 copy-start.7
  70.6 0.0 collective-permute-done.2.refs_2_.refs_11_
  70.6 0.0 copy-start.8
  70.6 0.0 collective-permute-done.5.refs_5_.refs_14_
  70.6 0.0 copy-start.6
  70.6 0.0 collective-permute-done.4.refs_4_.refs_13_
  70.6 0.0 copy-start.9
  70.7 0.0 collective-permute-done.7.refs_7_.refs_16_
  70.7 0.0 copy-done.5
  70.7 0.7 copy-done.7
  71.4 0.2 copy-done.8
  71.6 0.2 copy-done.6
  71.8 0.1 copy-done.9
  71.9 0.0 copy-start.10
  71.9 0.8 copy-done.10
  72.7 201.4 %shard_map.46 = bf16[256,3584]{1,0:T(8,128)(2,1)} custom-call(bf16[256,3584]{1,0:T(8,128)(2,1)} %q_ref.1, bf16[528,512]{1,0:T(8,128)(2,1)} %copy-done.4, bf16[528,512]{1,0:T(8,128)(2,1)} %copy-done.3, bf16[528,512]{1,0:T(8,128)(2,1)} %copy-done.8, bf16[528,512]{1,0:T(8,128)(2,1)} %copy-done.7, bf16[528,512]{1,0:T(8,128)(2,1)} %copy-done.9, ...), custom_call_target="tpu_custom_call" | custom-call | flops 8455716864 | bytes 8860000 | tf_op jit(solution)/shard_map/pallas_call | solution.py:163
  (2 shorter events, 0.0 us)
Async XLA Ops:
  0.0 31.6 %copy-start = (bf16[256,512]{1,0:T(8,128)(2,1)S(1)}, bf16[256,512]{1,0:T(8,128)(2,1)}, u32[]{:S(2)}) copy-start(bf16[256,512]{1,0:T(8,128)(2,1)} %param.6) | copy-start | bytes 786436
  0.0 31.6 %copy-start.1 = (bf16[256,512]{1,0:T(8,128)(2,1)S(1)}, bf16[256,512]{1,0:T(8,128)(2,1)}, u32[]{:S(2)}) copy-start(bf16[256,512]{1,0:T(8,128)(2,1)} %param.5) | copy-start | bytes 786436
  1.8 30.1 %copy-start.2 = (bf16[528,512]{1,0:T(8,128)(2,1)}, bf16[528,512]{1,0:T(8,128)(2,1)S(1)}, u32[]{:S(2)}) copy-start(bf16[528,512]{1,0:T(8,128)(2,1)S(1)} %fusion.1.refs_8_.refs_17_) | copy-start | bytes 1622020
  1.8 24.2 %collective-permute-start.1 = (bf16[528,512]{1,0:T(8,128)(2,1)S(1)}, bf16[528,512]{1,0:T(8,128)(2,1)S(1)}, u32[]{:S(2)}, u32[]{:S(2)}) collective-permute-start(bf16[528,512]{1,0:T(8,128)(2,1)S(1)} %fusion.1.refs_8_.refs_17_), channel_id=1, source_target_pairs={{0,8},{1,9},{2,10},{3,11},{4,12},{5,13},{6,14},{7,15},{8,16},{9,17... | collective-permute-start | bytes 1622024 | tf_op jit(solution)/shard_map/ppermute | solution.py:38
  6.7 25.0 %collective-permute-start = (bf16[528,512]{1,0:T(8,128)(2,1)S(1)}, bf16[528,512]{1,0:T(8,128)(2,1)S(1)}, u32[]{:S(2)}, u32[]{:S(2)}) collective-permute-start(bf16[528,512]{1,0:T(8,128)(2,1)S(1)} %fusion.1.refs_8_.refs_17_), channel_id=1, source_target_pairs={{0,4},{1,5},{2,6},{3,7},{4,8},{5,9},{6,10},{7,11},{8,12},{9,13},{1... | collective-permute-start | bytes 1622024 | tf_op jit(solution)/shard_map/ppermute | solution.py:38
  26.1 5.9 %copy-start.3 = (bf16[528,512]{1,0:T(8,128)(2,1)}, bf16[528,512]{1,0:T(8,128)(2,1)S(1)}, u32[]{:S(2)}) copy-start(bf16[528,512]{1,0:T(8,128)(2,1)S(1)} %collective-permute-done.1.refs_1_.refs_10_) | copy-start | bytes 1622020
  31.6 4.0 %copy-start.4 = (bf16[528,512]{1,0:T(8,128)(2,1)}, bf16[528,512]{1,0:T(8,128)(2,1)S(1)}, u32[]{:S(2)}) copy-start(bf16[528,512]{1,0:T(8,128)(2,1)S(1)} %collective-permute-done.refs_0_.refs_9_) | copy-start | bytes 1622020
  32.0 15.5 %collective-permute-start.6 = (bf16[528,512]{1,0:T(8,128)(2,1)S(1)}, bf16[528,512]{1,0:T(8,128)(2,1)S(1)}, u32[]{:S(2)}, u32[]{:S(2)}) collective-permute-start(bf16[528,512]{1,0:T(8,128)(2,1)S(1)} %get-tuple-element.7), channel_id=1, source_target_pairs={{0,2},{1,3},{2,0},{3,1},{4,6},{5,7},{6,4},{7,5},{8,10},{9,11},{10,... | collective-permute-start | bytes 1622024 | tf_op jit(solution)/shard_map/ppermute | solution.py:34
  34.8 35.8 %collective-permute-start.5 = (bf16[528,512]{1,0:T(8,128)(2,1)S(1)}, bf16[528,512]{1,0:T(8,128)(2,1)S(1)}, u32[]{:S(2)}, u32[]{:S(2)}) collective-permute-start(bf16[528,512]{1,0:T(8,128)(2,1)S(1)} %get-tuple-element.5), channel_id=1, source_target_pairs={{0,3},{1,0},{2,1},{3,2},{4,7},{5,4},{6,5},{7,6},{8,11},{9,8},{10,9... | collective-permute-start | bytes 1622024 | tf_op jit(solution)/shard_map/ppermute | solution.py:34
  35.7 35.0 %collective-permute-start.3 = (bf16[528,512]{1,0:T(8,128)(2,1)S(1)}, bf16[528,512]{1,0:T(8,128)(2,1)S(1)}, u32[]{:S(2)}, u32[]{:S(2)}) collective-permute-start(bf16[528,512]{1,0:T(8,128)(2,1)S(1)} %collective-permute-done.refs_0_.refs_9_), channel_id=1, source_target_pairs={{0,3},{1,0},{2,1},{3,2},{4,7},{5,4},{6,5},{7,6},{8,11},{9,8},{10,9... | collective-permute-start | bytes 1622024 | tf_op jit(solution)/shard_map/ppermute | solution.py:34
  35.7 34.9 %collective-permute-start.2 = (bf16[528,512]{1,0:T(8,128)(2,1)S(1)}, bf16[528,512]{1,0:T(8,128)(2,1)S(1)}, u32[]{:S(2)}, u32[]{:S(2)}) collective-permute-start(bf16[528,512]{1,0:T(8,128)(2,1)S(1)} %collective-permute-done.refs_0_.refs_9_), channel_id=1, source_target_pairs={{0,1},{1,2},{2,3},{3,0},{4,5},{5,6},{6,7},{7,4},{8,9},{9,10},{10,1... | collective-permute-start | bytes 1622024 | tf_op jit(solution)/shard_map/ppermute | solution.py:34
  37.1 33.5 %collective-permute-start.4 = (bf16[528,512]{1,0:T(8,128)(2,1)S(1)}, bf16[528,512]{1,0:T(8,128)(2,1)S(1)}, u32[]{:S(2)}, u32[]{:S(2)}) collective-permute-start(bf16[528,512]{1,0:T(8,128)(2,1)S(1)} %get-tuple-element.6), channel_id=1, source_target_pairs={{0,1},{1,2},{2,3},{3,0},{4,5},{5,6},{6,7},{7,4},{8,9},{9,10},{10,1... | collective-permute-start | bytes 1622024 | tf_op jit(solution)/shard_map/ppermute | solution.py:34
  47.5 23.2 %copy-start.5 = (bf16[528,512]{1,0:T(8,128)(2,1)}, bf16[528,512]{1,0:T(8,128)(2,1)S(1)}, u32[]{:S(2)}) copy-start(bf16[528,512]{1,0:T(8,128)(2,1)S(1)} %collective-permute-done.6.refs_6_.refs_15_) | copy-start | bytes 1622020
  47.5 23.1 %collective-permute-start.7 = (bf16[528,512]{1,0:T(8,128)(2,1)S(1)}, bf16[528,512]{1,0:T(8,128)(2,1)S(1)}, u32[]{:S(2)}, u32[]{:S(2)}) collective-permute-start(bf16[528,512]{1,0:T(8,128)(2,1)S(1)} %collective-permute-done.6.refs_6_.refs_15_), channel_id=1, source_target_pairs={{0,4},{1,5},{2,6},{3,7},{4,8},{5,9},{6,10},{7,11},{8,12},{9,13},{1... | collective-permute-start | bytes 1622024 | tf_op jit(solution)/shard_map/ppermute | solution.py:38
  70.6 0.8 copy-start.7
  70.6 1.0 copy-start.8
  70.6 1.2 copy-start.6
  70.6 1.3 copy-start.9
  71.9 0.8 copy-start.10

commit v2 on v1

v2 whole, which is shorter than its diff:
```python
import functools

import jax
import jax.numpy as jnp
from jax import lax
from jax.experimental import pallas as pl
from jax.experimental.pallas import tpu as pltpu
from jax.sharding import PartitionSpec as P

KEY_VALUE_HEADS = 4
GROUP = 7
WIDTH = 128
TOKENS = 256
EXTRA = 16
ROWS = 2 * TOKENS + EXTRA
AXES = ("dp", "seq")
SCALE = 1.4426950408889634 / WIDTH**0.5
LOW, HIGH = 1e-25, 1e30
VMEM_LIMIT = 60 * 1024 * 1024
NT = (((1,), (1,)), ((), ()))
NN = (((1,), (0,)), ((), ()))


def rank_of(plane, y, x):
    return (plane * 4 + y) * 4 + x


def turned_along_x(value, steps):
    pairs = [
        (rank_of(plane, y, x), rank_of(plane, y, (x + steps) % 4))
        for plane in range(16)
        for y in range(4)
        for x in range(4)
    ]
    return lax.ppermute(value, AXES, pairs)


def turned_along_y(value, steps):
    pairs = [
        (rank_of(plane, y, x), rank_of(plane, (y + steps) % 4, x))
        for plane in range(16)
        for y in range(4)
        for x in range(4)
    ]
    return lax.ppermute(value, AXES, pairs)


def two_rows_on(value):
    pairs = [
        (rank_of(plane, (y - 1) % 4, x), rank_of(plane, y, x) + 8)
        for plane in range(16)
        for y in range(4)
        for x in range(4)
        if rank_of(plane, y, x) + 8 < 256
    ]
    return lax.ppermute(value, AXES, pairs)


def shifted(value, steps):
    return lax.ppermute(value, AXES, [(r, r + steps) for r in range(256 - steps)])


def ids_down(rows):
    halves = [
        jnp.transpose(jnp.broadcast_to(rows[i : i + 1], (WIDTH, WIDTH))) for i in range(2)
    ]
    return jnp.concatenate(halves, axis=0)


def ids_across(rows, count):
    halves = [jnp.broadcast_to(rows[i : i + 1], (count, WIDTH)) for i in range(2)]
    return jnp.concatenate(halves, axis=1)


def ids_of(block):
    return block[2 * TOKENS : ROWS, :].astype(jnp.float32)[0:2]


def general_head(head, whole, q_ref, o_ref, held, top, total, mix, sem):
    count = len(whole)
    for b in range(count):
        columns = pl.ds(pl.multiple_of(head * WIDTH, WIDTH), WIDTH)
        copy = pltpu.make_async_copy(whole[b].at[:, columns], held.at[b], sem)
        copy.start()
        copy.wait()
    mine = ids_down(ids_of(held[count - 1]))
    mine = jnp.concatenate([mine, mine], axis=1)
    later = lax.broadcasted_iota(jnp.int32, (TOKENS, TOKENS), 1) > lax.broadcasted_iota(
        jnp.int32, (TOKENS, TOKENS), 0
    )

    @pl.loop(0, GROUP)
    def _(g):
        columns = pl.ds(pl.multiple_of(g * WIDTH, WIDTH), WIDTH)
        top[...] = jnp.full((TOKENS, WIDTH), -1e30, jnp.float32)
        total[...] = jnp.zeros((TOKENS, WIDTH), jnp.float32)
        mix[...] = jnp.zeros((TOKENS, WIDTH), jnp.float32)

        @pl.loop(0, count)
        def _(b):
            s = lax.dot_general(
                q_ref[:, columns], held[b, 0:TOKENS, :], NT, preferred_element_type=jnp.float32
            )
            s = s * SCALE
            theirs = ids_across(
                held[b, 2 * TOKENS : ROWS, :].astype(jnp.float32)[0:2], TOKENS
            )
            allowed = (mine == theirs) & ~(later & (b == count - 1))
            s = jnp.where(allowed, s, -1e30)
            now = jnp.maximum(top[:, 0:1], jnp.max(s, axis=1, keepdims=True))
            p = jnp.where(allowed, jnp.exp2(s - now), 0.0)
            keep = jnp.exp2(top[:, 0:1] - now)
            total[...] = total[...] * keep + jnp.sum(p, axis=1, keepdims=True)
            mix[...] = mix[...] * keep + lax.dot_general(
                p.astype(jnp.bfloat16),
                held[b, TOKENS : 2 * TOKENS, :],
                NN,
                preferred_element_type=jnp.float32,
            )
            top[...] = jnp.broadcast_to(now, (TOKENS, WIDTH))

        o_ref[:, columns] = (mix[...] / total[...]).astype(jnp.bfloat16)


def attend(prior, has_own, has_before, last, whole_count, q_ref, own, *refs):
    refs = list(refs)
    take = lambda n: [refs.pop(0) for _ in range(n)]
    blocks = take(prior)
    before = take(2) if has_before else None
    whole = take(whole_count)
    outs = take(1 if last else 2)
    mixed, picked, causal, rows_in = take(4)
    head = pl.program_id(0)
    count = prior + has_own

    @pl.when(head == 0)
    def _():
        ids = ids_of(own)
        down = ids_down(ids)
        first = ids[0:1, 0:1]
        rows_in[...] = jnp.where(down == first, 1.0, 0.0)
        if has_own:
            down = jnp.concatenate([down, down], axis=1)
            row = lax.broadcasted_iota(jnp.int32, (TOKENS, TOKENS), 0)
            column = lax.broadcasted_iota(jnp.int32, (TOKENS, TOKENS), 1)
            same = down == ids_across(ids, TOKENS)
            causal[...] = jnp.where(same & (column <= row), 1.0, 0.0)
        for b in range(prior):
            picked[b] = ids_down(jnp.where(ids_of(blocks[b]) == first, 1.0, 0.0)).astype(
                jnp.bfloat16
            )

    for b in range(prior):
        mixed[b, :, 0:WIDTH] = blocks[b][TOKENS : 2 * TOKENS, :] * picked[b]
        mixed[b, :, WIDTH:] = picked[b]
    if has_own:
        mixed[prior, :, 0:WIDTH] = own[TOKENS : 2 * TOKENS, :]
        mixed[prior, :, WIDTH:] = jnp.ones((TOKENS, WIDTH), jnp.bfloat16)

    def term(q, keys, b, mask=None):
        s = lax.dot_general(q, keys, NT, preferred_element_type=jnp.float32)
        p = jnp.exp2(s * SCALE)
        if mask is not None:
            p = p * mask
        return lax.dot_general(
            p.astype(jnp.bfloat16), mixed[b], NN, preferred_element_type=jnp.float32
        )

    good = None
    weights = None
    lane = lax.broadcasted_iota(jnp.int32, (TOKENS, WIDTH), 1)
    for g in range(GROUP):
        columns = slice(g * WIDTH, (g + 1) * WIDTH)
        q = q_ref[:, columns]
        sums = term(q, blocks[0][0:TOKENS, :], 0)
        for b in range(1, prior):
            sums = sums + term(q, blocks[b][0:TOKENS, :], b)
        inside = rows_in[...] > 0.5
        mix = jnp.where(inside, sums[:, :WIDTH], 0.0)
        weight = jnp.where(inside, sums[:, WIDTH:], 0.0)
        if has_own:
            sums = term(q, own[0:TOKENS, :], prior, causal[...])
            mix = mix + sums[:, :WIDTH]
            weight = weight + sums[:, WIDTH:]
        if has_before:
            mix = mix + before[0][:, columns]
            weight = weight + before[1][:, g : g + 1]
        if last:
            outs[0][:, columns] = (mix / weight).astype(jnp.bfloat16)
            fine = jnp.where((weight > LOW) & (weight < HIGH), 1.0, 0.0)
            good = fine if good is None else jnp.minimum(good, fine)
        else:
            outs[0][:, columns] = mix
            weights = weight if weights is None else jnp.where(lane == g, weight, weights)
    if last:

        @pl.when(jnp.min(good) < 0.5)
        def _():
            general_head(head, whole, q_ref, outs[0], *refs)
    else:
        outs[1][...] = weights


def attention(queries, own, blocks, has_own, before, whole, last):
    by_head = lambda rows, columns: pl.BlockSpec((rows, columns), lambda h: (0, h))
    count = len(blocks) + has_own
    wide, narrow = by_head(TOKENS, GROUP * WIDTH), by_head(TOKENS, WIDTH)
    before_specs = [wide, narrow] if before else []
    if last:
        out_specs = wide
        out_shape = jax.ShapeDtypeStruct(queries.shape, jnp.bfloat16)
    else:
        out_specs = [wide, narrow]
        out_shape = [
            jax.ShapeDtypeStruct(queries.shape, jnp.float32),
            jax.ShapeDtypeStruct((TOKENS, KEY_VALUE_HEADS * WIDTH), jnp.float32),
        ]
    scratch = [
        pltpu.VMEM((count, TOKENS, 2 * WIDTH), jnp.bfloat16),
        pltpu.VMEM((len(blocks), TOKENS, WIDTH), jnp.bfloat16),
        pltpu.VMEM((TOKENS, TOKENS), jnp.float32),
        pltpu.VMEM((TOKENS, WIDTH), jnp.float32),
    ]
    if last:
        scratch += [
            pltpu.VMEM((len(whole), ROWS, WIDTH), jnp.bfloat16),
            pltpu.VMEM((TOKENS, WIDTH), jnp.float32),
            pltpu.VMEM((TOKENS, WIDTH), jnp.float32),
            pltpu.VMEM((TOKENS, WIDTH), jnp.float32),
            pltpu.SemaphoreType.DMA,
        ]
    return pl.pallas_call(
        functools.partial(attend, len(blocks), has_own, bool(before), last, len(whole)),
        grid=(KEY_VALUE_HEADS,),
        in_specs=[wide]
        + [by_head(ROWS, WIDTH)] * (1 + len(blocks))
        + before_specs
        + [pl.BlockSpec(memory_space=pl.ANY)] * len(whole),
        out_specs=out_specs,
        out_shape=out_shape,
        scratch_shapes=scratch,
        compiler_params=pltpu.CompilerParams(vmem_limit_bytes=VMEM_LIMIT),
        cost_estimate=pl.CostEstimate(
            flops=28 * 256 * 256 * count * 1024,
            bytes_accessed=4_000_000 + count * 540_000,
            transcendentals=28 * 256 * 256 * count,
        ),
    )(queries, own, *blocks, *before, *whole)


def per_device(queries, key_states, value_vectors, segment_ids):
    ids = (segment_ids + 1).astype(jnp.bfloat16).reshape(2, WIDTH)
    ids = jnp.pad(jnp.tile(ids, (1, KEY_VALUE_HEADS)), ((0, EXTRA - 2), (0, 0)))
    own = jnp.concatenate([key_states, value_vectors, ids], axis=0)
    x = lax.axis_index("seq") % 4
    four = shifted(own, 4)
    two = shifted(own, 2)
    eight = two_rows_on(turned_along_y(own, -1))
    middle = [turned_along_x(four, a) for a in (1, 3)]
    six = shifted(two, 4)
    ends = [turned_along_x(jnp.where(x + a < 4, own, eight), a) for a in (1, 3)]
    stage = attention(queries, own, [four, two], True, [], [], False)
    stage = attention(queries, own, [eight, *middle], False, stage, [], False)
    whole = [four, two, eight, *middle, six, *ends, own]
    return attention(queries, own, [six, *ends], False, stage, whole, True)


def solution(mesh):
    rows = P(AXES, None)
    return jax.shard_map(
        per_device,
        mesh=mesh,
        in_specs=(rows, rows, rows, P(AXES)),
        out_specs=rows,
        check_vma=False,
    )
```

time: 275 us -> 254 us (0.924)
  waiting for transfers between devices: 53.6 us -> 17.4 us
  Pallas kernels: 201 us -> 210 us
  starting transfers between devices: 14.8 us -> 22 us
    ppermute x5 -> x4, waiting for transfers between devices: 31 us -> 0.01 us  [turned_along_x(): return lax.ppermute(value, AXES, pairs)]
    ppermute x3, waiting for transfers between devices: 22.6 us -> 13 us  [shifted(): lax.ppermute(value, AXES, [(r, r + steps) for r in range(256 - steps)])]
    pallas_call x1 -> x3, Pallas kernels: 201 us -> 210 us  [attention(): pl.pallas_call(functools.partial(attend, len(blocks), has_own, bool(befor...]
    ppermute x0 -> x2, starting transfers between devices: none -> 8.12 us  [the longest x1 5.31 us: two_rows_on(): return lax.ppermute(value, AXES, pairs)]
    ppermute x0 -> x2, waiting for transfers between devices: none -> 4.37 us  [the longest x1 4.37 us: turned_along_y(): return lax.ppermute(value, AXES, pairs)]
    ppermute x5 -> x4, starting transfers between devices: 5.76 us -> 5.42 us  [turned_along_x(): return lax.ppermute(value, AXES, pairs)]
  transfers between devices with their start and end apart: 8 -> 9, of which waited for: 4 -> 2; matrix products, arithmetic and copies ran while one was open for 0% -> 0% of each run, Pallas kernels for 0% -> 8%
where the time goes in v2:
time: 254 us; the launch traced here: 253 us
  Pallas kernels  210 us (83%)
  starting transfers between devices  22 us (9%)
  waiting for transfers between devices  17.4 us (7%)
    pallas_call x3, Pallas kernels, attention(): pl.pallas_call(functools.partial(attend, len(blocks), has_own, bool(befor...  210 us
    ppermute x3, waiting for transfers between devices, shifted(): lax.ppermute(value, AXES, [(r, r + steps) for r in range(256 - steps)])  13 us
    ppermute x3, starting transfers between devices, shifted(): lax.ppermute(value, AXES, [(r, r + steps) for r in range(256 - steps)])  8.47 us
    ppermute x4, starting transfers between devices, turned_along_x(): return lax.ppermute(value, AXES, pairs)  5.42 us
    ppermute x1, starting transfers between devices, two_rows_on(): return lax.ppermute(value, AXES, pairs)  5.31 us
  transfers between devices with their start and end apart: 9, of which 2 were waited for; matrix products, arithmetic and copies ran while one was open for 0% of the time, Pallas kernels for 8%

profile of v2, /device:TPU:97, one launch (start us, length us, event | category | flops | bytes accessed | tf_op | source)
XLA Modules:
  0.0 252.8 jit_solution(9840180720357931219)
XLA Ops:
  0.0 0.0 copy-start.1
  0.0 0.0 copy-start
  0.0 0.7 fusion.2
  0.8 1.1 fusion.1.own.refs_13_
  1.8 0.0 copy-start.2
  1.8 2.8 %collective-permute-start.2 = (bf16[528,512]{1,0:T(8,128)(2,1)S(1)}, bf16[528,512]{1,0:T(8,128)(2,1)S(1)}, u32[]{:S(2)}, u32[]{:S(2)}) collective-permute-start(bf16[528,512]{1,0:T(8,128)(2,1)S(1)} %fusion.1.own.refs_13_), channel_id=1, source_target_pairs={{0,12},{1,13},{2,14},{3,15},{4,0},{5,1},{6,2},{7,3},{8,4},{9,5},{1... | collective-permute-start | bytes 1622024 | tf_op jit(solution)/shard_map/ppermute | solution.py:45
  4.7 1.9 collective-permute-start.6
  6.6 4.7 %collective-permute-start = (bf16[528,512]{1,0:T(8,128)(2,1)S(1)}, bf16[528,512]{1,0:T(8,128)(2,1)S(1)}, u32[]{:S(2)}, u32[]{:S(2)}) collective-permute-start(bf16[528,512]{1,0:T(8,128)(2,1)S(1)} %fusion.1.own.refs_13_), channel_id=1, source_target_pairs={{0,2},{1,3},{2,4},{3,5},{4,6},{5,7},{6,8},{7,9},{8,10},{9,11},{10,... | collective-permute-start | bytes 1622024 | tf_op jit(solution)/shard_map/ppermute | solution.py:60
  11.2 4.4 %collective-permute-done.2 = bf16[528,512]{1,0:T(8,128)(2,1)S(1)} collective-permute-done((bf16[528,512]{1,0:T(8,128)(2,1)S(1)}, bf16[528,512]{1,0:T(8,128)(2,1)S(1)}, u32[]{:S(2)}, u32[]{:S(2)}) %collective-permute-start.2) | collective-permute-done | bytes 540704 | tf_op jit(solution)/shard_map/ppermute | solution.py:45
  15.6 5.3 %collective-permute-start.3 = (bf16[528,512]{1,0:T(8,128)(2,1)S(1)}, bf16[528,512]{1,0:T(8,128)(2,1)S(1)}, u32[]{:S(2)}, u32[]{:S(2)}) collective-permute-start(bf16[528,512]{1,0:T(8,128)(2,1)S(1)} %collective-permute-done.2), channel_id=1, source_target_pairs={{12,8},{13,9},{14,10},{15,11},{0,12},{1,13},{2,14},{3,15},{4,16},{... | collective-permute-start | bytes 1622024 | tf_op jit(solution)/shard_map/ppermute | solution.py:56
  20.9 13.0 %collective-permute-done.6.refs_0_.refs_5_ = bf16[528,512]{1,0:T(8,128)(2,1)S(1)} collective-permute-done((bf16[528,512]{1,0:T(8,128)(2,1)S(1)}, bf16[528,512]{1,0:T(8,128)(2,1)S(1)}, u32[]{:S(2)}, u32[]{:S(2)}) %collective-permute-start.6) | collective-permute-done | bytes 540704 | tf_op jit(solution)/shard_map/ppermute | solution.py:60
  33.9 0.0 copy-start.4
  33.9 1.2 collective-permute-start.7
  35.1 1.5 collective-permute-start.8
  36.6 0.0 collective-permute-done.refs_1_.refs_6_
  36.6 0.0 copy-start.5
  36.6 1.9 collective-permute-start.1
  38.5 0.0 collective-permute-done.3.refs_0_.refs_7_
  38.5 0.0 copy-done.1
  38.5 0.0 copy-done
  38.5 0.0 copy-start.3
  38.6 0.2 broadcast_select_fusion
  38.8 0.0 copy-done.2
  38.8 0.1 collective-permute-start.4
  38.9 2.7 %collective-permute-start.5 = (bf16[528,512]{1,0:T(8,128)(2,1)S(1)}, bf16[528,512]{1,0:T(8,128)(2,1)S(1)}, u32[]{:S(2)}, u32[]{:S(2)}) collective-permute-start(bf16[528,512]{1,0:T(8,128)(2,1)S(1)} %get-tuple-element.13), channel_id=1, source_target_pairs={{0,3},{1,0},{2,1},{3,2},{4,7},{5,4},{6,5},{7,6},{8,11},{9,8},{10,9... | collective-permute-start | bytes 1622024 | tf_op jit(solution)/shard_map/ppermute | solution.py:35
  41.5 0.0 copy-done.4
  41.5 0.0 copy-done.5
  41.5 10.6 %shard_map.46 = (f32[256,3584]{1,0:T(8,128)}, f32[256,512]{1,0:T(8,128)}) custom-call(bf16[256,3584]{1,0:T(8,128)(2,1)} %q_ref.5, bf16[528,512]{1,0:T(8,128)(2,1)} %copy-done.2, bf16[528,512]{1,0:T(8,128)(2,1)} %copy-done.4, bf16[528,512]{1,0:T(8,128)(2,1)} %copy-done.5), custom_call_target="tpu_custom_call" | custom-call | flops 5637144576 | bytes 5620000 | tf_op jit(solution)/shard_map/pallas_call | solution.py:232
  52.2 0.0 copy-done.3
  52.2 0.0 collective-permute-done.7.refs_1_.refs_8_
  52.2 0.0 collective-permute-done.8.refs_2_.refs_9_
  52.2 10.2 %shard_map.47 = (f32[256,3584]{1,0:T(8,128)}, f32[256,512]{1,0:T(8,128)}) custom-call(bf16[256,3584]{1,0:T(8,128)(2,1)} %q_ref.5, bf16[528,512]{1,0:T(8,128)(2,1)} %copy-done.2, bf16[528,512]{1,0:T(8,128)(2,1)} %copy-done.3, bf16[528,512]{1,0:T(8,128)(2,1)} %collective-permute-done.7.refs_1_.refs_8_, ...), custom_call_target="tpu_custom_call" | custom-call | flops 5637144576 | bytes 5620000 | tf_op jit(solution)/shard_map/pallas_call | solution.py:232
  62.4 0.0 collective-permute-done.1.refs_0_.refs_10_
  62.4 0.0 collective-permute-done.4.refs_1_.refs_11_
  62.4 0.0 copy-start.6
  62.4 0.0 collective-permute-done.5.refs_2_.refs_12_
  62.4 0.0 copy-start.7
  62.4 0.8 copy-done.6
  63.2 0.2 copy-done.7
  63.4 189.4 %shard_map.48 = bf16[256,3584]{1,0:T(8,128)(2,1)} custom-call(bf16[256,3584]{1,0:T(8,128)(2,1)} %q_ref.5, bf16[528,512]{1,0:T(8,128)(2,1)} %copy-done.2, bf16[528,512]{1,0:T(8,128)(2,1)} %collective-permute-done.1.refs_0_.refs_10_, bf16[528,512]{1,0:T(8,128)(2,1)} %copy-done.6, bf16[528,512]{1,0:T(8,128)(2,1)} %copy-done.7, ...), custom_call_target="tpu_custom_call" | custom-call | flops 5637144576 | bytes 5620000 | tf_op jit(solution)/shard_map/pallas_call | solution.py:232
  (2 shorter events, 0.0 us)
Async XLA Ops:
  0.0 38.5 %copy-start.1 = (bf16[256,512]{1,0:T(8,128)(2,1)S(1)}, bf16[256,512]{1,0:T(8,128)(2,1)}, u32[]{:S(2)}) copy-start(bf16[256,512]{1,0:T(8,128)(2,1)} %param.5) | copy-start | bytes 786436
  0.0 38.5 %copy-start = (bf16[256,512]{1,0:T(8,128)(2,1)S(1)}, bf16[256,512]{1,0:T(8,128)(2,1)}, u32[]{:S(2)}) copy-start(bf16[256,512]{1,0:T(8,128)(2,1)} %param.6) | copy-start | bytes 786436
  1.8 36.9 %copy-start.2 = (bf16[528,512]{1,0:T(8,128)(2,1)}, bf16[528,512]{1,0:T(8,128)(2,1)S(1)}, u32[]{:S(2)}) copy-start(bf16[528,512]{1,0:T(8,128)(2,1)S(1)} %fusion.1.own.refs_13_) | copy-start | bytes 1622020
  1.8 13.8 %collective-permute-start.2 = (bf16[528,512]{1,0:T(8,128)(2,1)S(1)}, bf16[528,512]{1,0:T(8,128)(2,1)S(1)}, u32[]{:S(2)}, u32[]{:S(2)}) collective-permute-start(bf16[528,512]{1,0:T(8,128)(2,1)S(1)} %fusion.1.own.refs_13_), channel_id=1, source_target_pairs={{0,12},{1,13},{2,14},{3,15},{4,0},{5,1},{6,2},{7,3},{8,4},{9,5},{1... | collective-permute-start | bytes 1622024 | tf_op jit(solution)/shard_map/ppermute | solution.py:45
  4.7 29.3 %collective-permute-start.6 = (bf16[528,512]{1,0:T(8,128)(2,1)S(1)}, bf16[528,512]{1,0:T(8,128)(2,1)S(1)}, u32[]{:S(2)}, u32[]{:S(2)}) collective-permute-start(bf16[528,512]{1,0:T(8,128)(2,1)S(1)} %fusion.1.own.refs_13_), channel_id=1, source_target_pairs={{0,4},{1,5},{2,6},{3,7},{4,8},{5,9},{6,10},{7,11},{8,12},{9,13},{1... | collective-permute-start | bytes 1622024 | tf_op jit(solution)/shard_map/ppermute | solution.py:60
  6.6 30.0 %collective-permute-start = (bf16[528,512]{1,0:T(8,128)(2,1)S(1)}, bf16[528,512]{1,0:T(8,128)(2,1)S(1)}, u32[]{:S(2)}, u32[]{:S(2)}) collective-permute-start(bf16[528,512]{1,0:T(8,128)(2,1)S(1)} %fusion.1.own.refs_13_), channel_id=1, source_target_pairs={{0,2},{1,3},{2,4},{3,5},{4,6},{5,7},{6,8},{7,9},{8,10},{9,11},{10,... | collective-permute-start | bytes 1622024 | tf_op jit(solution)/shard_map/ppermute | solution.py:60
  15.6 22.9 %collective-permute-start.3 = (bf16[528,512]{1,0:T(8,128)(2,1)S(1)}, bf16[528,512]{1,0:T(8,128)(2,1)S(1)}, u32[]{:S(2)}, u32[]{:S(2)}) collective-permute-start(bf16[528,512]{1,0:T(8,128)(2,1)S(1)} %collective-permute-done.2), channel_id=1, source_target_pairs={{12,8},{13,9},{14,10},{15,11},{0,12},{1,13},{2,14},{3,15},{4,16},{... | collective-permute-start | bytes 1622024 | tf_op jit(solution)/shard_map/ppermute | solution.py:56
  33.9 7.6 %copy-start.4 = (bf16[528,512]{1,0:T(8,128)(2,1)}, bf16[528,512]{1,0:T(8,128)(2,1)S(1)}, u32[]{:S(2)}) copy-start(bf16[528,512]{1,0:T(8,128)(2,1)S(1)} %collective-permute-done.6.refs_0_.refs_5_) | copy-start | bytes 1622020
  33.9 18.3 %collective-permute-start.7 = (bf16[528,512]{1,0:T(8,128)(2,1)S(1)}, bf16[528,512]{1,0:T(8,128)(2,1)}, u32[]{:S(2)}, u32[]{:S(2)}) collective-permute-start(bf16[528,512]{1,0:T(8,128)(2,1)S(1)} %collective-permute-done.6.refs_0_.refs_5_), channel_id=1, source_target_pairs={{0,1},{1,2},{2,3},{3,0},{4,5},{5,6},{6,7},{7,4},{8,9},{9,10},{10,1... | collective-permute-start | bytes 1622024 | tf_op jit(solution)/shard_map/ppermute | solution.py:35
  35.1 17.1 %collective-permute-start.8 = (bf16[528,512]{1,0:T(8,128)(2,1)S(1)}, bf16[528,512]{1,0:T(8,128)(2,1)}, u32[]{:S(2)}, u32[]{:S(2)}) collective-permute-start(bf16[528,512]{1,0:T(8,128)(2,1)S(1)} %collective-permute-done.6.refs_0_.refs_5_), channel_id=1, source_target_pairs={{0,3},{1,0},{2,1},{3,2},{4,7},{5,4},{6,5},{7,6},{8,11},{9,8},{10,9... | collective-permute-start | bytes 1622024 | tf_op jit(solution)/shard_map/ppermute | solution.py:35
  36.6 4.9 %copy-start.5 = (bf16[528,512]{1,0:T(8,128)(2,1)}, bf16[528,512]{1,0:T(8,128)(2,1)S(1)}, u32[]{:S(2)}) copy-start(bf16[528,512]{1,0:T(8,128)(2,1)S(1)} %collective-permute-done.refs_1_.refs_6_) | copy-start | bytes 1622020
  36.6 25.8 %collective-permute-start.1 = (bf16[528,512]{1,0:T(8,128)(2,1)S(1)}, bf16[528,512]{1,0:T(8,128)(2,1)}, u32[]{:S(2)}, u32[]{:S(2)}) collective-permute-start(bf16[528,512]{1,0:T(8,128)(2,1)S(1)} %collective-permute-done.refs_1_.refs_6_), channel_id=1, source_target_pairs={{0,4},{1,5},{2,6},{3,7},{4,8},{5,9},{6,10},{7,11},{8,12},{9,13},{1... | collective-permute-start | bytes 1622024 | tf_op jit(solution)/shard_map/ppermute | solution.py:60
  38.5 13.6 %copy-start.3 = (bf16[528,512]{1,0:T(8,128)(2,1)}, bf16[528,512]{1,0:T(8,128)(2,1)S(1)}, u32[]{:S(2)}) copy-start(bf16[528,512]{1,0:T(8,128)(2,1)S(1)} %collective-permute-done.3.refs_0_.refs_7_) | copy-start | bytes 1622020
  38.8 23.6 %collective-permute-start.4 = (bf16[528,512]{1,0:T(8,128)(2,1)S(1)}, bf16[528,512]{1,0:T(8,128)(2,1)S(1)}, u32[]{:S(2)}, u32[]{:S(2)}) collective-permute-start(bf16[528,512]{1,0:T(8,128)(2,1)S(1)} %get-tuple-element.14), channel_id=1, source_target_pairs={{0,1},{1,2},{2,3},{3,0},{4,5},{5,6},{6,7},{7,4},{8,9},{9,10},{10,1... | collective-permute-start | bytes 1622024 | tf_op jit(solution)/shard_map/ppermute | solution.py:35
  38.9 23.6 %collective-permute-start.5 = (bf16[528,512]{1,0:T(8,128)(2,1)S(1)}, bf16[528,512]{1,0:T(8,128)(2,1)S(1)}, u32[]{:S(2)}, u32[]{:S(2)}) collective-permute-start(bf16[528,512]{1,0:T(8,128)(2,1)S(1)} %get-tuple-element.13), channel_id=1, source_target_pairs={{0,3},{1,0},{2,1},{3,2},{4,7},{5,4},{6,5},{7,6},{8,11},{9,8},{10,9... | collective-permute-start | bytes 1622024 | tf_op jit(solution)/shard_map/ppermute | solution.py:35
  62.4 0.8 copy-start.6
  62.4 1.0 copy-start.7

commit v3 on v2

--- a/solution.py
+++ b/solution.py
@@ -16,7 +16,7 @@
 AXES = ("dp", "seq")
 SCALE = 1.4426950408889634 / WIDTH**0.5
 LOW, HIGH = 1e-25, 1e30
-VMEM_LIMIT = 60 * 1024 * 1024
+VMEM_LIMIT = 24 * 1024 * 1024
 NT = (((1,), (1,)), ((), ()))
 NN = (((1,), (0,)), ((), ()))
 
@@ -56,8 +56,8 @@
     return lax.ppermute(value, AXES, pairs)
 
 
-def shifted(value, steps):
-    return lax.ppermute(value, AXES, [(r, r + steps) for r in range(256 - steps)])
+def row_on(value, columns=range(4)):
+    return lax.ppermute(value, AXES, [(r, r + 4) for r in range(252) if r % 4 in columns])
 
 
 def ids_down(rows):
@@ -253,16 +253,19 @@
     ids = jnp.pad(jnp.tile(ids, (1, KEY_VALUE_HEADS)), ((0, EXTRA - 2), (0, 0)))
     own = jnp.concatenate([key_states, value_vectors, ids], axis=0)
     x = lax.axis_index("seq") % 4
-    four = shifted(own, 4)
-    two = shifted(own, 2)
-    eight = two_rows_on(turned_along_y(own, -1))
+    four = row_on(own)
+    back = turned_along_y(own, -1)
+    across = turned_along_x(own, 2)
     middle = [turned_along_x(four, a) for a in (1, 3)]
-    six = shifted(two, 4)
+    eight = two_rows_on(back)
+    next_across = row_on(across)
     ends = [turned_along_x(jnp.where(x + a < 4, own, eight), a) for a in (1, 3)]
-    stage = attention(queries, own, [four, two], True, [], [], False)
-    stage = attention(queries, own, [eight, *middle], False, stage, [], False)
-    whole = [four, two, eight, *middle, six, *ends, own]
-    return attention(queries, own, [six, *ends], False, stage, whole, True)
+    far_across = row_on(next_across, (0, 1))
+    across = jnp.where(x < 2, far_across, across)
+    early = [four, *middle, next_across, eight]
+    late = [*ends, across]
+    stage = attention(queries, own, early, True, [], [], False)
+    return attention(queries, own, late, False, stage, [*early, *late, own], True)
 
 
 def solution(mesh):

time: 254 us -> 228 us (0.90)
  Pallas kernels: 210 us -> 184 us
    pallas_call x3 -> x2, Pallas kernels: 210 us -> 184 us  [attention(): pl.pallas_call(functools.partial(attend, len(blocks), has_own, bool(befor...]
    ppermute x3, waiting for transfers between devices: 13 us -> 2.62 us  [row_on(): lax.ppermute(value, AXES, [(r, r + 4) for r in range(252) if r % 4 in col...]
    ppermute x1, waiting for transfers between devices: 0.01 us -> 5.77 us  [two_rows_on(): return lax.ppermute(value, AXES, pairs)]
    ppermute x4 -> x5, starting transfers between devices: 5.42 us -> 7.56 us  [turned_along_x(): return lax.ppermute(value, AXES, pairs)]
  transfers between devices with their start and end apart: 9 -> 10, of which waited for: 2 -> 5; matrix products, arithmetic and copies ran while one was open for 0% -> 1% of each run, Pallas kernels for 8% -> 7%
where the time goes in v3:
time: 228 us; the launch traced here: 226 us
  Pallas kernels  184 us (81%)
  starting transfers between devices  23.5 us (10%)
  waiting for transfers between devices  15.9 us (7%)
  other arithmetic  3.04 us (1%)
    pallas_call x2, Pallas kernels, attention(): pl.pallas_call(functools.partial(attend, len(blocks), has_own, bool(befor...  184 us
    ppermute x3, starting transfers between devices, row_on(): lax.ppermute(value, AXES, [(r, r + 4) for r in range(252) if r % 4 in col...  7.74 us
    ppermute x5, starting transfers between devices, turned_along_x(): return lax.ppermute(value, AXES, pairs)  7.56 us
    ppermute x1, waiting for transfers between devices, turned_along_y(): return lax.ppermute(value, AXES, pairs)  6.28 us
    ppermute x1, waiting for transfers between devices, two_rows_on(): return lax.ppermute(value, AXES, pairs)  5.77 us
    ppermute x1, starting transfers between devices, two_rows_on(): return lax.ppermute(value, AXES, pairs)  5.41 us
  transfers between devices with their start and end apart: 10, of which 5 were waited for; matrix products, arithmetic and copies ran while one was open for 1% of the time, Pallas kernels for 7%

profile of v3, /device:TPU:97, one launch (start us, length us, event | category | flops | bytes accessed | tf_op | source)
XLA Modules:
  0.0 226.1 jit_solution(7446146701461778078)
XLA Ops:
  0.0 0.7 fusion.2
  0.7 1.1 fusion.1.own.refs_13_
  1.8 2.8 %collective-permute-start = (bf16[528,512]{1,0:T(8,128)(2,1)S(1)}, bf16[528,512]{1,0:T(8,128)(2,1)}, u32[]{:S(2)}, u32[]{:S(2)}) collective-permute-start(bf16[528,512]{1,0:T(8,128)(2,1)S(1)} %fusion.1.own.refs_13_), channel_id=1, source_target_pairs={{0,12},{1,13},{2,14},{3,15},{4,0},{5,1},{6,2},{7,3},{8,4},{9,5},{1... | collective-permute-start | bytes 1622024 | tf_op jit(solution)/shard_map/ppermute | solution.py:45
  4.6 2.7 %collective-permute-start.4 = (bf16[528,512]{1,0:T(8,128)(2,1)S(1)}, bf16[528,512]{1,0:T(8,128)(2,1)}, u32[]{:S(2)}, u32[]{:S(2)}) collective-permute-start(bf16[528,512]{1,0:T(8,128)(2,1)S(1)} %fusion.1.own.refs_13_), channel_id=1, source_target_pairs={{0,2},{1,3},{2,0},{3,1},{4,6},{5,7},{6,4},{7,5},{8,10},{9,11},{10,... | collective-permute-start | bytes 1622024 | tf_op jit(solution)/shard_map/ppermute | solution.py:35
  7.3 1.9 collective-permute-start.7
  9.2 6.3 %collective-permute-done = bf16[528,512]{1,0:T(8,128)(2,1)} collective-permute-done((bf16[528,512]{1,0:T(8,128)(2,1)S(1)}, bf16[528,512]{1,0:T(8,128)(2,1)}, u32[]{:S(2)}, u32[]{:S(2)}) %collective-permute-start) | collective-permute-done | bytes 540704 | tf_op jit(solution)/shard_map/ppermute | solution.py:45
  15.5 5.4 %collective-permute-start.1 = (bf16[528,512]{1,0:T(8,128)(2,1)}, bf16[528,512]{1,0:T(8,128)(2,1)S(1)}, u32[]{:S(2)}, u32[]{:S(2)}) collective-permute-start(bf16[528,512]{1,0:T(8,128)(2,1)} %collective-permute-done), channel_id=1, source_target_pairs={{12,8},{13,9},{14,10},{15,11},{0,12},{1,13},{2,14},{3,15},{4,16},{... | collective-permute-start | bytes 1622024 | tf_op jit(solution)/shard_map/ppermute | solution.py:56
  20.9 0.0 collective-permute-done.4
  21.0 3.9 %collective-permute-start.5 = (bf16[528,512]{1,0:T(8,128)(2,1)}, bf16[528,512]{1,0:T(8,128)(2,1)}, u32[]{:S(2)}, u32[]{:S(2)}) collective-permute-start(bf16[528,512]{1,0:T(8,128)(2,1)} %collective-permute-done.4), channel_id=1, source_target_pairs={{0,4},{1,5},{2,6},{3,7},{4,8},{5,9},{6,10},{7,11},{8,12},{9,13},{1... | collective-permute-start | bytes 1622024 | tf_op jit(solution)/shard_map/ppermute | solution.py:60
  24.8 0.3 collective-permute-done.7.refs_0_.refs_5_
  25.1 2.3 collective-permute-start.9
  27.4 0.0 collective-permute-start.8
  27.4 0.0 copy-start
  27.4 5.8 %collective-permute-done.1.refs_4_.refs_9_ = bf16[528,512]{1,0:T(8,128)(2,1)S(1)} collective-permute-done((bf16[528,512]{1,0:T(8,128)(2,1)}, bf16[528,512]{1,0:T(8,128)(2,1)S(1)}, u32[]{:S(2)}, u32[]{:S(2)}) %collective-permute-start.1) | collective-permute-done | bytes 540704 | tf_op jit(solution)/shard_map/ppermute | solution.py:56
  33.2 1.2 broadcast_select_fusion.1
  34.4 2.6 %collective-permute-start.3 = (bf16[528,512]{1,0:T(8,128)(2,1)S(1)}, bf16[528,512]{1,0:T(8,128)(2,1)S(1)}, u32[]{:S(2)}, u32[]{:S(2)}) collective-permute-start(bf16[528,512]{1,0:T(8,128)(2,1)S(1)} %get-tuple-element.9), channel_id=1, source_target_pairs={{0,3},{1,0},{2,1},{3,2},{4,7},{5,4},{6,5},{7,6},{8,11},{9,8},{10,9... | collective-permute-start | bytes 1622024 | tf_op jit(solution)/shard_map/ppermute | solution.py:35
  36.9 0.0 collective-permute-start.2
  36.9 2.3 %collective-permute-done.5.refs_3_.refs_8_ = bf16[528,512]{1,0:T(8,128)(2,1)} collective-permute-done((bf16[528,512]{1,0:T(8,128)(2,1)}, bf16[528,512]{1,0:T(8,128)(2,1)}, u32[]{:S(2)}, u32[]{:S(2)}) %collective-permute-start.5) | collective-permute-done | bytes 540704 | tf_op jit(solution)/shard_map/ppermute | solution.py:60
  39.2 2.0 collective-permute-start.6
  41.2 0.0 collective-permute-done.9.refs_2_.refs_7_
  41.2 1.2 collective-permute-done.8.refs_1_.refs_6_
  42.4 0.0 copy-done
  42.4 15.9 %shard_map.46 = (f32[256,3584]{1,0:T(8,128)S(1)}, f32[256,512]{1,0:T(8,128)S(1)}) custom-call(bf16[256,3584]{1,0:T(8,128)(2,1)S(1)} %copy-done, bf16[528,512]{1,0:T(8,128)(2,1)S(1)} %fusion.1.own.refs_13_, bf16[528,512]{1,0:T(8,128)(2,1)S(1)} %collective-permute-done.7.refs_0_.refs_5_, bf16[528,512]{1,0:T(8,128)(2,1)} %collective-permute-done.8.refs_1_.refs_6_, ...), custom_call_target="tpu_custom_call" | custom-call | flops 11274289152 | bytes 7240000 | tf_op jit(solution)/shard_map/pallas_call | solution.py:232
  58.3 0.0 collective-permute-done.6
  58.4 0.1 broadcast_select_fusion.refs_2_.refs_12_
  58.4 0.0 collective-permute-done.3.refs_1_.refs_11_
  58.4 0.0 collective-permute-done.2.refs_0_.refs_10_
  58.5 167.7 %shard_map.47 = bf16[256,3584]{1,0:T(8,128)(2,1)} custom-call(bf16[256,3584]{1,0:T(8,128)(2,1)S(1)} %copy-done, bf16[528,512]{1,0:T(8,128)(2,1)S(1)} %fusion.1.own.refs_13_, bf16[528,512]{1,0:T(8,128)(2,1)S(1)} %collective-permute-done.2.refs_0_.refs_10_, bf16[528,512]{1,0:T(8,128)(2,1)S(1)} %collective-permute-done.3.refs_1_.refs_11_, ...), custom_call_target="tpu_custom_call" | custom-call | flops 5637144576 | bytes 5620000 | tf_op jit(solution)/shard_map/pallas_call | solution.py:232
  (2 shorter events, 0.0 us)
Async XLA Ops:
  1.8 13.8 %collective-permute-start = (bf16[528,512]{1,0:T(8,128)(2,1)S(1)}, bf16[528,512]{1,0:T(8,128)(2,1)}, u32[]{:S(2)}, u32[]{:S(2)}) collective-permute-start(bf16[528,512]{1,0:T(8,128)(2,1)S(1)} %fusion.1.own.refs_13_), channel_id=1, source_target_pairs={{0,12},{1,13},{2,14},{3,15},{4,0},{5,1},{6,2},{7,3},{8,4},{9,5},{1... | collective-permute-start | bytes 1622024 | tf_op jit(solution)/shard_map/ppermute | solution.py:45
  4.6 16.4 %collective-permute-start.4 = (bf16[528,512]{1,0:T(8,128)(2,1)S(1)}, bf16[528,512]{1,0:T(8,128)(2,1)}, u32[]{:S(2)}, u32[]{:S(2)}) collective-permute-start(bf16[528,512]{1,0:T(8,128)(2,1)S(1)} %fusion.1.own.refs_13_), channel_id=1, source_target_pairs={{0,2},{1,3},{2,0},{3,1},{4,6},{5,7},{6,4},{7,5},{8,10},{9,11},{10,... | collective-permute-start | bytes 1622024 | tf_op jit(solution)/shard_map/ppermute | solution.py:35
  7.3 17.8 %collective-permute-start.7 = (bf16[528,512]{1,0:T(8,128)(2,1)S(1)}, bf16[528,512]{1,0:T(8,128)(2,1)S(1)}, u32[]{:S(2)}, u32[]{:S(2)}) collective-permute-start(bf16[528,512]{1,0:T(8,128)(2,1)S(1)} %fusion.1.own.refs_13_), channel_id=1, source_target_pairs={{0,4},{1,5},{2,6},{3,7},{4,8},{5,9},{6,10},{7,11},{8,12},{9,13},{1... | collective-permute-start | bytes 1622024 | tf_op jit(solution)/shard_map/ppermute | solution.py:60
  15.5 17.6 %collective-permute-start.1 = (bf16[528,512]{1,0:T(8,128)(2,1)}, bf16[528,512]{1,0:T(8,128)(2,1)S(1)}, u32[]{:S(2)}, u32[]{:S(2)}) collective-permute-start(bf16[528,512]{1,0:T(8,128)(2,1)} %collective-permute-done), channel_id=1, source_target_pairs={{12,8},{13,9},{14,10},{15,11},{0,12},{1,13},{2,14},{3,15},{4,16},{... | collective-permute-start | bytes 1622024 | tf_op jit(solution)/shard_map/ppermute | solution.py:56
  21.0 18.3 %collective-permute-start.5 = (bf16[528,512]{1,0:T(8,128)(2,1)}, bf16[528,512]{1,0:T(8,128)(2,1)}, u32[]{:S(2)}, u32[]{:S(2)}) collective-permute-start(bf16[528,512]{1,0:T(8,128)(2,1)} %collective-permute-done.4), channel_id=1, source_target_pairs={{0,4},{1,5},{2,6},{3,7},{4,8},{5,9},{6,10},{7,11},{8,12},{9,13},{1... | collective-permute-start | bytes 1622024 | tf_op jit(solution)/shard_map/ppermute | solution.py:60
  25.1 16.1 %collective-permute-start.9 = (bf16[528,512]{1,0:T(8,128)(2,1)S(1)}, bf16[528,512]{1,0:T(8,128)(2,1)}, u32[]{:S(2)}, u32[]{:S(2)}) collective-permute-start(bf16[528,512]{1,0:T(8,128)(2,1)S(1)} %collective-permute-done.7.refs_0_.refs_5_), channel_id=1, source_target_pairs={{0,3},{1,0},{2,1},{3,2},{4,7},{5,4},{6,5},{7,6},{8,11},{9,8},{10,9... | collective-permute-start | bytes 1622024 | tf_op jit(solution)/shard_map/ppermute | solution.py:35
  27.4 15.0 %collective-permute-start.8 = (bf16[528,512]{1,0:T(8,128)(2,1)S(1)}, bf16[528,512]{1,0:T(8,128)(2,1)}, u32[]{:S(2)}, u32[]{:S(2)}) collective-permute-start(bf16[528,512]{1,0:T(8,128)(2,1)S(1)} %collective-permute-done.7.refs_0_.refs_5_), channel_id=1, source_target_pairs={{0,1},{1,2},{2,3},{3,0},{4,5},{5,6},{6,7},{7,4},{8,9},{9,10},{10,1... | collective-permute-start | bytes 1622024 | tf_op jit(solution)/shard_map/ppermute | solution.py:35
  27.4 15.0 %copy-start = (bf16[256,3584]{1,0:T(8,128)(2,1)S(1)}, bf16[256,3584]{1,0:T(8,128)(2,1)}, u32[]{:S(2)}) copy-start(bf16[256,3584]{1,0:T(8,128)(2,1)} %q_ref.3) | copy-start | bytes 5505028
  34.4 24.1 %collective-permute-start.3 = (bf16[528,512]{1,0:T(8,128)(2,1)S(1)}, bf16[528,512]{1,0:T(8,128)(2,1)S(1)}, u32[]{:S(2)}, u32[]{:S(2)}) collective-permute-start(bf16[528,512]{1,0:T(8,128)(2,1)S(1)} %get-tuple-element.9), channel_id=1, source_target_pairs={{0,3},{1,0},{2,1},{3,2},{4,7},{5,4},{6,5},{7,6},{8,11},{9,8},{10,9... | collective-permute-start | bytes 1622024 | tf_op jit(solution)/shard_map/ppermute | solution.py:35
  36.9 21.5 %collective-permute-start.2 = (bf16[528,512]{1,0:T(8,128)(2,1)S(1)}, bf16[528,512]{1,0:T(8,128)(2,1)S(1)}, u32[]{:S(2)}, u32[]{:S(2)}) collective-permute-start(bf16[528,512]{1,0:T(8,128)(2,1)S(1)} %get-tuple-element.10), channel_id=1, source_target_pairs={{0,1},{1,2},{2,3},{3,0},{4,5},{5,6},{6,7},{7,4},{8,9},{9,10},{10,1... | collective-permute-start | bytes 1622024 | tf_op jit(solution)/shard_map/ppermute | solution.py:35
  39.2 19.1 %collective-permute-start.6 = (bf16[528,512]{1,0:T(8,128)(2,1)}, bf16[528,512]{1,0:T(8,128)(2,1)S(1)}, u32[]{:S(2)}, u32[]{:S(2)}) collective-permute-start(bf16[528,512]{1,0:T(8,128)(2,1)} %collective-permute-done.5.refs_3_.refs_8_), channel_id=1, source_target_pairs={{0,4},{1,5},{4,8},{5,9},{8,12},{9,13},{12,16},{13,17},{16,20},{17,... | collective-permute-start | bytes 1622024 | tf_op jit(solution)/shard_map/ppermute | solution.py:60

commit v4 on v3

--- a/solution.py
+++ b/solution.py
@@ -47,17 +47,16 @@
 
 def two_rows_on(value):
     pairs = [
-        (rank_of(plane, (y - 1) % 4, x), rank_of(plane, y, x) + 8)
+        (rank_of(plane, (y - 1) % 4, x), (rank_of(plane, y, x) + 8) % 256)
         for plane in range(16)
         for y in range(4)
         for x in range(4)
-        if rank_of(plane, y, x) + 8 < 256
     ]
     return lax.ppermute(value, AXES, pairs)
 
 
-def row_on(value, columns=range(4)):
-    return lax.ppermute(value, AXES, [(r, r + 4) for r in range(252) if r % 4 in columns])
+def row_on(value):
+    return lax.ppermute(value, AXES, [(r, (r + 4) % 256) for r in range(256)])
 
 
 def ids_down(rows):
@@ -172,12 +171,14 @@
     for g in range(GROUP):
         columns = slice(g * WIDTH, (g + 1) * WIDTH)
         q = q_ref[:, columns]
-        sums = term(q, blocks[0][0:TOKENS, :], 0)
-        for b in range(1, prior):
-            sums = sums + term(q, blocks[b][0:TOKENS, :], b)
-        inside = rows_in[...] > 0.5
-        mix = jnp.where(inside, sums[:, :WIDTH], 0.0)
-        weight = jnp.where(inside, sums[:, WIDTH:], 0.0)
+        mix, weight = 0.0, 0.0
+        if prior:
+            sums = term(q, blocks[0][0:TOKENS, :], 0)
+            for b in range(1, prior):
+                sums = sums + term(q, blocks[b][0:TOKENS, :], b)
+            inside = rows_in[...] > 0.5
+            mix = jnp.where(inside, sums[:, :WIDTH], 0.0)
+            weight = jnp.where(inside, sums[:, WIDTH:], 0.0)
         if has_own:
             sums = term(q, own[0:TOKENS, :], prior, causal[...])
             mix = mix + sums[:, :WIDTH]
@@ -217,7 +218,7 @@
         ]
     scratch = [
         pltpu.VMEM((count, TOKENS, 2 * WIDTH), jnp.bfloat16),
-        pltpu.VMEM((len(blocks), TOKENS, WIDTH), jnp.bfloat16),
+        pltpu.VMEM((max(len(blocks), 1), TOKENS, WIDTH), jnp.bfloat16),
         pltpu.VMEM((TOKENS, TOKENS), jnp.float32),
         pltpu.VMEM((TOKENS, WIDTH), jnp.float32),
     ]
@@ -253,18 +254,21 @@
     ids = jnp.pad(jnp.tile(ids, (1, KEY_VALUE_HEADS)), ((0, EXTRA - 2), (0, 0)))
     own = jnp.concatenate([key_states, value_vectors, ids], axis=0)
     x = lax.axis_index("seq") % 4
+    own = lax.optimization_barrier(own)
     four = row_on(own)
     back = turned_along_y(own, -1)
     across = turned_along_x(own, 2)
+    stage = attention(queries, own, [], True, [], [], False)
+    four, back, across, *stage = lax.optimization_barrier((four, back, across, *stage))
     middle = [turned_along_x(four, a) for a in (1, 3)]
     eight = two_rows_on(back)
     next_across = row_on(across)
     ends = [turned_along_x(jnp.where(x + a < 4, own, eight), a) for a in (1, 3)]
-    far_across = row_on(next_across, (0, 1))
+    far_across = row_on(next_across)
     across = jnp.where(x < 2, far_across, across)
     early = [four, *middle, next_across, eight]
     late = [*ends, across]
-    stage = attention(queries, own, early, True, [], [], False)
+    stage = attention(queries, own, early, False, stage, [], False)
     return attention(queries, own, late, False, stage, [*early, *late, own], True)
 
 

time: 228 us -> 215 us (0.943)
  Pallas kernels: 184 us -> 173 us
  local copies, waits for them, and re-layouts: 0.02 us -> 7.17 us
  starting transfers between devices: 23.5 us -> 18.1 us
  waiting for transfers between devices: 15.9 us -> 12.5 us
    pallas_call x2 -> x3, Pallas kernels: 184 us -> 173 us  [attention(): pl.pallas_call(functools.partial(attend, len(blocks), has_own, bool(befor...]
    unnamed x4 -> x14, local copies, waits for them, and re-layouts: 0.02 us -> 7.17 us
    ppermute x1, waiting for transfers between devices: 6.28 us -> 0.01 us  [turned_along_y(): return lax.ppermute(value, AXES, pairs)]
    ppermute x3, starting transfers between devices: 7.74 us -> 3.69 us  [row_on(): return lax.ppermute(value, AXES, [(r, (r + 4) % 256) for r in range(256)])]
    ppermute x1, starting transfers between devices: 5.41 us -> 1.77 us  [two_rows_on(): return lax.ppermute(value, AXES, pairs)]
    ppermute x5, waiting for transfers between devices: 1.18 us -> 4.04 us  [turned_along_x(): return lax.ppermute(value, AXES, pairs)]
  transfers between devices with their start and end apart: 10 -> 10, of which waited for: 5 -> 6; matrix products, arithmetic and copies ran while one was open for 1% -> 0% of each run, Pallas kernels for 7% -> 8%
where the time goes in v4:
time: 215 us; the launch traced here: 213 us
  Pallas kernels  173 us (80%)
  starting transfers between devices  18.1 us (8%)
  waiting for transfers between devices  12.5 us (6%)
  local copies, waits for them, and re-layouts  7.17 us (3%)
    pallas_call x3, Pallas kernels, attention(): pl.pallas_call(functools.partial(attend, len(blocks), has_own, bool(befor...  173 us
    ppermute x5, starting transfers between devices, turned_along_x(): return lax.ppermute(value, AXES, pairs)  8.17 us
    ppermute x1, waiting for transfers between devices, two_rows_on(): return lax.ppermute(value, AXES, pairs)  7.59 us
    unnamed x14, local copies, waits for them, and re-layouts  7.17 us
    ppermute x1, starting transfers between devices, turned_along_y(): return lax.ppermute(value, AXES, pairs)  4.51 us
  transfers between devices with their start and end apart: 10, of which 6 were waited for; matrix products, arithmetic and copies ran while one was open for 0% of the time, Pallas kernels for 8%

profile of v4, /device:TPU:97, one launch (start us, length us, event | category | flops | bytes accessed | tf_op | source)
XLA Modules:
  0.0 213.3 jit_solution(7698830754529479186)
XLA Ops:
  0.0 0.7 fusion.2
  0.7 1.1 fusion.1.own.refs_13_
  1.8 1.4 collective-permute-start
  3.1 4.5 %collective-permute-start.1 = (bf16[528,512]{1,0:T(8,128)(2,1)S(1)}, bf16[528,512]{1,0:T(8,128)(2,1)}, u32[]{:S(2)}, u32[]{:S(2)}) collective-permute-start(bf16[528,512]{1,0:T(8,128)(2,1)S(1)} %fusion.1.own.refs_13_), channel_id=1, source_target_pairs={{0,12},{1,13},{2,14},{3,15},{4,0},{5,1},{6,2},{7,3},{8,4},{9,5},{1... | collective-permute-start | bytes 1622024 | tf_op jit(solution)/shard_map/ppermute | solution.py:45
  7.7 2.7 %collective-permute-start.2 = (bf16[528,512]{1,0:T(8,128)(2,1)S(1)}, bf16[528,512]{1,0:T(8,128)(2,1)}, u32[]{:S(2)}, u32[]{:S(2)}) collective-permute-start(bf16[528,512]{1,0:T(8,128)(2,1)S(1)} %fusion.1.own.refs_13_), channel_id=1, source_target_pairs={{0,2},{1,3},{2,0},{3,1},{4,6},{5,7},{6,4},{7,5},{8,10},{9,11},{10,... | collective-permute-start | bytes 1622024 | tf_op jit(solution)/shard_map/ppermute | solution.py:35
  10.4 0.0 copy-start
  10.4 1.5 copy-done
  11.9 3.7 %shard_map.46 = (f32[256,3584]{1,0:T(8,128)S(1)}, f32[256,512]{1,0:T(8,128)S(1)}) custom-call(bf16[256,3584]{1,0:T(8,128)(2,1)S(1)} %copy-done, bf16[528,512]{1,0:T(8,128)(2,1)S(1)} %fusion.1.own.refs_13_), custom_call_target="tpu_custom_call" | custom-call | flops 1879048192 | bytes 4540000 | tf_op jit(solution)/shard_map/pallas_call | solution.py:233
  15.6 0.0 copy-start.2
  15.6 1.8 copy-done.2
  17.3 0.0 copy-start.4
  17.3 0.8 copy-done.4
  18.1 0.2 collective-permute-done.refs_0_.refs_5_
  18.4 0.0 collective-permute-done.1
  18.4 3.3 %collective-permute-done.2 = bf16[528,512]{1,0:T(8,128)(2,1)} collective-permute-done((bf16[528,512]{1,0:T(8,128)(2,1)S(1)}, bf16[528,512]{1,0:T(8,128)(2,1)}, u32[]{:S(2)}, u32[]{:S(2)}) %collective-permute-start.2) | collective-permute-done | bytes 540704 | tf_op jit(solution)/shard_map/ppermute | solution.py:35
  21.7 1.8 collective-permute-start.3
  23.5 2.3 %collective-permute-start.6 = (bf16[528,512]{1,0:T(8,128)(2,1)}, bf16[528,512]{1,0:T(8,128)(2,1)S(1)}, u32[]{:S(2)}, u32[]{:S(2)}) collective-permute-start(bf16[528,512]{1,0:T(8,128)(2,1)} %collective-permute-done.2), channel_id=1, source_target_pairs={{0,4},{1,5},{2,6},{3,7},{4,8},{5,9},{6,10},{7,11},{8,12},{9,13},{1... | collective-permute-start | bytes 1622024 | tf_op jit(solution)/shard_map/ppermute | solution.py:59
  25.8 1.2 collective-permute-start.8
  27.0 1.5 collective-permute-start.9
  28.5 0.0 copy-start.1
  28.5 7.6 %collective-permute-done.3.refs_4_.refs_9_ = bf16[528,512]{1,0:T(8,128)(2,1)S(1)} collective-permute-done((bf16[528,512]{1,0:T(8,128)(2,1)}, bf16[528,512]{1,0:T(8,128)(2,1)S(1)}, u32[]{:S(2)}, u32[]{:S(2)}) %collective-permute-start.3) | collective-permute-done | bytes 540704 | tf_op jit(solution)/shard_map/ppermute | solution.py:55
  36.0 0.1 broadcast_select_fusion.1
  36.1 1.3 collective-permute-start.4
  37.4 1.5 collective-permute-start.5
  38.9 0.6 collective-permute-done.6.refs_3_.refs_8_
  39.5 0.0 collective-permute-start.7
  39.5 0.4 collective-permute-done.8.refs_1_.refs_6_
  39.9 0.3 collective-permute-done.9.refs_2_.refs_7_
  40.2 0.0 copy-done.1
  40.2 0.0 copy-start.3
  40.2 2.0 copy-done.3
  42.2 0.0 copy-start.5
  42.2 1.0 copy-done.5
  43.3 12.6 %shard_map.47 = (f32[256,3584]{1,0:T(8,128)S(1)}, f32[256,512]{1,0:T(8,128)S(1)}) custom-call(bf16[256,3584]{1,0:T(8,128)(2,1)S(1)} %copy-done.1, bf16[528,512]{1,0:T(8,128)(2,1)S(1)} %fusion.1.own.refs_13_, bf16[528,512]{1,0:T(8,128)(2,1)S(1)} %collective-permute-done.refs_0_.refs_5_, bf16[528,512]{1,0:T(8,128)(2,1)S(1)} %collective-permute-done.8.refs_1_.refs_6_, ...), custom_call_target="tpu_custom_call" | custom-call | flops 9395240960 | bytes 6700000 | tf_op jit(solution)/shard_map/pallas_call | solution.py:233
  55.9 0.0 collective-permute-done.7
  55.9 0.1 broadcast_select_fusion.refs_2_.refs_12_
  56.0 0.0 collective-permute-done.4.refs_0_.refs_10_
  56.0 0.0 collective-permute-done.5.refs_1_.refs_11_
  56.0 157.1 %shard_map.48 = bf16[256,3584]{1,0:T(8,128)(2,1)} custom-call(bf16[256,3584]{1,0:T(8,128)(2,1)S(1)} %copy-done.1, bf16[528,512]{1,0:T(8,128)(2,1)S(1)} %fusion.1.own.refs_13_, bf16[528,512]{1,0:T(8,128)(2,1)S(1)} %collective-permute-done.4.refs_0_.refs_10_, bf16[528,512]{1,0:T(8,128)(2,1)S(1)} %collective-permute-done.5.refs_1_.refs_11_, ...), custom_call_target="tpu_custom_call" | custom-call | flops 5637144576 | bytes 5620000 | tf_op jit(solution)/shard_map/pallas_call | solution.py:233
  (2 shorter events, 0.0 us)
Async XLA Ops:
  1.8 16.6 %collective-permute-start = (bf16[528,512]{1,0:T(8,128)(2,1)S(1)}, bf16[528,512]{1,0:T(8,128)(2,1)S(1)}, u32[]{:S(2)}, u32[]{:S(2)}) collective-permute-start(bf16[528,512]{1,0:T(8,128)(2,1)S(1)} %fusion.1.own.refs_13_), channel_id=1, source_target_pairs={{0,4},{1,5},{2,6},{3,7},{4,8},{5,9},{6,10},{7,11},{8,12},{9,13},{1... | collective-permute-start | bytes 1622024 | tf_op jit(solution)/shard_map/ppermute | solution.py:59
  3.1 15.2 %collective-permute-start.1 = (bf16[528,512]{1,0:T(8,128)(2,1)S(1)}, bf16[528,512]{1,0:T(8,128)(2,1)}, u32[]{:S(2)}, u32[]{:S(2)}) collective-permute-start(bf16[528,512]{1,0:T(8,128)(2,1)S(1)} %fusion.1.own.refs_13_), channel_id=1, source_target_pairs={{0,12},{1,13},{2,14},{3,15},{4,0},{5,1},{6,2},{7,3},{8,4},{9,5},{1... | collective-permute-start | bytes 1622024 | tf_op jit(solution)/shard_map/ppermute | solution.py:45
  7.7 14.0 %collective-permute-start.2 = (bf16[528,512]{1,0:T(8,128)(2,1)S(1)}, bf16[528,512]{1,0:T(8,128)(2,1)}, u32[]{:S(2)}, u32[]{:S(2)}) collective-permute-start(bf16[528,512]{1,0:T(8,128)(2,1)S(1)} %fusion.1.own.refs_13_), channel_id=1, source_target_pairs={{0,2},{1,3},{2,0},{3,1},{4,6},{5,7},{6,4},{7,5},{8,10},{9,11},{10,... | collective-permute-start | bytes 1622024 | tf_op jit(solution)/shard_map/ppermute | solution.py:35
  10.4 1.5 copy-start
  15.6 1.8 copy-start.2
  17.3 0.8 copy-start.4
  21.7 14.3 %collective-permute-start.3 = (bf16[528,512]{1,0:T(8,128)(2,1)}, bf16[528,512]{1,0:T(8,128)(2,1)S(1)}, u32[]{:S(2)}, u32[]{:S(2)}) collective-permute-start(bf16[528,512]{1,0:T(8,128)(2,1)} %collective-permute-done.1), channel_id=1, source_target_pairs={{12,8},{13,9},{14,10},{15,11},{0,12},{1,13},{2,14},{3,15},{4,16},{... | collective-permute-start | bytes 1622024 | tf_op jit(solution)/shard_map/ppermute | solution.py:55
  23.5 16.0 %collective-permute-start.6 = (bf16[528,512]{1,0:T(8,128)(2,1)}, bf16[528,512]{1,0:T(8,128)(2,1)S(1)}, u32[]{:S(2)}, u32[]{:S(2)}) collective-permute-start(bf16[528,512]{1,0:T(8,128)(2,1)} %collective-permute-done.2), channel_id=1, source_target_pairs={{0,4},{1,5},{2,6},{3,7},{4,8},{5,9},{6,10},{7,11},{8,12},{9,13},{1... | collective-permute-start | bytes 1622024 | tf_op jit(solution)/shard_map/ppermute | solution.py:59
  25.8 14.1 %collective-permute-start.8 = (bf16[528,512]{1,0:T(8,128)(2,1)S(1)}, bf16[528,512]{1,0:T(8,128)(2,1)S(1)}, u32[]{:S(2)}, u32[]{:S(2)}) collective-permute-start(bf16[528,512]{1,0:T(8,128)(2,1)S(1)} %collective-permute-done.refs_0_.refs_5_), channel_id=1, source_target_pairs={{0,1},{1,2},{2,3},{3,0},{4,5},{5,6},{6,7},{7,4},{8,9},{9,10},{10,1... | collective-permute-start | bytes 1622024 | tf_op jit(solution)/shard_map/ppermute | solution.py:35
  27.0 13.2 %collective-permute-start.9 = (bf16[528,512]{1,0:T(8,128)(2,1)S(1)}, bf16[528,512]{1,0:T(8,128)(2,1)S(1)}, u32[]{:S(2)}, u32[]{:S(2)}) collective-permute-start(bf16[528,512]{1,0:T(8,128)(2,1)S(1)} %collective-permute-done.refs_0_.refs_5_), channel_id=1, source_target_pairs={{0,3},{1,0},{2,1},{3,2},{4,7},{5,4},{6,5},{7,6},{8,11},{9,8},{10,9... | collective-permute-start | bytes 1622024 | tf_op jit(solution)/shard_map/ppermute | solution.py:35
  28.5 11.7 %copy-start.1 = (bf16[256,3584]{1,0:T(8,128)(2,1)S(1)}, bf16[256,3584]{1,0:T(8,128)(2,1)}, u32[]{:S(2)}) copy-start(bf16[256,3584]{1,0:T(8,128)(2,1)} %q_ref.5) | copy-start | bytes 5505028
  36.1 19.9 %collective-permute-start.4 = (bf16[528,512]{1,0:T(8,128)(2,1)S(1)}, bf16[528,512]{1,0:T(8,128)(2,1)S(1)}, u32[]{:S(2)}, u32[]{:S(2)}) collective-permute-start(bf16[528,512]{1,0:T(8,128)(2,1)S(1)} %get-tuple-element.24), channel_id=1, source_target_pairs={{0,1},{1,2},{2,3},{3,0},{4,5},{5,6},{6,7},{7,4},{8,9},{9,10},{10,1... | collective-permute-start | bytes 1622024 | tf_op jit(solution)/shard_map/ppermute | solution.py:35
  37.4 18.6 %collective-permute-start.5 = (bf16[528,512]{1,0:T(8,128)(2,1)S(1)}, bf16[528,512]{1,0:T(8,128)(2,1)S(1)}, u32[]{:S(2)}, u32[]{:S(2)}) collective-permute-start(bf16[528,512]{1,0:T(8,128)(2,1)S(1)} %get-tuple-element.23), channel_id=1, source_target_pairs={{0,3},{1,0},{2,1},{3,2},{4,7},{5,4},{6,5},{7,6},{8,11},{9,8},{10,9... | collective-permute-start | bytes 1622024 | tf_op jit(solution)/shard_map/ppermute | solution.py:35
  39.5 16.5 %collective-permute-start.7 = (bf16[528,512]{1,0:T(8,128)(2,1)S(1)}, bf16[528,512]{1,0:T(8,128)(2,1)S(1)}, u32[]{:S(2)}, u32[]{:S(2)}) collective-permute-start(bf16[528,512]{1,0:T(8,128)(2,1)S(1)} %collective-permute-done.6.refs_3_.refs_8_), channel_id=1, source_target_pairs={{0,4},{1,5},{2,6},{3,7},{4,8},{5,9},{6,10},{7,11},{8,12},{9,13},{1... | collective-permute-start | bytes 1622024 | tf_op jit(solution)/shard_map/ppermute | solution.py:59
  40.2 2.0 copy-start.3
  42.2 1.0 copy-start.5

commit v5 on v4

--- a/solution.py
+++ b/solution.py
@@ -16,7 +16,7 @@
 AXES = ("dp", "seq")
 SCALE = 1.4426950408889634 / WIDTH**0.5
 LOW, HIGH = 1e-25, 1e30
-VMEM_LIMIT = 24 * 1024 * 1024
+VMEM_LIMIT = 16 * 1024 * 1024
 NT = (((1,), (1,)), ((), ()))
 NN = (((1,), (0,)), ((), ()))
 
@@ -127,7 +127,7 @@
     blocks = take(prior)
     before = take(2) if has_before else None
     whole = take(whole_count)
-    outs = take(1 if last else 2)
+    outs = take(1 if last else 3)
     mixed, picked, causal, rows_in = take(4)
     head = pl.program_id(0)
     count = prior + has_own
@@ -200,6 +200,7 @@
             general_head(head, whole, q_ref, outs[0], *refs)
     else:
         outs[1][...] = weights
+        outs[2][...] = jnp.zeros_like(outs[2])
 
 
 def attention(queries, own, blocks, has_own, before, whole, last):
@@ -211,10 +212,11 @@
         out_specs = wide
         out_shape = jax.ShapeDtypeStruct(queries.shape, jnp.bfloat16)
     else:
-        out_specs = [wide, narrow]
+        out_specs = [wide, narrow, by_head(8, WIDTH)]
         out_shape = [
             jax.ShapeDtypeStruct(queries.shape, jnp.float32),
             jax.ShapeDtypeStruct((TOKENS, KEY_VALUE_HEADS * WIDTH), jnp.float32),
+            jax.ShapeDtypeStruct((8, KEY_VALUE_HEADS * WIDTH), jnp.float32),
         ]
     scratch = [
         pltpu.VMEM((count, TOKENS, 2 * WIDTH), jnp.bfloat16),
@@ -258,18 +260,18 @@
     four = row_on(own)
     back = turned_along_y(own, -1)
     across = turned_along_x(own, 2)
-    stage = attention(queries, own, [], True, [], [], False)
-    four, back, across, *stage = lax.optimization_barrier((four, back, across, *stage))
     middle = [turned_along_x(four, a) for a in (1, 3)]
     eight = two_rows_on(back)
     next_across = row_on(across)
+    *stage, done = attention(queries, own, [four], True, [], [], False)
+    eight, _ = lax.optimization_barrier((eight, done))
     ends = [turned_along_x(jnp.where(x + a < 4, own, eight), a) for a in (1, 3)]
     far_across = row_on(next_across)
     across = jnp.where(x < 2, far_across, across)
-    early = [four, *middle, next_across, eight]
+    early = [*middle, next_across, eight]
     late = [*ends, across]
-    stage = attention(queries, own, early, False, stage, [], False)
-    return attention(queries, own, late, False, stage, [*early, *late, own], True)
+    *stage, _ = attention(queries, own, early, False, stage, [], False)
+    return attention(queries, own, late, False, stage, [four, *early, *late, own], True)
 
 
 def solution(mesh):

time: 215 us -> 212 us (0.986)
  local copies, waits for them, and re-layouts: 7.17 us -> 1.51 us
  waiting for transfers between devices: 12.5 us -> 16.1 us
  starting transfers between devices: 18.1 us -> 15 us
    ppermute x1, waiting for transfers between devices: 0.01 us -> 8.2 us  [turned_along_y(): return lax.ppermute(value, AXES, pairs)]
    ppermute x1, waiting for transfers between devices: 7.59 us -> 0.01 us  [two_rows_on(): return lax.ppermute(value, AXES, pairs)]
    ppermute x3, waiting for transfers between devices: 0.83 us -> 7.91 us  [row_on(): return lax.ppermute(value, AXES, [(r, (r + 4) % 256) for r in range(256)])]
    unnamed x14 -> x4, local copies, waits for them, and re-layouts: 7.17 us -> 1.51 us
    ppermute x5, waiting for transfers between devices: 4.04 us -> 0.01 us  [turned_along_x(): return lax.ppermute(value, AXES, pairs)]
    ppermute x3, starting transfers between devices: 3.69 us -> 0.61 us  [row_on(): return lax.ppermute(value, AXES, [(r, (r + 4) % 256) for r in range(256)])]
  transfers between devices with their start and end apart: 10 -> 10, of which waited for: 6 -> 4; matrix products, arithmetic and copies ran while one was open for 0% -> 0% of each run, Pallas kernels for 8% -> 8%
where the time goes in v5:
time: 212 us; the launch traced here: 210 us
  Pallas kernels  175 us (83%)
  waiting for transfers between devices  16.1 us (8%)
  starting transfers between devices  15 us (7%)
    pallas_call x3, Pallas kernels, attention(): pl.pallas_call(functools.partial(attend, len(blocks), has_own, bool(befor...  175 us
    ppermute x1, waiting for transfers between devices, turned_along_y(): return lax.ppermute(value, AXES, pairs)  8.2 us
    ppermute x5, starting transfers between devices, turned_along_x(): return lax.ppermute(value, AXES, pairs)  8.17 us
    ppermute x3, waiting for transfers between devices, row_on(): return lax.ppermute(value, AXES, [(r, (r + 4) % 256) for r in range(256)])  7.91 us
  transfers between devices with their start and end apart: 10, of which 4 were waited for; matrix products, arithmetic and copies ran while one was open for 0% of the time, Pallas kernels for 8%

profile of v5, /device:TPU:97, one launch (start us, length us, event | category | flops | bytes accessed | tf_op | source)
XLA Modules:
  0.0 209.5 jit_solution(1760832662028712510)
XLA Ops:
  0.0 0.7 fusion.2
  0.7 1.1 fusion.1.own.refs_13_
  1.8 2.8 %collective-permute-start = (bf16[528,512]{1,0:T(8,128)(2,1)S(1)}, bf16[528,512]{1,0:T(8,128)(2,1)S(1)}, u32[]{:S(2)}, u32[]{:S(2)}) collective-permute-start(bf16[528,512]{1,0:T(8,128)(2,1)S(1)} %fusion.1.own.refs_13_), channel_id=1, source_target_pairs={{0,12},{1,13},{2,14},{3,15},{4,0},{5,1},{6,2},{7,3},{8,4},{9,5},{1... | collective-permute-start | bytes 1622024 | tf_op jit(solution)/shard_map/ppermute | solution.py:45
  4.6 0.0 collective-permute-start.7
  4.6 2.7 %collective-permute-start.4 = (bf16[528,512]{1,0:T(8,128)(2,1)S(1)}, bf16[528,512]{1,0:T(8,128)(2,1)S(1)}, u32[]{:S(2)}, u32[]{:S(2)}) collective-permute-start(bf16[528,512]{1,0:T(8,128)(2,1)S(1)} %fusion.1.own.refs_13_), channel_id=1, source_target_pairs={{0,2},{1,3},{2,0},{3,1},{4,6},{5,7},{6,4},{7,5},{8,10},{9,11},{10,... | collective-permute-start | bytes 1622024 | tf_op jit(solution)/shard_map/ppermute | solution.py:35
  7.3 8.2 %collective-permute-done = bf16[528,512]{1,0:T(8,128)(2,1)S(1)} collective-permute-done((bf16[528,512]{1,0:T(8,128)(2,1)S(1)}, bf16[528,512]{1,0:T(8,128)(2,1)S(1)}, u32[]{:S(2)}, u32[]{:S(2)}) %collective-permute-start) | collective-permute-done | bytes 540704 | tf_op jit(solution)/shard_map/ppermute | solution.py:45
  15.5 3.4 %collective-permute-start.1 = (bf16[528,512]{1,0:T(8,128)(2,1)S(1)}, bf16[528,512]{1,0:T(8,128)(2,1)S(1)}, u32[]{:S(2)}, u32[]{:S(2)}) collective-permute-start(bf16[528,512]{1,0:T(8,128)(2,1)S(1)} %collective-permute-done), channel_id=1, source_target_pairs={{12,8},{13,9},{14,10},{15,11},{0,12},{1,13},{2,14},{3,15},{4,16},{... | collective-permute-start | bytes 1622024 | tf_op jit(solution)/shard_map/ppermute | solution.py:55
  18.9 1.4 collective-permute-done.7.refs_0_.refs_5_
  20.4 1.2 collective-permute-start.8
  21.6 1.5 collective-permute-start.9
  23.1 0.0 collective-permute-done.4
  23.1 0.6 collective-permute-start.5
  23.7 0.0 copy-start
  23.7 1.5 copy-done
  25.2 6.4 %shard_map.46 = (f32[256,3584]{1,0:T(8,128)S(1)}, f32[256,512]{1,0:T(8,128)S(1)}, f32[8,512]{1,0:T(8,128)}) custom-call(bf16[256,3584]{1,0:T(8,128)(2,1)S(1)} %copy-done, bf16[528,512]{1,0:T(8,128)(2,1)S(1)} %fusion.1.own.refs_13_, bf16[528,512]{1,0:T(8,128)(2,1)S(1)} %collective-permute-done.7.refs_0_.refs_5_), custom_call_target="tpu_custom_call" | custom-call | flops 3758096384 | bytes 5080000 | tf_op jit(solution)/shard_map/pallas_call | solution.py:235
  31.6 0.0 collective-permute-done.1.refs_3_.refs_9_
  31.6 0.1 broadcast_select_fusion.1
  31.6 0.6 collective-permute-start.2
  32.2 2.2 %collective-permute-start.3 = (bf16[528,512]{1,0:T(8,128)(2,1)S(1)}, bf16[528,512]{1,0:T(8,128)(2,1)S(1)}, u32[]{:S(2)}, u32[]{:S(2)}) collective-permute-start(bf16[528,512]{1,0:T(8,128)(2,1)S(1)} %get-tuple-element.13), channel_id=1, source_target_pairs={{0,3},{1,0},{2,1},{3,2},{4,7},{5,4},{6,5},{7,6},{8,11},{9,8},{10,9... | collective-permute-start | bytes 1622024 | tf_op jit(solution)/shard_map/ppermute | solution.py:35
  34.4 4.8 %collective-permute-done.5.refs_2_.refs_8_ = bf16[528,512]{1,0:T(8,128)(2,1)S(1)} collective-permute-done((bf16[528,512]{1,0:T(8,128)(2,1)S(1)}, bf16[528,512]{1,0:T(8,128)(2,1)S(1)}, u32[]{:S(2)}, u32[]{:S(2)}) %collective-permute-start.5) | collective-permute-done | bytes 540704 | tf_op jit(solution)/shard_map/ppermute | solution.py:59
  39.1 0.0 collective-permute-start.6
  39.1 0.0 collective-permute-done.8.refs_0_.refs_6_
  39.2 0.0 collective-permute-done.9.refs_1_.refs_7_
  39.2 11.3 %shard_map.47 = (f32[256,3584]{1,0:T(8,128)S(1)}, f32[256,512]{1,0:T(8,128)S(1)}, f32[8,512]{1,0:T(8,128)}) custom-call(bf16[256,3584]{1,0:T(8,128)(2,1)S(1)} %copy-done, bf16[528,512]{1,0:T(8,128)(2,1)S(1)} %fusion.1.own.refs_13_, bf16[528,512]{1,0:T(8,128)(2,1)S(1)} %collective-permute-done.8.refs_0_.refs_6_, ...), custom_call_target="tpu_custom_call" | custom-call | flops 7516192768 | bytes 6160000 | tf_op jit(solution)/shard_map/pallas_call | solution.py:235
  50.4 1.7 collective-permute-done.6
  52.2 0.1 broadcast_select_fusion.refs_2_.refs_12_
  52.2 0.0 collective-permute-done.2.refs_0_.refs_10_
  52.2 0.0 collective-permute-done.3.refs_1_.refs_11_
  52.2 157.1 %shard_map.48 = bf16[256,3584]{1,0:T(8,128)(2,1)} custom-call(bf16[256,3584]{1,0:T(8,128)(2,1)S(1)} %copy-done, bf16[528,512]{1,0:T(8,128)(2,1)S(1)} %fusion.1.own.refs_13_, bf16[528,512]{1,0:T(8,128)(2,1)S(1)} %collective-permute-done.2.refs_0_.refs_10_, bf16[528,512]{1,0:T(8,128)(2,1)S(1)} %collective-permute-done.3.refs_1_.refs_11_, ...), custom_call_target="tpu_custom_call" | custom-call | flops 5637144576 | bytes 5620000 | tf_op jit(solution)/shard_map/pallas_call | solution.py:235
  (2 shorter events, 0.0 us)
Async XLA Ops:
  1.8 13.8 %collective-permute-start = (bf16[528,512]{1,0:T(8,128)(2,1)S(1)}, bf16[528,512]{1,0:T(8,128)(2,1)S(1)}, u32[]{:S(2)}, u32[]{:S(2)}) collective-permute-start(bf16[528,512]{1,0:T(8,128)(2,1)S(1)} %fusion.1.own.refs_13_), channel_id=1, source_target_pairs={{0,12},{1,13},{2,14},{3,15},{4,0},{5,1},{6,2},{7,3},{8,4},{9,5},{1... | collective-permute-start | bytes 1622024 | tf_op jit(solution)/shard_map/ppermute | solution.py:45
  4.6 15.8 %collective-permute-start.7 = (bf16[528,512]{1,0:T(8,128)(2,1)S(1)}, bf16[528,512]{1,0:T(8,128)(2,1)S(1)}, u32[]{:S(2)}, u32[]{:S(2)}) collective-permute-start(bf16[528,512]{1,0:T(8,128)(2,1)S(1)} %fusion.1.own.refs_13_), channel_id=1, source_target_pairs={{0,4},{1,5},{2,6},{3,7},{4,8},{5,9},{6,10},{7,11},{8,12},{9,13},{1... | collective-permute-start | bytes 1622024 | tf_op jit(solution)/shard_map/ppermute | solution.py:59
  4.6 18.5 %collective-permute-start.4 = (bf16[528,512]{1,0:T(8,128)(2,1)S(1)}, bf16[528,512]{1,0:T(8,128)(2,1)S(1)}, u32[]{:S(2)}, u32[]{:S(2)}) collective-permute-start(bf16[528,512]{1,0:T(8,128)(2,1)S(1)} %fusion.1.own.refs_13_), channel_id=1, source_target_pairs={{0,2},{1,3},{2,0},{3,1},{4,6},{5,7},{6,4},{7,5},{8,10},{9,11},{10,... | collective-permute-start | bytes 1622024 | tf_op jit(solution)/shard_map/ppermute | solution.py:35
  15.5 16.0 %collective-permute-start.1 = (bf16[528,512]{1,0:T(8,128)(2,1)S(1)}, bf16[528,512]{1,0:T(8,128)(2,1)S(1)}, u32[]{:S(2)}, u32[]{:S(2)}) collective-permute-start(bf16[528,512]{1,0:T(8,128)(2,1)S(1)} %collective-permute-done), channel_id=1, source_target_pairs={{12,8},{13,9},{14,10},{15,11},{0,12},{1,13},{2,14},{3,15},{4,16},{... | collective-permute-start | bytes 1622024 | tf_op jit(solution)/shard_map/ppermute | solution.py:55
  20.4 18.8 %collective-permute-start.8 = (bf16[528,512]{1,0:T(8,128)(2,1)S(1)}, bf16[528,512]{1,0:T(8,128)(2,1)S(1)}, u32[]{:S(2)}, u32[]{:S(2)}) collective-permute-start(bf16[528,512]{1,0:T(8,128)(2,1)S(1)} %collective-permute-done.7.refs_0_.refs_5_), channel_id=1, source_target_pairs={{0,1},{1,2},{2,3},{3,0},{4,5},{5,6},{6,7},{7,4},{8,9},{9,10},{10,1... | collective-permute-start | bytes 1622024 | tf_op jit(solution)/shard_map/ppermute | solution.py:35
  21.6 17.6 %collective-permute-start.9 = (bf16[528,512]{1,0:T(8,128)(2,1)S(1)}, bf16[528,512]{1,0:T(8,128)(2,1)S(1)}, u32[]{:S(2)}, u32[]{:S(2)}) collective-permute-start(bf16[528,512]{1,0:T(8,128)(2,1)S(1)} %collective-permute-done.7.refs_0_.refs_5_), channel_id=1, source_target_pairs={{0,3},{1,0},{2,1},{3,2},{4,7},{5,4},{6,5},{7,6},{8,11},{9,8},{10,9... | collective-permute-start | bytes 1622024 | tf_op jit(solution)/shard_map/ppermute | solution.py:35
  23.1 16.1 %collective-permute-start.5 = (bf16[528,512]{1,0:T(8,128)(2,1)S(1)}, bf16[528,512]{1,0:T(8,128)(2,1)S(1)}, u32[]{:S(2)}, u32[]{:S(2)}) collective-permute-start(bf16[528,512]{1,0:T(8,128)(2,1)S(1)} %collective-permute-done.4), channel_id=1, source_target_pairs={{0,4},{1,5},{2,6},{3,7},{4,8},{5,9},{6,10},{7,11},{8,12},{9,13},{1... | collective-permute-start | bytes 1622024 | tf_op jit(solution)/shard_map/ppermute | solution.py:59
  23.7 1.5 copy-start
  31.6 20.6 %collective-permute-start.2 = (bf16[528,512]{1,0:T(8,128)(2,1)S(1)}, bf16[528,512]{1,0:T(8,128)(2,1)S(1)}, u32[]{:S(2)}, u32[]{:S(2)}) collective-permute-start(bf16[528,512]{1,0:T(8,128)(2,1)S(1)} %get-tuple-element.14), channel_id=1, source_target_pairs={{0,1},{1,2},{2,3},{3,0},{4,5},{5,6},{6,7},{7,4},{8,9},{9,10},{10,1... | collective-permute-start | bytes 1622024 | tf_op jit(solution)/shard_map/ppermute | solution.py:35
  32.2 20.0 %collective-permute-start.3 = (bf16[528,512]{1,0:T(8,128)(2,1)S(1)}, bf16[528,512]{1,0:T(8,128)(2,1)S(1)}, u32[]{:S(2)}, u32[]{:S(2)}) collective-permute-start(bf16[528,512]{1,0:T(8,128)(2,1)S(1)} %get-tuple-element.13), channel_id=1, source_target_pairs={{0,3},{1,0},{2,1},{3,2},{4,7},{5,4},{6,5},{7,6},{8,11},{9,8},{10,9... | collective-permute-start | bytes 1622024 | tf_op jit(solution)/shard_map/ppermute | solution.py:35
  39.1 13.0 %collective-permute-start.6 = (bf16[528,512]{1,0:T(8,128)(2,1)S(1)}, bf16[528,512]{1,0:T(8,128)(2,1)S(1)}, u32[]{:S(2)}, u32[]{:S(2)}) collective-permute-start(bf16[528,512]{1,0:T(8,128)(2,1)S(1)} %collective-permute-done.5.refs_2_.refs_8_), channel_id=1, source_target_pairs={{0,4},{1,5},{2,6},{3,7},{4,8},{5,9},{6,10},{7,11},{8,12},{9,13},{1... | collective-permute-start | bytes 1622024 | tf_op jit(solution)/shard_map/ppermute | solution.py:59

commit v6 on v5

--- a/solution.py
+++ b/solution.py
@@ -55,8 +55,8 @@
     return lax.ppermute(value, AXES, pairs)
 
 
-def row_on(value):
-    return lax.ppermute(value, AXES, [(r, (r + 4) % 256) for r in range(256)])
+def rows_on(value, rows):
+    return lax.ppermute(value, AXES, [(r, (r + 4 * rows) % 256) for r in range(256)])
 
 
 def ids_down(rows):
@@ -75,11 +75,12 @@
     return block[2 * TOKENS : ROWS, :].astype(jnp.float32)[0:2]
 
 
-def general_head(head, whole, q_ref, o_ref, held, top, total, mix, sem):
-    count = len(whole)
-    for b in range(count):
+def general_head(head, whole, chosen, q_ref, o_ref, held, top, total, mix, sem):
+    count = len(whole) + 1
+    held[count - 2] = chosen[...]
+    for b, place in enumerate([*range(count - 2), count - 1]):
         columns = pl.ds(pl.multiple_of(head * WIDTH, WIDTH), WIDTH)
-        copy = pltpu.make_async_copy(whole[b].at[:, columns], held.at[b], sem)
+        copy = pltpu.make_async_copy(whole[b].at[:, columns], held.at[place], sem)
         copy.start()
         copy.wait()
     mine = ids_down(ids_of(held[count - 1]))
@@ -121,16 +122,23 @@
         o_ref[:, columns] = (mix[...] / total[...]).astype(jnp.bfloat16)
 
 
-def attend(prior, has_own, has_before, last, whole_count, q_ref, own, *refs):
+def attend(prior, has_own, has_before, last, whole_count, *refs):
     refs = list(refs)
     take = lambda n: [refs.pop(0) for _ in range(n)]
+    which = take(1)[0] if last else None
+    q_ref, own = take(2)
     blocks = take(prior)
     before = take(2) if has_before else None
     whole = take(whole_count)
     outs = take(1 if last else 3)
     mixed, picked, causal, rows_in = take(4)
     head = pl.program_id(0)
-    count = prior + has_own
+    if last:
+        chosen = take(1)[0]
+        latter = blocks.pop()
+        chosen[...] = jnp.where(which[0] == 1, latter[...], blocks[-1][...])
+        blocks[-1] = chosen
+        prior -= 1
 
     @pl.when(head == 0)
     def _():
@@ -197,15 +205,16 @@
 
         @pl.when(jnp.min(good) < 0.5)
         def _():
-            general_head(head, whole, q_ref, outs[0], *refs)
+            general_head(head, whole, chosen, q_ref, outs[0], *refs)
     else:
         outs[1][...] = weights
         outs[2][...] = jnp.zeros_like(outs[2])
 
 
-def attention(queries, own, blocks, has_own, before, whole, last):
+def attention(queries, own, blocks, has_own, before, whole, which):
     by_head = lambda rows, columns: pl.BlockSpec((rows, columns), lambda h: (0, h))
-    count = len(blocks) + has_own
+    last = which is not None
+    count = len(blocks) + has_own - last
     wide, narrow = by_head(TOKENS, GROUP * WIDTH), by_head(TOKENS, WIDTH)
     before_specs = [wide, narrow] if before else []
     if last:
@@ -226,7 +235,8 @@
     ]
     if last:
         scratch += [
-            pltpu.VMEM((len(whole), ROWS, WIDTH), jnp.bfloat16),
+            pltpu.VMEM((ROWS, WIDTH), jnp.bfloat16),
+            pltpu.VMEM((len(whole) + 1, ROWS, WIDTH), jnp.bfloat16),
             pltpu.VMEM((TOKENS, WIDTH), jnp.float32),
             pltpu.VMEM((TOKENS, WIDTH), jnp.float32),
             pltpu.VMEM((TOKENS, WIDTH), jnp.float32),
@@ -235,7 +245,8 @@
     return pl.pallas_call(
         functools.partial(attend, len(blocks), has_own, bool(before), last, len(whole)),
         grid=(KEY_VALUE_HEADS,),
-        in_specs=[wide]
+        in_specs=[pl.BlockSpec(memory_space=pltpu.SMEM)] * last
+        + [wide]
         + [by_head(ROWS, WIDTH)] * (1 + len(blocks))
         + before_specs
         + [pl.BlockSpec(memory_space=pl.ANY)] * len(whole),
@@ -248,30 +259,31 @@
             bytes_accessed=4_000_000 + count * 540_000,
             transcendentals=28 * 256 * 256 * count,
         ),
-    )(queries, own, *blocks, *before, *whole)
+    )(*([which.astype(jnp.int32)] if last else []), queries, own, *blocks, *before, *whole)
 
 
 def per_device(queries, key_states, value_vectors, segment_ids):
-    ids = (segment_ids + 1).astype(jnp.bfloat16).reshape(2, WIDTH)
+    ids = segment_ids.astype(jnp.bfloat16).reshape(2, WIDTH)
     ids = jnp.pad(jnp.tile(ids, (1, KEY_VALUE_HEADS)), ((0, EXTRA - 2), (0, 0)))
     own = jnp.concatenate([key_states, value_vectors, ids], axis=0)
     x = lax.axis_index("seq") % 4
     own = lax.optimization_barrier(own)
-    four = row_on(own)
+    four = rows_on(own, 1)
     back = turned_along_y(own, -1)
     across = turned_along_x(own, 2)
     middle = [turned_along_x(four, a) for a in (1, 3)]
     eight = two_rows_on(back)
-    next_across = row_on(across)
-    *stage, done = attention(queries, own, [four], True, [], [], False)
+    next_across = rows_on(across, 1)
+    *stage, done = attention(queries, own, [four], True, [], [], None)
     eight, _ = lax.optimization_barrier((eight, done))
     ends = [turned_along_x(jnp.where(x + a < 4, own, eight), a) for a in (1, 3)]
-    far_across = row_on(next_across)
-    across = jnp.where(x < 2, far_across, across)
+    across, next_across = lax.optimization_barrier((across, next_across))
+    far_across = rows_on(across, 2)
     early = [*middle, next_across, eight]
-    late = [*ends, across]
-    *stage, _ = attention(queries, own, early, False, stage, [], False)
-    return attention(queries, own, late, False, stage, [four, *early, *late, own], True)
+    *stage, _ = attention(queries, own, early, False, stage, [], None)
+    late = [*ends, across, far_across]
+    whole = [four, *early, *ends, own]
+    return attention(queries, own, late, False, stage, whole, jnp.reshape(x < 2, (1,)))
 
 
 def solution(mesh):

time: 212 us -> 213 us (level); the launches traced: 210 us -> 213 us
  starting transfers between devices: 15 us -> 17.5 us
    ppermute x5, waiting for transfers between devices: 0.01 us -> 9.18 us  [turned_along_x(): return lax.ppermute(value, AXES, pairs)]
    ppermute x1, waiting for transfers between devices: 8.2 us -> 0.16 us  [turned_along_y(): return lax.ppermute(value, AXES, pairs)]
where the time goes in v6:
time: 213 us
  Pallas kernels  175 us (82%)
  starting transfers between devices  17.5 us (8%)
  waiting for transfers between devices  16.8 us (8%)
    pallas_call x3, Pallas kernels, attention(): pl.pallas_call(functools.partial(attend, len(blocks), has_own, bool(befor...  175 us
    ppermute x5, waiting for transfers between devices, turned_along_x(): return lax.ppermute(value, AXES, pairs)  9.18 us
    ppermute x5, starting transfers between devices, turned_along_x(): return lax.ppermute(value, AXES, pairs)  8.25 us
    ppermute x3, waiting for transfers between devices, rows_on(): lax.ppermute(value, AXES, [(r, (r + 4 * rows) % 256) for r in range(256)])  7.46 us
    ppermute x1, starting transfers between devices, two_rows_on(): return lax.ppermute(value, AXES, pairs)  5.22 us
  transfers between devices with their start and end apart: 10, of which 4 were waited for; matrix products, arithmetic and copies ran while one was open for 0% of the time, Pallas kernels for 8%

profile of v6, /device:TPU:97, one launch (start us, length us, event | category | flops | bytes accessed | tf_op | source)
XLA Modules:
  0.0 213.0 jit_solution(2215758179391231534)
XLA Ops:
  0.0 0.7 convert_bitcast_fusion
  0.7 1.1 fusion.1.refs_1_.refs_2_.refs_16_
  1.8 2.8 %collective-permute-start.4 = (bf16[528,512]{1,0:T(8,128)(2,1)S(1)}, bf16[528,512]{1,0:T(8,128)(2,1)S(1)}, u32[]{:S(2)}, u32[]{:S(2)}) collective-permute-start(bf16[528,512]{1,0:T(8,128)(2,1)S(1)} %fusion.1.refs_1_.refs_2_.refs_16_), channel_id=1, source_target_pairs={{0,2},{1,3},{2,0},{3,1},{4,6},{5,7},{6,4},{7,5},{8,10},{9,11},{10,... | collective-permute-start | bytes 1622024 | tf_op jit(solution)/shard_map/ppermute | solution.py:35
  4.6 2.7 %collective-permute-start = (bf16[528,512]{1,0:T(8,128)(2,1)S(1)}, bf16[528,512]{1,0:T(8,128)(2,1)S(1)}, u32[]{:S(2)}, u32[]{:S(2)}) collective-permute-start(bf16[528,512]{1,0:T(8,128)(2,1)S(1)} %fusion.1.refs_1_.refs_2_.refs_16_), channel_id=1, source_target_pairs={{0,12},{1,13},{2,14},{3,15},{4,0},{5,1},{6,2},{7,3},{8,4},{9,5},{1... | collective-permute-start | bytes 1622024 | tf_op jit(solution)/shard_map/ppermute | solution.py:45
  7.3 0.0 collective-permute-start.7
  7.3 9.2 %collective-permute-done.4.refs_5_ = bf16[528,512]{1,0:T(8,128)(2,1)S(1)} collective-permute-done((bf16[528,512]{1,0:T(8,128)(2,1)S(1)}, bf16[528,512]{1,0:T(8,128)(2,1)S(1)}, u32[]{:S(2)}, u32[]{:S(2)}) %collective-permute-start.4) | collective-permute-done | bytes 540704 | tf_op jit(solution)/shard_map/ppermute | solution.py:35
  16.5 1.3 collective-permute-start.5
  17.8 0.2 collective-permute-done
  18.0 5.2 %collective-permute-start.1 = (bf16[528,512]{1,0:T(8,128)(2,1)S(1)}, bf16[528,512]{1,0:T(8,128)(2,1)S(1)}, u32[]{:S(2)}, u32[]{:S(2)}) collective-permute-start(bf16[528,512]{1,0:T(8,128)(2,1)S(1)} %collective-permute-done), channel_id=1, source_target_pairs={{12,8},{13,9},{14,10},{15,11},{0,12},{1,13},{2,14},{3,15},{4,16},{... | collective-permute-start | bytes 1622024 | tf_op jit(solution)/shard_map/ppermute | solution.py:55
  23.2 6.0 %collective-permute-done.7.refs_2_.refs_9_ = bf16[528,512]{1,0:T(8,128)(2,1)S(1)} collective-permute-done((bf16[528,512]{1,0:T(8,128)(2,1)S(1)}, bf16[528,512]{1,0:T(8,128)(2,1)S(1)}, u32[]{:S(2)}, u32[]{:S(2)}) %collective-permute-start.7) | collective-permute-done | bytes 540704 | tf_op jit(solution)/shard_map/ppermute | solution.py:59
  29.2 0.0 collective-permute-start.8
  29.2 2.7 %collective-permute-start.9 = (bf16[528,512]{1,0:T(8,128)(2,1)S(1)}, bf16[528,512]{1,0:T(8,128)(2,1)S(1)}, u32[]{:S(2)}, u32[]{:S(2)}) collective-permute-start(bf16[528,512]{1,0:T(8,128)(2,1)S(1)} %collective-permute-done.7.refs_2_.refs_9_), channel_id=1, source_target_pairs={{0,3},{1,0},{2,1},{3,2},{4,7},{5,4},{6,5},{7,6},{8,11},{9,8},{10,9... | collective-permute-start | bytes 1622024 | tf_op jit(solution)/shard_map/ppermute | solution.py:35
  31.9 0.0 copy-start
  31.9 1.5 copy-done
  33.4 6.4 %shard_map.46 = (f32[256,3584]{1,0:T(8,128)S(1)}, f32[256,512]{1,0:T(8,128)S(1)}, f32[8,512]{1,0:T(8,128)}) custom-call(bf16[256,3584]{1,0:T(8,128)(2,1)S(1)} %copy-done, bf16[528,512]{1,0:T(8,128)(2,1)S(1)} %fusion.1.refs_1_.refs_2_.refs_16_, bf16[528,512]{1,0:T(8,128)(2,1)S(1)} %collective-permute-done.7.refs_2_.refs_9_), custom_call_target="tpu_custom_call" | custom-call | flops 3758096384 | bytes 5080000 | tf_op jit(solution)/shard_map/pallas_call | solution.py:245
  39.8 0.0 collective-permute-done.5.refs_4_.refs_12_
  39.8 0.0 collective-permute-done.1.refs_5_.refs_13_
  39.8 0.1 broadcast_select_fusion
  39.9 0.1 collective-permute-start.2
  39.9 2.7 %collective-permute-start.3 = (bf16[528,512]{1,0:T(8,128)(2,1)S(1)}, bf16[528,512]{1,0:T(8,128)(2,1)S(1)}, u32[]{:S(2)}, u32[]{:S(2)}) collective-permute-start(bf16[528,512]{1,0:T(8,128)(2,1)S(1)} %get-tuple-element.17), channel_id=1, source_target_pairs={{0,3},{1,0},{2,1},{3,2},{4,7},{5,4},{6,5},{7,6},{8,11},{9,8},{10,9... | collective-permute-start | bytes 1622024 | tf_op jit(solution)/shard_map/ppermute | solution.py:35
  42.6 0.0 collective-permute-start.6
  42.6 0.0 collective-permute-done.8.refs_2_.refs_10_
  42.6 0.0 collective-permute-done.9.refs_3_.refs_11_
  42.6 11.3 %shard_map.47 = (f32[256,3584]{1,0:T(8,128)S(1)}, f32[256,512]{1,0:T(8,128)S(1)}, f32[8,512]{1,0:T(8,128)}) custom-call(bf16[256,3584]{1,0:T(8,128)(2,1)S(1)} %copy-done, bf16[528,512]{1,0:T(8,128)(2,1)S(1)} %fusion.1.refs_1_.refs_2_.refs_16_, bf16[528,512]{1,0:T(8,128)(2,1)S(1)} %collective-permute-done.8.refs_2_.refs_10_, ...), custom_call_target="tpu_custom_call" | custom-call | flops 7516192768 | bytes 6160000 | tf_op jit(solution)/shard_map/pallas_call | solution.py:245
  53.9 0.0 collective-permute-done.2.refs_3_.refs_14_
  53.9 0.0 collective-permute-done.3.refs_4_.refs_15_
  53.9 1.4 collective-permute-done.6.refs_6_
  55.4 157.4 %shard_map.48 = bf16[256,3584]{1,0:T(8,128)(2,1)} custom-call(s32[1]{0:T(128)} %bitcast.refs_0_, bf16[256,3584]{1,0:T(8,128)(2,1)S(1)} %copy-done, bf16[528,512]{1,0:T(8,128)(2,1)S(1)} %fusion.1.refs_1_.refs_2_.refs_16_, bf16[528,512]{1,0:T(8,128)(2,1)S(1)} %collective-permute-done.2.refs_3_.refs_14_, ...), custom_call_target="tpu_custom_call" | custom-call | flops 5637144576 | bytes 5620000 | tf_op jit(solution)/shard_map/pallas_call | solution.py:245
  (2 shorter events, 0.0 us)
Async XLA Ops:
  1.8 14.7 %collective-permute-start.4 = (bf16[528,512]{1,0:T(8,128)(2,1)S(1)}, bf16[528,512]{1,0:T(8,128)(2,1)S(1)}, u32[]{:S(2)}, u32[]{:S(2)}) collective-permute-start(bf16[528,512]{1,0:T(8,128)(2,1)S(1)} %fusion.1.refs_1_.refs_2_.refs_16_), channel_id=1, source_target_pairs={{0,2},{1,3},{2,0},{3,1},{4,6},{5,7},{6,4},{7,5},{8,10},{9,11},{10,... | collective-permute-start | bytes 1622024 | tf_op jit(solution)/shard_map/ppermute | solution.py:35
  4.6 13.4 %collective-permute-start = (bf16[528,512]{1,0:T(8,128)(2,1)S(1)}, bf16[528,512]{1,0:T(8,128)(2,1)S(1)}, u32[]{:S(2)}, u32[]{:S(2)}) collective-permute-start(bf16[528,512]{1,0:T(8,128)(2,1)S(1)} %fusion.1.refs_1_.refs_2_.refs_16_), channel_id=1, source_target_pairs={{0,12},{1,13},{2,14},{3,15},{4,0},{5,1},{6,2},{7,3},{8,4},{9,5},{1... | collective-permute-start | bytes 1622024 | tf_op jit(solution)/shard_map/ppermute | solution.py:45
  7.3 21.9 %collective-permute-start.7 = (bf16[528,512]{1,0:T(8,128)(2,1)S(1)}, bf16[528,512]{1,0:T(8,128)(2,1)S(1)}, u32[]{:S(2)}, u32[]{:S(2)}) collective-permute-start(bf16[528,512]{1,0:T(8,128)(2,1)S(1)} %fusion.1.refs_1_.refs_2_.refs_16_), channel_id=1, source_target_pairs={{0,4},{1,5},{2,6},{3,7},{4,8},{5,9},{6,10},{7,11},{8,12},{9,13},{1... | collective-permute-start | bytes 1622024 | tf_op jit(solution)/shard_map/ppermute | solution.py:59
  16.5 23.3 %collective-permute-start.5 = (bf16[528,512]{1,0:T(8,128)(2,1)S(1)}, bf16[528,512]{1,0:T(8,128)(2,1)S(1)}, u32[]{:S(2)}, u32[]{:S(2)}) collective-permute-start(bf16[528,512]{1,0:T(8,128)(2,1)S(1)} %collective-permute-done.4.refs_5_), channel_id=1, source_target_pairs={{0,4},{1,5},{2,6},{3,7},{4,8},{5,9},{6,10},{7,11},{8,12},{9,13},{1... | collective-permute-start | bytes 1622024 | tf_op jit(solution)/shard_map/ppermute | solution.py:59
  18.0 21.8 %collective-permute-start.1 = (bf16[528,512]{1,0:T(8,128)(2,1)S(1)}, bf16[528,512]{1,0:T(8,128)(2,1)S(1)}, u32[]{:S(2)}, u32[]{:S(2)}) collective-permute-start(bf16[528,512]{1,0:T(8,128)(2,1)S(1)} %collective-permute-done), channel_id=1, source_target_pairs={{12,8},{13,9},{14,10},{15,11},{0,12},{1,13},{2,14},{3,15},{4,16},{... | collective-permute-start | bytes 1622024 | tf_op jit(solution)/shard_map/ppermute | solution.py:55
  29.2 13.4 %collective-permute-start.8 = (bf16[528,512]{1,0:T(8,128)(2,1)S(1)}, bf16[528,512]{1,0:T(8,128)(2,1)S(1)}, u32[]{:S(2)}, u32[]{:S(2)}) collective-permute-start(bf16[528,512]{1,0:T(8,128)(2,1)S(1)} %collective-permute-done.7.refs_2_.refs_9_), channel_id=1, source_target_pairs={{0,1},{1,2},{2,3},{3,0},{4,5},{5,6},{6,7},{7,4},{8,9},{9,10},{10,1... | collective-permute-start | bytes 1622024 | tf_op jit(solution)/shard_map/ppermute | solution.py:35
  29.2 13.4 %collective-permute-start.9 = (bf16[528,512]{1,0:T(8,128)(2,1)S(1)}, bf16[528,512]{1,0:T(8,128)(2,1)S(1)}, u32[]{:S(2)}, u32[]{:S(2)}) collective-permute-start(bf16[528,512]{1,0:T(8,128)(2,1)S(1)} %collective-permute-done.7.refs_2_.refs_9_), channel_id=1, source_target_pairs={{0,3},{1,0},{2,1},{3,2},{4,7},{5,4},{6,5},{7,6},{8,11},{9,8},{10,9... | collective-permute-start | bytes 1622024 | tf_op jit(solution)/shard_map/ppermute | solution.py:35
  31.9 1.5 copy-start
  39.9 14.1 %collective-permute-start.2 = (bf16[528,512]{1,0:T(8,128)(2,1)S(1)}, bf16[528,512]{1,0:T(8,128)(2,1)S(1)}, u32[]{:S(2)}, u32[]{:S(2)}) collective-permute-start(bf16[528,512]{1,0:T(8,128)(2,1)S(1)} %get-tuple-element.18), channel_id=1, source_target_pairs={{0,1},{1,2},{2,3},{3,0},{4,5},{5,6},{6,7},{7,4},{8,9},{9,10},{10,1... | collective-permute-start | bytes 1622024 | tf_op jit(solution)/shard_map/ppermute | solution.py:35
  39.9 14.0 %collective-permute-start.3 = (bf16[528,512]{1,0:T(8,128)(2,1)S(1)}, bf16[528,512]{1,0:T(8,128)(2,1)S(1)}, u32[]{:S(2)}, u32[]{:S(2)}) collective-permute-start(bf16[528,512]{1,0:T(8,128)(2,1)S(1)} %get-tuple-element.17), channel_id=1, source_target_pairs={{0,3},{1,0},{2,1},{3,2},{4,7},{5,4},{6,5},{7,6},{8,11},{9,8},{10,9... | collective-permute-start | bytes 1622024 | tf_op jit(solution)/shard_map/ppermute | solution.py:35
  42.6 12.7 %collective-permute-start.6 = (bf16[528,512]{1,0:T(8,128)(2,1)S(1)}, bf16[528,512]{1,0:T(8,128)(2,1)S(1)}, u32[]{:S(2)}, u32[]{:S(2)}) collective-permute-start(bf16[528,512]{1,0:T(8,128)(2,1)S(1)} %collective-permute-done.4.refs_5_), channel_id=1, source_target_pairs={{0,8},{1,9},{2,10},{3,11},{4,12},{5,13},{6,14},{7,15},{8,16},{9,17... | collective-permute-start | bytes 1622024 | tf_op jit(solution)/shard_map/ppermute | solution.py:59

commit v7 on v6

v7 whole, which is shorter than its diff:
```python
import functools

import jax
import jax.numpy as jnp
from jax import lax
from jax.experimental import pallas as pl
from jax.experimental.pallas import tpu as pltpu
from jax.sharding import PartitionSpec as P

KEY_VALUE_HEADS = 4
GROUP = 7
WIDTH = 128
TOKENS = 256
EXTRA = 16
ROWS = 2 * TOKENS + EXTRA
AXES = ("dp", "seq")
SCALE = 1.4426950408889634 / WIDTH**0.5
LOW, HIGH = 1e-25, 1e30
VMEM_LIMIT = 16 * 1024 * 1024
NT = (((1,), (1,)), ((), ()))
NN = (((1,), (0,)), ((), ()))


def rank_of(plane, y, x):
    return (plane * 4 + y) * 4 + x


def turned_along_x(value, steps):
    pairs = [
        (rank_of(plane, y, x), rank_of(plane, y, (x + steps) % 4))
        for plane in range(16)
        for y in range(4)
        for x in range(4)
    ]
    return lax.ppermute(value, AXES, pairs)


def turned_along_y(value, steps):
    pairs = [
        (rank_of(plane, y, x), rank_of(plane, (y + steps) % 4, x))
        for plane in range(16)
        for y in range(4)
        for x in range(4)
    ]
    return lax.ppermute(value, AXES, pairs)


def two_rows_on(value):
    pairs = [
        (rank_of(plane, (y - 1) % 4, x), (rank_of(plane, y, x) + 8) % 256)
        for plane in range(16)
        for y in range(4)
        for x in range(4)
    ]
    return lax.ppermute(value, AXES, pairs)


def rows_on(value, rows):
    return lax.ppermute(value, AXES, [(r, (r + 4 * rows) % 256) for r in range(256)])


def ids_down(rows):
    halves = [
        jnp.transpose(jnp.broadcast_to(rows[i : i + 1], (WIDTH, WIDTH))) for i in range(2)
    ]
    return jnp.concatenate(halves, axis=0)


def ids_across(rows, count):
    halves = [jnp.broadcast_to(rows[i : i + 1], (count, WIDTH)) for i in range(2)]
    return jnp.concatenate(halves, axis=1)


def ids_of(block):
    return block[2 * TOKENS : ROWS, :].astype(jnp.float32)[0:2]


def general(whole, chosen, q_ref, o_ref, out, held, top, total, mix, sem):
    count = len(whole) + 1

    @pl.loop(0, KEY_VALUE_HEADS)
    def _(head):
        keys = pl.ds(pl.multiple_of(head * WIDTH, WIDTH), WIDTH)
        held[count - 2] = chosen[:, keys]
        for b, place in enumerate([*range(count - 2), count - 1]):
            held[place] = whole[b][:, keys]
        mine = ids_down(ids_of(held[count - 1]))
        mine = jnp.concatenate([mine, mine], axis=1)
        later = lax.broadcasted_iota(jnp.int32, (TOKENS, TOKENS), 1) > lax.broadcasted_iota(
            jnp.int32, (TOKENS, TOKENS), 0
        )

        @pl.loop(0, GROUP)
        def _(g):
            columns = pl.ds(pl.multiple_of((head * GROUP + g) * WIDTH, WIDTH), WIDTH)
            top[...] = jnp.full((TOKENS, WIDTH), -1e30, jnp.float32)
            total[...] = jnp.zeros((TOKENS, WIDTH), jnp.float32)
            mix[...] = jnp.zeros((TOKENS, WIDTH), jnp.float32)

            @pl.loop(0, count)
            def _(b):
                s = lax.dot_general(
                    q_ref[:, columns],
                    held[b, 0:TOKENS, :],
                    NT,
                    preferred_element_type=jnp.float32,
                )
                s = s * SCALE
                theirs = held[b, 2 * TOKENS : ROWS, :].astype(jnp.float32)[0:2]
                allowed = (mine == ids_across(theirs, TOKENS)) & ~(later & (b == count - 1))
                s = jnp.where(allowed, s, -1e30)
                now = jnp.maximum(top[:, 0:1], jnp.max(s, axis=1, keepdims=True))
                p = jnp.where(allowed, jnp.exp2(s - now), 0.0)
                keep = jnp.exp2(top[:, 0:1] - now)
                total[...] = total[...] * keep + jnp.sum(p, axis=1, keepdims=True)
                mix[...] = mix[...] * keep + lax.dot_general(
                    p.astype(jnp.bfloat16),
                    held[b, TOKENS : 2 * TOKENS, :],
                    NN,
                    preferred_element_type=jnp.float32,
                )
                top[...] = jnp.broadcast_to(now, (TOKENS, WIDTH))

            out[:, columns] = (mix[...] / total[...]).astype(jnp.bfloat16)

    copy = pltpu.make_async_copy(out, o_ref, sem)
    copy.start()
    copy.wait()


def attend(prior, has_own, has_before, last, whole_count, *refs):
    refs = list(refs)
    take = lambda n: [refs.pop(0) for _ in range(n)]
    which = take(1)[0] if last else None
    q_ref, own = take(2)
    blocks = take(prior)
    before = take(2) if has_before else None
    whole = take(whole_count)
    outs = take(1 if last else 3)
    mixed, picked, causal, rows_in = take(4)
    if last:
        chosen, out, sems = take(3)
        latter = blocks.pop()
        chosen[...] = jnp.where(which[0] == 1, latter[...], blocks[-1][...])
        blocks[-1] = chosen
        prior -= 1

    ids = ids_of(own[:, 0:WIDTH])
    down = ids_down(ids)
    first = ids[0:1, 0:1]
    rows_in[...] = jnp.where(down == first, 1.0, 0.0)
    if has_own:
        down = jnp.concatenate([down, down], axis=1)
        row = lax.broadcasted_iota(jnp.int32, (TOKENS, TOKENS), 0)
        column = lax.broadcasted_iota(jnp.int32, (TOKENS, TOKENS), 1)
        same = down == ids_across(ids, TOKENS)
        causal[...] = jnp.where(same & (column <= row), 1.0, 0.0)
    for b in range(prior):
        theirs = ids_of(blocks[b][:, 0:WIDTH])
        picked[b] = ids_down(jnp.where(theirs == first, 1.0, 0.0)).astype(jnp.bfloat16)

    def term(q, keys, b, mask=None):
        s = lax.dot_general(q, keys, NT, preferred_element_type=jnp.float32)
        p = jnp.exp2(s * SCALE)
        if mask is not None:
            p = p * mask
        return lax.dot_general(
            p.astype(jnp.bfloat16), mixed[b], NN, preferred_element_type=jnp.float32
        )

    good = None
    copies = []
    lane = lax.broadcasted_iota(jnp.int32, (TOKENS, WIDTH), 1)
    for head in range(KEY_VALUE_HEADS):
        keys = slice(head * WIDTH, (head + 1) * WIDTH)
        for b in range(prior):
            mixed[b, :, 0:WIDTH] = blocks[b][TOKENS : 2 * TOKENS, keys] * picked[b]
            mixed[b, :, WIDTH:] = picked[b]
        if has_own:
            mixed[prior, :, 0:WIDTH] = own[TOKENS : 2 * TOKENS, keys]
            mixed[prior, :, WIDTH:] = jnp.ones((TOKENS, WIDTH), jnp.bfloat16)
        weights = None
        for g in range(GROUP):
            columns = slice((head * GROUP + g) * WIDTH, (head * GROUP + g + 1) * WIDTH)
            q = q_ref[:, columns]
            mix, weight = 0.0, 0.0
            if prior:
                sums = term(q, blocks[0][0:TOKENS, keys], 0)
                for b in range(1, prior):
                    sums = sums + term(q, blocks[b][0:TOKENS, keys], b)
                inside = rows_in[...] > 0.5
                mix = jnp.where(inside, sums[:, :WIDTH], 0.0)
                weight = jnp.where(inside, sums[:, WIDTH:], 0.0)
            if has_own:
                sums = term(q, own[0:TOKENS, keys], prior, causal[...])
                mix = mix + sums[:, :WIDTH]
                weight = weight + sums[:, WIDTH:]
            if has_before:
                mix = mix + before[0][:, columns]
                weight = weight + before[1][:, head * WIDTH + g : head * WIDTH + g + 1]
            if last:
                out[:, columns] = (mix / weight).astype(jnp.bfloat16)
                fine = jnp.where((weight > LOW) & (weight < HIGH), 1.0, 0.0)
                good = fine if good is None else jnp.minimum(good, fine)
            else:
                outs[0][:, columns] = mix
                weights = weight if weights is None else jnp.where(lane == g, weight, weights)
        if last:
            columns = slice(head * GROUP * WIDTH, (head + 1) * GROUP * WIDTH)
            copy = pltpu.make_async_copy(
                out.at[:, columns], outs[0].at[:, columns], sems.at[head]
            )
            copy.start()
            copies.append(copy)
        else:
            outs[1][:, keys] = weights
    if last:
        for copy in copies:
            copy.wait()

        @pl.when(jnp.min(good) < 0.5)
        def _():
            general(whole, chosen, q_ref, outs[0], out, *refs, sems.at[0])
    else:
        outs[2][...] = jnp.zeros_like(outs[2])


def attention(queries, own, blocks, has_own, before, whole, which):
    last = which is not None
    count = len(blocks) + has_own - last
    inside = pl.BlockSpec(memory_space=pltpu.VMEM)
    if last:
        out_specs = pl.BlockSpec(memory_space=pl.ANY)
        out_shape = jax.ShapeDtypeStruct(queries.shape, jnp.bfloat16)
    else:
        out_specs = [inside] * 3
        out_shape = [
            jax.ShapeDtypeStruct(queries.shape, jnp.float32),
            jax.ShapeDtypeStruct((TOKENS, KEY_VALUE_HEADS * WIDTH), jnp.float32),
            jax.ShapeDtypeStruct((8, WIDTH), jnp.float32),
        ]
    scratch = [
        pltpu.VMEM((count, TOKENS, 2 * WIDTH), jnp.bfloat16),
        pltpu.VMEM((max(len(blocks), 1), TOKENS, WIDTH), jnp.bfloat16),
        pltpu.VMEM((TOKENS, TOKENS), jnp.float32),
        pltpu.VMEM((TOKENS, WIDTH), jnp.float32),
    ]
    if last:
        scratch += [
            pltpu.VMEM((ROWS, KEY_VALUE_HEADS * WIDTH), jnp.bfloat16),
            pltpu.VMEM(queries.shape, jnp.bfloat16),
            pltpu.SemaphoreType.DMA((KEY_VALUE_HEADS,)),
            pltpu.VMEM((len(whole) + 1, ROWS, WIDTH), jnp.bfloat16),
            pltpu.VMEM((TOKENS, WIDTH), jnp.float32),
            pltpu.VMEM((TOKENS, WIDTH), jnp.float32),
            pltpu.VMEM((TOKENS, WIDTH), jnp.float32),
        ]
    return pl.pallas_call(
        functools.partial(attend, len(blocks), has_own, bool(before), last, len(whole)),
        in_specs=[pl.BlockSpec(memory_space=pltpu.SMEM)] * last
        + [inside] * (2 + len(blocks) + len(before) + len(whole)),
        out_specs=out_specs,
        out_shape=out_shape,
        scratch_shapes=scratch,
        compiler_params=pltpu.CompilerParams(vmem_limit_bytes=VMEM_LIMIT),
        cost_estimate=pl.CostEstimate(
            flops=28 * 256 * 256 * count * 1024,
            bytes_accessed=4_000_000 + count * 540_000,
            transcendentals=28 * 256 * 256 * count,
        ),
    )(*([which.astype(jnp.int32)] if last else []), queries, own, *blocks, *before, *whole)


def per_device(queries, key_states, value_vectors, segment_ids):
    ids = segment_ids.astype(jnp.bfloat16).reshape(2, WIDTH)
    ids = jnp.pad(jnp.tile(ids, (1, KEY_VALUE_HEADS)), ((0, EXTRA - 2), (0, 0)))
    own = jnp.concatenate([key_states, value_vectors, ids], axis=0)
    x = lax.axis_index("seq") % 4
    own = lax.optimization_barrier(own)
    four = rows_on(own, 1)
    back = turned_along_y(own, -1)
    across = turned_along_x(own, 2)
    middle = [turned_along_x(four, a) for a in (1, 3)]
    eight = two_rows_on(back)
    next_across = rows_on(across, 1)
    *stage, done = attention(queries, own, [four], True, [], [], None)
    eight, across, _ = lax.optimization_barrier((eight, across, done))
    far_across = rows_on(across, 2)
    ends = [turned_along_x(jnp.where(x + a < 4, own, eight), a) for a in (1, 3)]
    early = [*middle, next_across, eight]
    *stage, _ = attention(queries, own, early, False, stage, [], None)
    late = [*ends, across, far_across]
    whole = [four, *early, *ends, own]
    return attention(queries, own, late, False, stage, whole, jnp.reshape(x < 2, (1,)))


def solution(mesh):
    rows = P(AXES, None)
    return jax.shard_map(
        per_device,
        mesh=mesh,
        in_specs=(rows, rows, rows, P(AXES)),
        out_specs=rows,
        check_vma=False,
    )
```

time: 213 us -> 209 us (0.981)
  Pallas kernels: 175 us -> 170 us
  starting transfers between devices: 17.5 us -> 15.2 us
  waiting for transfers between devices: 16.8 us -> 19.1 us
    ppermute x1, waiting for transfers between devices: 0.16 us -> 8.2 us  [turned_along_y(): return lax.ppermute(value, AXES, pairs)]
    ppermute x5, waiting for transfers between devices: 9.18 us -> 1.4 us  [turned_along_x(): return lax.ppermute(value, AXES, pairs)]
    pallas_call x3, Pallas kernels: 175 us -> 170 us  [attention(): pl.pallas_call(functools.partial(attend, len(blocks), has_own, bool(befor...]
  transfers between devices with their start and end apart: 10 -> 10, of which waited for: 4 -> 6; matrix products, arithmetic and copies ran while one was open for 0% -> 0% of each run, Pallas kernels for 8% -> 6%
where the time goes in v7:
time: 209 us; the launch traced here: 208 us
  Pallas kernels  170 us (81%)
  waiting for transfers between devices  19.1 us (9%)
  starting transfers between devices  15.2 us (7%)
    pallas_call x3, Pallas kernels, attention(): pl.pallas_call(functools.partial(attend, len(blocks), has_own, bool(befor...  170 us
    ppermute x3, waiting for transfers between devices, rows_on(): lax.ppermute(value, AXES, [(r, (r + 4 * rows) % 256) for r in range(256)])  8.27 us
    ppermute x1, waiting for transfers between devices, turned_along_y(): return lax.ppermute(value, AXES, pairs)  8.2 us
    ppermute x5, starting transfers between devices, turned_along_x(): return lax.ppermute(value, AXES, pairs)  8.17 us
  transfers between devices with their start and end apart: 10, of which 6 were waited for; matrix products, arithmetic and copies ran while one was open for 0% of the time, Pallas kernels for 6%

profile of v7, /device:TPU:97, one launch (start us, length us, event | category | flops | bytes accessed | tf_op | source)
XLA Modules:
  0.0 208.1 jit_solution(12390338220204820757)
XLA Ops:
  0.0 0.7 convert_bitcast_fusion
  0.7 1.1 fusion.1.refs_1_.refs_2_.refs_16_
  1.8 2.8 %collective-permute-start = (bf16[528,512]{1,0:T(8,128)(2,1)S(1)}, bf16[528,512]{1,0:T(8,128)(2,1)S(1)}, u32[]{:S(2)}, u32[]{:S(2)}) collective-permute-start(bf16[528,512]{1,0:T(8,128)(2,1)S(1)} %fusion.1.refs_1_.refs_2_.refs_16_), channel_id=1, source_target_pairs={{0,12},{1,13},{2,14},{3,15},{4,0},{5,1},{6,2},{7,3},{8,4},{9,5},{1... | collective-permute-start | bytes 1622024 | tf_op jit(solution)/shard_map/ppermute | solution.py:45
  4.6 0.0 collective-permute-start.6
  4.6 2.7 %collective-permute-start.2 = (bf16[528,512]{1,0:T(8,128)(2,1)S(1)}, bf16[528,512]{1,0:T(8,128)(2,1)S(1)}, u32[]{:S(2)}, u32[]{:S(2)}) collective-permute-start(bf16[528,512]{1,0:T(8,128)(2,1)S(1)} %fusion.1.refs_1_.refs_2_.refs_16_), channel_id=1, source_target_pairs={{0,2},{1,3},{2,0},{3,1},{4,6},{5,7},{6,4},{7,5},{8,10},{9,11},{10,... | collective-permute-start | bytes 1622024 | tf_op jit(solution)/shard_map/ppermute | solution.py:35
  7.3 8.2 %collective-permute-done = bf16[528,512]{1,0:T(8,128)(2,1)S(1)} collective-permute-done((bf16[528,512]{1,0:T(8,128)(2,1)S(1)}, bf16[528,512]{1,0:T(8,128)(2,1)S(1)}, u32[]{:S(2)}, u32[]{:S(2)}) %collective-permute-start) | collective-permute-done | bytes 540704 | tf_op jit(solution)/shard_map/ppermute | solution.py:45
  15.5 3.4 %collective-permute-start.1 = (bf16[528,512]{1,0:T(8,128)(2,1)S(1)}, bf16[528,512]{1,0:T(8,128)(2,1)S(1)}, u32[]{:S(2)}, u32[]{:S(2)}) collective-permute-start(bf16[528,512]{1,0:T(8,128)(2,1)S(1)} %collective-permute-done), channel_id=1, source_target_pairs={{12,8},{13,9},{14,10},{15,11},{0,12},{1,13},{2,14},{3,15},{4,16},{... | collective-permute-start | bytes 1622024 | tf_op jit(solution)/shard_map/ppermute | solution.py:55
  18.9 1.4 collective-permute-done.6.refs_2_.refs_9_
  20.4 1.2 collective-permute-start.7
  21.6 1.5 collective-permute-start.8
  23.1 0.0 collective-permute-done.2.refs_5_
  23.1 0.6 collective-permute-start.9
  23.7 0.0 copy-start
  23.7 1.5 copy-done
  25.2 4.5 %shard_map.46 = (f32[256,3584]{1,0:T(8,128)S(1)}, f32[256,512]{1,0:T(8,128)S(1)}, f32[8,128]{1,0:T(8,128)}) custom-call(bf16[256,3584]{1,0:T(8,128)(2,1)S(1)} %copy-done, bf16[528,512]{1,0:T(8,128)(2,1)S(1)} %fusion.1.refs_1_.refs_2_.refs_16_, bf16[528,512]{1,0:T(8,128)(2,1)S(1)} %collective-permute-done.6.refs_2_.refs_9_), custom_call_target="tpu_custom_call" | custom-call | flops 3758096384 | bytes 5080000 | tf_op jit(solution)/shard_map/pallas_call | solution.py:258
  29.7 1.2 collective-permute-done.1.refs_5_.refs_13_
  30.8 0.1 broadcast_select_fusion
  30.9 1.3 collective-permute-start.3
  32.2 1.5 collective-permute-start.4
  33.7 1.4 collective-permute-done.7.refs_2_.refs_10_
  35.1 0.2 collective-permute-start.5
  35.3 0.0 collective-permute-done.8.refs_3_.refs_11_
  35.3 3.8 %collective-permute-done.9.refs_4_.refs_12_ = bf16[528,512]{1,0:T(8,128)(2,1)S(1)} collective-permute-done((bf16[528,512]{1,0:T(8,128)(2,1)S(1)}, bf16[528,512]{1,0:T(8,128)(2,1)S(1)}, u32[]{:S(2)}, u32[]{:S(2)}) %collective-permute-start.9) | collective-permute-done | bytes 540704 | tf_op jit(solution)/shard_map/ppermute | solution.py:59
  39.1 9.0 %shard_map.47 = (f32[256,3584]{1,0:T(8,128)S(1)}, f32[256,512]{1,0:T(8,128)S(1)}, f32[8,128]{1,0:T(8,128)}) custom-call(bf16[256,3584]{1,0:T(8,128)(2,1)S(1)} %copy-done, bf16[528,512]{1,0:T(8,128)(2,1)S(1)} %fusion.1.refs_1_.refs_2_.refs_16_, bf16[528,512]{1,0:T(8,128)(2,1)S(1)} %collective-permute-done.7.refs_2_.refs_10_, ...), custom_call_target="tpu_custom_call" | custom-call | flops 7516192768 | bytes 6160000 | tf_op jit(solution)/shard_map/pallas_call | solution.py:258
  48.1 0.0 collective-permute-done.3.refs_3_.refs_14_
  48.2 0.0 collective-permute-done.4.refs_4_.refs_15_
  48.2 3.0 %collective-permute-done.5.refs_6_ = bf16[528,512]{1,0:T(8,128)(2,1)S(1)} collective-permute-done((bf16[528,512]{1,0:T(8,128)(2,1)S(1)}, bf16[528,512]{1,0:T(8,128)(2,1)S(1)}, u32[]{:S(2)}, u32[]{:S(2)}) %collective-permute-start.5) | collective-permute-done | bytes 540704 | tf_op jit(solution)/shard_map/ppermute | solution.py:59
  51.1 156.7 %shard_map.48 = bf16[256,3584]{1,0:T(8,128)(2,1)} custom-call(s32[1]{0:T(128)} %bitcast.refs_0_, bf16[256,3584]{1,0:T(8,128)(2,1)S(1)} %copy-done, bf16[528,512]{1,0:T(8,128)(2,1)S(1)} %fusion.1.refs_1_.refs_2_.refs_16_, bf16[528,512]{1,0:T(8,128)(2,1)S(1)} %collective-permute-done.3.refs_3_.refs_14_, ...), custom_call_target="tpu_custom_call" | custom-call | flops 5637144576 | bytes 5620000 | tf_op jit(solution)/shard_map/pallas_call | solution.py:258
  (2 shorter events, 0.0 us)
Async XLA Ops:
  1.8 13.8 %collective-permute-start = (bf16[528,512]{1,0:T(8,128)(2,1)S(1)}, bf16[528,512]{1,0:T(8,128)(2,1)S(1)}, u32[]{:S(2)}, u32[]{:S(2)}) collective-permute-start(bf16[528,512]{1,0:T(8,128)(2,1)S(1)} %fusion.1.refs_1_.refs_2_.refs_16_), channel_id=1, source_target_pairs={{0,12},{1,13},{2,14},{3,15},{4,0},{5,1},{6,2},{7,3},{8,4},{9,5},{1... | collective-permute-start | bytes 1622024 | tf_op jit(solution)/shard_map/ppermute | solution.py:45
  4.6 15.8 %collective-permute-start.6 = (bf16[528,512]{1,0:T(8,128)(2,1)S(1)}, bf16[528,512]{1,0:T(8,128)(2,1)S(1)}, u32[]{:S(2)}, u32[]{:S(2)}) collective-permute-start(bf16[528,512]{1,0:T(8,128)(2,1)S(1)} %fusion.1.refs_1_.refs_2_.refs_16_), channel_id=1, source_target_pairs={{0,4},{1,5},{2,6},{3,7},{4,8},{5,9},{6,10},{7,11},{8,12},{9,13},{1... | collective-permute-start | bytes 1622024 | tf_op jit(solution)/shard_map/ppermute | solution.py:59
  4.6 18.5 %collective-permute-start.2 = (bf16[528,512]{1,0:T(8,128)(2,1)S(1)}, bf16[528,512]{1,0:T(8,128)(2,1)S(1)}, u32[]{:S(2)}, u32[]{:S(2)}) collective-permute-start(bf16[528,512]{1,0:T(8,128)(2,1)S(1)} %fusion.1.refs_1_.refs_2_.refs_16_), channel_id=1, source_target_pairs={{0,2},{1,3},{2,0},{3,1},{4,6},{5,7},{6,4},{7,5},{8,10},{9,11},{10,... | collective-permute-start | bytes 1622024 | tf_op jit(solution)/shard_map/ppermute | solution.py:35
  15.5 15.3 %collective-permute-start.1 = (bf16[528,512]{1,0:T(8,128)(2,1)S(1)}, bf16[528,512]{1,0:T(8,128)(2,1)S(1)}, u32[]{:S(2)}, u32[]{:S(2)}) collective-permute-start(bf16[528,512]{1,0:T(8,128)(2,1)S(1)} %collective-permute-done), channel_id=1, source_target_pairs={{12,8},{13,9},{14,10},{15,11},{0,12},{1,13},{2,14},{3,15},{4,16},{... | collective-permute-start | bytes 1622024 | tf_op jit(solution)/shard_map/ppermute | solution.py:55
  20.4 14.7 %collective-permute-start.7 = (bf16[528,512]{1,0:T(8,128)(2,1)S(1)}, bf16[528,512]{1,0:T(8,128)(2,1)S(1)}, u32[]{:S(2)}, u32[]{:S(2)}) collective-permute-start(bf16[528,512]{1,0:T(8,128)(2,1)S(1)} %collective-permute-done.6.refs_2_.refs_9_), channel_id=1, source_target_pairs={{0,1},{1,2},{2,3},{3,0},{4,5},{5,6},{6,7},{7,4},{8,9},{9,10},{10,1... | collective-permute-start | bytes 1622024 | tf_op jit(solution)/shard_map/ppermute | solution.py:35
  21.6 13.7 %collective-permute-start.8 = (bf16[528,512]{1,0:T(8,128)(2,1)S(1)}, bf16[528,512]{1,0:T(8,128)(2,1)S(1)}, u32[]{:S(2)}, u32[]{:S(2)}) collective-permute-start(bf16[528,512]{1,0:T(8,128)(2,1)S(1)} %collective-permute-done.6.refs_2_.refs_9_), channel_id=1, source_target_pairs={{0,3},{1,0},{2,1},{3,2},{4,7},{5,4},{6,5},{7,6},{8,11},{9,8},{10,9... | collective-permute-start | bytes 1622024 | tf_op jit(solution)/shard_map/ppermute | solution.py:35
  23.1 16.1 %collective-permute-start.9 = (bf16[528,512]{1,0:T(8,128)(2,1)S(1)}, bf16[528,512]{1,0:T(8,128)(2,1)S(1)}, u32[]{:S(2)}, u32[]{:S(2)}) collective-permute-start(bf16[528,512]{1,0:T(8,128)(2,1)S(1)} %collective-permute-done.2.refs_5_), channel_id=1, source_target_pairs={{0,4},{1,5},{2,6},{3,7},{4,8},{5,9},{6,10},{7,11},{8,12},{9,13},{1... | collective-permute-start | bytes 1622024 | tf_op jit(solution)/shard_map/ppermute | solution.py:59
  23.7 1.5 copy-start
  30.9 17.2 %collective-permute-start.3 = (bf16[528,512]{1,0:T(8,128)(2,1)S(1)}, bf16[528,512]{1,0:T(8,128)(2,1)S(1)}, u32[]{:S(2)}, u32[]{:S(2)}) collective-permute-start(bf16[528,512]{1,0:T(8,128)(2,1)S(1)} %get-tuple-element.18), channel_id=1, source_target_pairs={{0,1},{1,2},{2,3},{3,0},{4,5},{5,6},{6,7},{7,4},{8,9},{9,10},{10,1... | collective-permute-start | bytes 1622024 | tf_op jit(solution)/shard_map/ppermute | solution.py:35
  32.2 15.9 %collective-permute-start.4 = (bf16[528,512]{1,0:T(8,128)(2,1)S(1)}, bf16[528,512]{1,0:T(8,128)(2,1)S(1)}, u32[]{:S(2)}, u32[]{:S(2)}) collective-permute-start(bf16[528,512]{1,0:T(8,128)(2,1)S(1)} %get-tuple-element.17), channel_id=1, source_target_pairs={{0,3},{1,0},{2,1},{3,2},{4,7},{5,4},{6,5},{7,6},{8,11},{9,8},{10,9... | collective-permute-start | bytes 1622024 | tf_op jit(solution)/shard_map/ppermute | solution.py:35
  35.1 16.1 %collective-permute-start.5 = (bf16[528,512]{1,0:T(8,128)(2,1)S(1)}, bf16[528,512]{1,0:T(8,128)(2,1)S(1)}, u32[]{:S(2)}, u32[]{:S(2)}) collective-permute-start(bf16[528,512]{1,0:T(8,128)(2,1)S(1)} %collective-permute-done.2.refs_5_), channel_id=1, source_target_pairs={{0,8},{1,9},{2,10},{3,11},{4,12},{5,13},{6,14},{7,15},{8,16},{9,17... | collective-permute-start | bytes 1622024 | tf_op jit(solution)/shard_map/ppermute | solution.py:59

commit v8 on v7

--- a/solution.py
+++ b/solution.py
@@ -1,3 +1,4 @@
+import dataclasses
 import functools
 
 import jax
@@ -17,6 +18,7 @@
 SCALE = 1.4426950408889634 / WIDTH**0.5
 LOW, HIGH = 1e-25, 1e30
 VMEM_LIMIT = 16 * 1024 * 1024
+COST = 512
 NT = (((1,), (1,)), ((), ()))
 NN = (((1,), (0,)), ((), ()))
 
@@ -83,7 +85,15 @@
         keys = pl.ds(pl.multiple_of(head * WIDTH, WIDTH), WIDTH)
         held[count - 2] = chosen[:, keys]
         for b, place in enumerate([*range(count - 2), count - 1]):
-            held[place] = whole[b][:, keys]
+            if len(whole[b]) == 1:
+                held[place] = whole[b][0][:, keys]
+                continue
+            for part in range(2):
+
+                @pl.when(head // 2 == part)
+                def _():
+                    there = pl.ds(pl.multiple_of((head - 2 * part) * WIDTH, WIDTH), WIDTH)
+                    held[place] = whole[b][part][:, there]
         mine = ids_down(ids_of(held[count - 1]))
         mine = jnp.concatenate([mine, mine], axis=1)
         later = lax.broadcasted_iota(jnp.int32, (TOKENS, TOKENS), 1) > lax.broadcasted_iota(
@@ -128,22 +138,23 @@
     copy.wait()
 
 
-def attend(prior, has_own, has_before, last, whole_count, *refs):
+def attend(stage, *refs):
     refs = list(refs)
     take = lambda n: [refs.pop(0) for _ in range(n)]
+    last, has_own = stage.last, stage.has_own
     which = take(1)[0] if last else None
     q_ref, own = take(2)
-    blocks = take(prior)
-    before = take(2) if has_before else None
-    whole = take(whole_count)
+    blocks = list(zip(take(len(stage.heads)), stage.heads))
+    before = [(*take(2), heads) for heads in stage.before]
+    whole = [take(n) for n in stage.whole]
     outs = take(1 if last else 3)
     mixed, picked, causal, rows_in = take(4)
     if last:
         chosen, out, sems = take(3)
-        latter = blocks.pop()
-        chosen[...] = jnp.where(which[0] == 1, latter[...], blocks[-1][...])
-        blocks[-1] = chosen
-        prior -= 1
+        latter, _ = blocks.pop()
+        former, heads = blocks.pop()
+        chosen[...] = jnp.where(which[0] == 1, latter[...], former[...])
+        blocks.append((chosen, heads))
 
     ids = ids_of(own[:, 0:WIDTH])
     down = ids_down(ids)
@@ -155,8 +166,8 @@
         column = lax.broadcasted_iota(jnp.int32, (TOKENS, TOKENS), 1)
         same = down == ids_across(ids, TOKENS)
         causal[...] = jnp.where(same & (column <= row), 1.0, 0.0)
-    for b in range(prior):
-        theirs = ids_of(blocks[b][:, 0:WIDTH])
+    for b, (block, _) in enumerate(blocks):
+        theirs = ids_of(block[:, 0:WIDTH])
         picked[b] = ids_down(jnp.where(theirs == first, 1.0, 0.0)).astype(jnp.bfloat16)
 
     def term(q, keys, b, mask=None):
@@ -171,39 +182,47 @@
     good = None
     copies = []
     lane = lax.broadcasted_iota(jnp.int32, (TOKENS, WIDTH), 1)
-    for head in range(KEY_VALUE_HEADS):
-        keys = slice(head * WIDTH, (head + 1) * WIDTH)
-        for b in range(prior):
-            mixed[b, :, 0:WIDTH] = blocks[b][TOKENS : 2 * TOKENS, keys] * picked[b]
-            mixed[b, :, WIDTH:] = picked[b]
+    for head in stage.out_heads:
+        here = []
+        for b, (block, heads) in enumerate(blocks):
+            if head in heads:
+                keys = slice(heads.index(head) * WIDTH, (heads.index(head) + 1) * WIDTH)
+                mixed[b, :, 0:WIDTH] = block[TOKENS : 2 * TOKENS, keys] * picked[b]
+                mixed[b, :, WIDTH:] = picked[b]
+                here.append((b, block, keys))
         if has_own:
-            mixed[prior, :, 0:WIDTH] = own[TOKENS : 2 * TOKENS, keys]
-            mixed[prior, :, WIDTH:] = jnp.ones((TOKENS, WIDTH), jnp.bfloat16)
+            own_keys = slice(head * WIDTH, (head + 1) * WIDTH)
+            mixed[len(blocks), :, 0:WIDTH] = own[TOKENS : 2 * TOKENS, own_keys]
+            mixed[len(blocks), :, WIDTH:] = jnp.ones((TOKENS, WIDTH), jnp.bfloat16)
+        place = stage.out_heads.index(head)
         weights = None
         for g in range(GROUP):
-            columns = slice((head * GROUP + g) * WIDTH, (head * GROUP + g + 1) * WIDTH)
-            q = q_ref[:, columns]
-            mix, weight = 0.0, 0.0
-            if prior:
-                sums = term(q, blocks[0][0:TOKENS, keys], 0)
-                for b in range(1, prior):
-                    sums = sums + term(q, blocks[b][0:TOKENS, keys], b)
-                inside = rows_in[...] > 0.5
-                mix = jnp.where(inside, sums[:, :WIDTH], 0.0)
-                weight = jnp.where(inside, sums[:, WIDTH:], 0.0)
+            column = (head * GROUP + g) * WIDTH
+            q = q_ref[:, column : column + WIDTH]
+            sums = None
+            for b, block, keys in here:
+                t = term(q, block[0:TOKENS, keys], b)
+                sums = t if sums is None else sums + t
+            inside = rows_in[...] > 0.5
+            mix = jnp.where(inside, sums[:, :WIDTH], 0.0)
+            weight = jnp.where(inside, sums[:, WIDTH:], 0.0)
             if has_own:
-                sums = term(q, own[0:TOKENS, keys], prior, causal[...])
+                sums = term(q, own[0:TOKENS, own_keys], len(blocks), causal[...])
                 mix = mix + sums[:, :WIDTH]
                 weight = weight + sums[:, WIDTH:]
-            if has_before:
-                mix = mix + before[0][:, columns]
-                weight = weight + before[1][:, head * WIDTH + g : head * WIDTH + g + 1]
+            for wide, narrow, heads in before:
+                if head in heads:
+                    i = heads.index(head)
+                    at = (i * GROUP + g) * WIDTH
+                    mix = mix + wide[:, at : at + WIDTH]
+                    weight = weight + narrow[:, i * WIDTH + g : i * WIDTH + g + 1]
             if last:
-                out[:, columns] = (mix / weight).astype(jnp.bfloat16)
+                out[:, column : column + WIDTH] = (mix / weight).astype(jnp.bfloat16)
                 fine = jnp.where((weight > LOW) & (weight < HIGH), 1.0, 0.0)
                 good = fine if good is None else jnp.minimum(good, fine)
             else:
-                outs[0][:, columns] = mix
+                at = (place * GROUP + g) * WIDTH
+                outs[0][:, at : at + WIDTH] = mix
                 weights = weight if weights is None else jnp.where(lane == g, weight, weights)
         if last:
             columns = slice(head * GROUP * WIDTH, (head + 1) * GROUP * WIDTH)
@@ -213,35 +232,53 @@
             copy.start()
             copies.append(copy)
         else:
-            outs[1][:, keys] = weights
+            outs[1][:, place * WIDTH : (place + 1) * WIDTH] = weights
     if last:
+        bad = jnp.min(good) < 0.5
         for copy in copies:
             copy.wait()
 
-        @pl.when(jnp.min(good) < 0.5)
+        @pl.when(bad)
         def _():
             general(whole, chosen, q_ref, outs[0], out, *refs, sems.at[0])
     else:
         outs[2][...] = jnp.zeros_like(outs[2])
 
 
-def attention(queries, own, blocks, has_own, before, whole, which):
-    last = which is not None
-    count = len(blocks) + has_own - last
+ALL, LOW_HEADS, HIGH_HEADS = (0, 1, 2, 3), (0, 1), (2, 3)
+NOT_LOW = (None, None, 2, 3)
+
+
+@dataclasses.dataclass(frozen=True)
+class Stage:
+    heads: tuple
+    before: tuple = ()
+    out_heads: tuple = ALL
+    has_own: bool = False
+    cost: int = COST
+    last: bool = False
+    whole: tuple = ()
+
+
+def attention(stage, queries, own, blocks, before=(), whole=(), which=None):
+    last = stage.last
+    count = len(blocks) + stage.has_own - last
+    tiles = sum(len(set(heads) & set(stage.out_heads)) for heads in stage.heads[: count + last])
     inside = pl.BlockSpec(memory_space=pltpu.VMEM)
     if last:
         out_specs = pl.BlockSpec(memory_space=pl.ANY)
         out_shape = jax.ShapeDtypeStruct(queries.shape, jnp.bfloat16)
     else:
         out_specs = [inside] * 3
+        n = len(stage.out_heads)
         out_shape = [
-            jax.ShapeDtypeStruct(queries.shape, jnp.float32),
-            jax.ShapeDtypeStruct((TOKENS, KEY_VALUE_HEADS * WIDTH), jnp.float32),
+            jax.ShapeDtypeStruct((TOKENS, n * GROUP * WIDTH), jnp.float32),
+            jax.ShapeDtypeStruct((TOKENS, n * WIDTH), jnp.float32),
             jax.ShapeDtypeStruct((8, WIDTH), jnp.float32),
         ]
     scratch = [
         pltpu.VMEM((count, TOKENS, 2 * WIDTH), jnp.bfloat16),
-        pltpu.VMEM((max(len(blocks), 1), TOKENS, WIDTH), jnp.bfloat16),
+        pltpu.VMEM((len(blocks), TOKENS, WIDTH), jnp.bfloat16),
         pltpu.VMEM((TOKENS, TOKENS), jnp.float32),
         pltpu.VMEM((TOKENS, WIDTH), jnp.float32),
     ]
@@ -255,20 +292,23 @@
             pltpu.VMEM((TOKENS, WIDTH), jnp.float32),
             pltpu.VMEM((TOKENS, WIDTH), jnp.float32),
         ]
+    stage = dataclasses.replace(stage, whole=tuple(len(parts) for parts in whole))
+    operands = [queries, own, *blocks]
+    operands += [array for sums in before for array in sums]
+    operands += [array for parts in whole for array in parts]
     return pl.pallas_call(
-        functools.partial(attend, len(blocks), has_own, bool(before), last, len(whole)),
-        in_specs=[pl.BlockSpec(memory_space=pltpu.SMEM)] * last
-        + [inside] * (2 + len(blocks) + len(before) + len(whole)),
+        functools.partial(attend, stage),
+        in_specs=[pl.BlockSpec(memory_space=pltpu.SMEM)] * last + [inside] * len(operands),
         out_specs=out_specs,
         out_shape=out_shape,
         scratch_shapes=scratch,
         compiler_params=pltpu.CompilerParams(vmem_limit_bytes=VMEM_LIMIT),
         cost_estimate=pl.CostEstimate(
-            flops=28 * 256 * 256 * count * 1024,
+            flops=7 * 256 * 256 * (tiles + 4 * stage.has_own) * stage.cost,
             bytes_accessed=4_000_000 + count * 540_000,
             transcendentals=28 * 256 * 256 * count,
         ),
-    )(*([which.astype(jnp.int32)] if last else []), queries, own, *blocks, *before, *whole)
+    )(*([which.astype(jnp.int32)] if last else []), *operands)
 
 
 def per_device(queries, key_states, value_vectors, segment_ids):
@@ -283,15 +323,30 @@
     middle = [turned_along_x(four, a) for a in (1, 3)]
     eight = two_rows_on(back)
     next_across = rows_on(across, 1)
-    *stage, done = attention(queries, own, [four], True, [], [], None)
+    *sums, done = attention(Stage((ALL,), has_own=True, cost=2048), queries, own, [four])
     eight, across, _ = lax.optimization_barrier((eight, across, done))
     far_across = rows_on(across, 2)
-    ends = [turned_along_x(jnp.where(x + a < 4, own, eight), a) for a in (1, 3)]
+    low, high = [
+        [
+            turned_along_x(jnp.where(x + a < 4, own[:, columns], eight[:, columns]), a)
+            for a in (1, 3)
+        ]
+        for columns in (slice(0, 2 * WIDTH), slice(2 * WIDTH, 4 * WIDTH))
+    ]
     early = [*middle, next_across, eight]
-    *stage, _ = attention(queries, own, early, False, stage, [], None)
-    late = [*ends, across, far_across]
-    whole = [four, *early, *ends, own]
-    return attention(queries, own, late, False, stage, whole, jnp.reshape(x < 2, (1,)))
+    *sums, _ = attention(Stage((ALL,) * 4, before=(ALL,)), queries, own, early, [sums])
+    *low_sums, _ = attention(
+        Stage((LOW_HEADS,) * 2, before=(ALL,), out_heads=LOW_HEADS), queries, own, low, [sums]
+    )
+    return attention(
+        Stage((HIGH_HEADS, HIGH_HEADS, ALL, ALL), before=(NOT_LOW, LOW_HEADS), last=True),
+        queries,
+        own,
+        [*high, across, far_across],
+        [sums, low_sums],
+        [*[(block,) for block in [four, *early]], *zip(low, high), (own,)],
+        jnp.reshape(x < 2, (1,)),
+    )
 
 
 def solution(mesh):

time: 209 us -> 218 us (1.043)
  waiting for transfers between devices: 19.1 us -> 26.2 us
    ppermute x3, waiting for transfers between devices: 8.27 us -> 20 us  [rows_on(): lax.ppermute(value, AXES, [(r, (r + 4 * rows) % 256) for r in range(256)])]
    ppermute x1, waiting for transfers between devices: 8.2 us -> 0.01 us  [turned_along_y(): return lax.ppermute(value, AXES, pairs)]
    ppermute x1, waiting for transfers between devices: 1.18 us -> 4.88 us  [two_rows_on(): return lax.ppermute(value, AXES, pairs)]
    ppermute x1, starting transfers between devices: 3.41 us -> 0.36 us  [two_rows_on(): return lax.ppermute(value, AXES, pairs)]
    ppermute x5 -> x7, starting transfers between devices: 8.17 us -> 9.39 us  [turned_along_x(): return lax.ppermute(value, AXES, pairs)]
    pallas_call x3 -> x4, Pallas kernels: 170 us -> 171 us  [attention(): pl.pallas_call(functools.partial(attend, stage), in_specs=[pl.BlockSpec(m...]
  transfers between devices with their start and end apart: 10 -> 12, of which waited for: 6 -> 4; matrix products, arithmetic and copies ran while one was open for 0% -> 0% of each run, Pallas kernels for 6% -> 7%
where the time goes in v8:
time: 218 us; the launch traced here: 217 us
  Pallas kernels  171 us (78%)
  waiting for transfers between devices  26.2 us (12%)
  starting transfers between devices  16.2 us (7%)
    pallas_call x4, Pallas kernels, attention(): pl.pallas_call(functools.partial(attend, stage), in_specs=[pl.BlockSpec(m...  171 us
    ppermute x3, waiting for transfers between devices, rows_on(): lax.ppermute(value, AXES, [(r, (r + 4 * rows) % 256) for r in range(256)])  20 us
    ppermute x7, starting transfers between devices, turned_along_x(): return lax.ppermute(value, AXES, pairs)  9.39 us
    ppermute x1, waiting for transfers between devices, two_rows_on(): return lax.ppermute(value, AXES, pairs)  4.88 us
    ppermute x1, starting transfers between devices, turned_along_y(): return lax.ppermute(value, AXES, pairs)  4.51 us
  transfers between devices with their start and end apart: 12, of which 4 were waited for; matrix products, arithmetic and copies ran while one was open for 0% of the time, Pallas kernels for 7%

profile of v8, /device:TPU:97, one launch (start us, length us, event | category | flops | bytes accessed | tf_op | source)
XLA Modules:
  0.0 216.8 jit_solution(13649226579161187094)
XLA Ops:
  0.0 0.7 convert_bitcast_fusion
  0.7 1.1 fusion.1.refs_1_.refs_2_.refs_20_
  1.8 1.4 collective-permute-start.6
  3.1 4.5 %collective-permute-start = (bf16[528,512]{1,0:T(8,128)(2,1)S(1)}, bf16[528,512]{1,0:T(8,128)(2,1)S(1)}, u32[]{:S(2)}, u32[]{:S(2)}) collective-permute-start(bf16[528,512]{1,0:T(8,128)(2,1)S(1)} %fusion.1.refs_1_.refs_2_.refs_20_), channel_id=1, source_target_pairs={{0,12},{1,13},{2,14},{3,15},{4,0},{5,1},{6,2},{7,3},{8,4},{9,5},{1... | collective-permute-start | bytes 1622024 | tf_op jit(solution)/shard_map/ppermute | solution.py:47
  7.7 2.7 %collective-permute-start.2 = (bf16[528,512]{1,0:T(8,128)(2,1)S(1)}, bf16[528,512]{1,0:T(8,128)(2,1)S(1)}, u32[]{:S(2)}, u32[]{:S(2)}) collective-permute-start(bf16[528,512]{1,0:T(8,128)(2,1)S(1)} %fusion.1.refs_1_.refs_2_.refs_20_), channel_id=1, source_target_pairs={{0,2},{1,3},{2,0},{3,1},{4,6},{5,7},{6,4},{7,5},{8,10},{9,11},{10,... | collective-permute-start | bytes 1622024 | tf_op jit(solution)/shard_map/ppermute | solution.py:37
  10.4 7.9 %collective-permute-done.6.refs_2_.refs_11_ = bf16[528,512]{1,0:T(8,128)(2,1)S(1)} collective-permute-done((bf16[528,512]{1,0:T(8,128)(2,1)S(1)}, bf16[528,512]{1,0:T(8,128)(2,1)S(1)}, u32[]{:S(2)}, u32[]{:S(2)}) %collective-permute-start.6) | collective-permute-done | bytes 540704 | tf_op jit(solution)/shard_map/ppermute | solution.py:61
  18.3 1.1 collective-permute-start.7
  19.3 1.6 collective-permute-start.8
  21.0 0.0 collective-permute-done
  21.0 0.4 collective-permute-start.1
  21.3 1.2 collective-permute-done.2.refs_5_
  22.6 0.2 collective-permute-start.9
  22.8 0.0 copy-start
  22.8 1.5 copy-done
  24.3 4.5 %shard_map.46 = (f32[256,3584]{1,0:T(8,128)S(1)}, f32[256,512]{1,0:T(8,128)S(1)}, f32[8,128]{1,0:T(8,128)}) custom-call(bf16[256,3584]{1,0:T(8,128)(2,1)S(1)} %copy-done, bf16[528,512]{1,0:T(8,128)(2,1)S(1)} %fusion.1.refs_1_.refs_2_.refs_20_, bf16[528,512]{1,0:T(8,128)(2,1)S(1)} %collective-permute-done.6.refs_2_.refs_11_), custom_call_target="tpu_custom_call" | custom-call | flops 7516192768 | bytes 5080000 | tf_op jit(solution)/shard_map/pallas_call | solution.py:299
  28.8 4.9 %collective-permute-done.1.refs_5_.refs_15_ = bf16[528,512]{1,0:T(8,128)(2,1)S(1)} collective-permute-done((bf16[528,512]{1,0:T(8,128)(2,1)S(1)}, bf16[528,512]{1,0:T(8,128)(2,1)S(1)}, u32[]{:S(2)}, u32[]{:S(2)}) %collective-permute-start.1) | collective-permute-done | bytes 540704 | tf_op jit(solution)/shard_map/ppermute | solution.py:57
  33.7 0.4 collective-permute-start.5
  34.0 0.1 broadcast_select_fusion
  34.1 2.4 %collective-permute-start.10 = (bf16[528,256]{1,0:T(8,128)(2,1)S(1)}, bf16[528,256]{1,0:T(8,128)(2,1)S(1)}, u32[]{:S(2)}, u32[]{:S(2)}) collective-permute-start(bf16[528,256]{1,0:T(8,128)(2,1)S(1)} %get-tuple-element.22), channel_id=1, source_target_pairs={{0,1},{1,2},{2,3},{3,0},{4,5},{5,6},{6,7},{7,4},{8,9},{9,10},{10,1... | collective-permute-start | bytes 811016 | tf_op jit(solution)/shard_map/ppermute | solution.py:37
  36.5 0.0 collective-permute-done.7.refs_2_.refs_12_
  36.5 1.5 collective-permute-start.11
  38.1 0.0 collective-permute-done.8.refs_3_.refs_13_
  38.1 0.0 collective-permute-start.3
  38.1 12.1 %collective-permute-done.9.refs_4_.refs_14_ = bf16[528,512]{1,0:T(8,128)(2,1)S(1)} collective-permute-done((bf16[528,512]{1,0:T(8,128)(2,1)S(1)}, bf16[528,512]{1,0:T(8,128)(2,1)S(1)}, u32[]{:S(2)}, u32[]{:S(2)}) %collective-permute-start.9) | collective-permute-done | bytes 540704 | tf_op jit(solution)/shard_map/ppermute | solution.py:61
  50.2 0.0 collective-permute-start.4
  50.2 8.9 %shard_map.47 = (f32[256,3584]{1,0:T(8,128)S(1)}, f32[256,512]{1,0:T(8,128)S(1)}, f32[8,128]{1,0:T(8,128)}) custom-call(bf16[256,3584]{1,0:T(8,128)(2,1)S(1)} %copy-done, bf16[528,512]{1,0:T(8,128)(2,1)S(1)} %fusion.1.refs_1_.refs_2_.refs_20_, bf16[528,512]{1,0:T(8,128)(2,1)S(1)} %collective-permute-done.7.refs_2_.refs_12_, ...), custom_call_target="tpu_custom_call" | custom-call | flops 3758096384 | bytes 6160000 | tf_op jit(solution)/shard_map/pallas_call | solution.py:299
  59.1 0.0 collective-permute-done.10.refs_2_.refs_16_
  59.2 0.0 collective-permute-done.11.refs_3_.refs_18_
  59.2 2.6 %shard_map.48 = (f32[256,1792]{1,0:T(8,128)S(1)}, f32[256,256]{1,0:T(8,128)S(1)}, f32[8,128]{1,0:T(8,128)}) custom-call(bf16[256,3584]{1,0:T(8,128)(2,1)S(1)} %copy-done, bf16[528,512]{1,0:T(8,128)(2,1)S(1)} %fusion.1.refs_1_.refs_2_.refs_20_, bf16[528,256]{1,0:T(8,128)(2,1)S(1)} %collective-permute-done.10.refs_2_.refs_16_, ...), custom_call_target="tpu_custom_call" | custom-call | flops 939524096 | bytes 5080000 | tf_op jit(solution)/shard_map/pallas_call | solution.py:299
  61.7 0.0 collective-permute-done.3.refs_3_.refs_17_
  61.7 0.0 collective-permute-done.4.refs_4_.refs_19_
  61.8 0.0 collective-permute-done.5.refs_6_
  61.8 154.9 %shard_map.49 = bf16[256,3584]{1,0:T(8,128)(2,1)} custom-call(s32[1]{0:T(128)} %bitcast.refs_0_, bf16[256,3584]{1,0:T(8,128)(2,1)S(1)} %copy-done, bf16[528,512]{1,0:T(8,128)(2,1)S(1)} %fusion.1.refs_1_.refs_2_.refs_20_, bf16[528,256]{1,0:T(8,128)(2,1)S(1)} %collective-permute-done.3.refs_3_.refs_17_, ...), custom_call_target="tpu_custom_call" | custom-call | flops 2818572288 | bytes 5620000 | tf_op jit(solution)/shard_map/pallas_call | solution.py:299
  (2 shorter events, 0.0 us)
Async XLA Ops:
  1.8 16.5 %collective-permute-start.6 = (bf16[528,512]{1,0:T(8,128)(2,1)S(1)}, bf16[528,512]{1,0:T(8,128)(2,1)S(1)}, u32[]{:S(2)}, u32[]{:S(2)}) collective-permute-start(bf16[528,512]{1,0:T(8,128)(2,1)S(1)} %fusion.1.refs_1_.refs_2_.refs_20_), channel_id=1, source_target_pairs={{0,4},{1,5},{2,6},{3,7},{4,8},{5,9},{6,10},{7,11},{8,12},{9,13},{1... | collective-permute-start | bytes 1622024 | tf_op jit(solution)/shard_map/ppermute | solution.py:61
  3.1 17.8 %collective-permute-start = (bf16[528,512]{1,0:T(8,128)(2,1)S(1)}, bf16[528,512]{1,0:T(8,128)(2,1)S(1)}, u32[]{:S(2)}, u32[]{:S(2)}) collective-permute-start(bf16[528,512]{1,0:T(8,128)(2,1)S(1)} %fusion.1.refs_1_.refs_2_.refs_20_), channel_id=1, source_target_pairs={{0,12},{1,13},{2,14},{3,15},{4,0},{5,1},{6,2},{7,3},{8,4},{9,5},{1... | collective-permute-start | bytes 1622024 | tf_op jit(solution)/shard_map/ppermute | solution.py:47
  7.7 14.9 %collective-permute-start.2 = (bf16[528,512]{1,0:T(8,128)(2,1)S(1)}, bf16[528,512]{1,0:T(8,128)(2,1)S(1)}, u32[]{:S(2)}, u32[]{:S(2)}) collective-permute-start(bf16[528,512]{1,0:T(8,128)(2,1)S(1)} %fusion.1.refs_1_.refs_2_.refs_20_), channel_id=1, source_target_pairs={{0,2},{1,3},{2,0},{3,1},{4,6},{5,7},{6,4},{7,5},{8,10},{9,11},{10,... | collective-permute-start | bytes 1622024 | tf_op jit(solution)/shard_map/ppermute | solution.py:37
  18.3 18.3 %collective-permute-start.7 = (bf16[528,512]{1,0:T(8,128)(2,1)S(1)}, bf16[528,512]{1,0:T(8,128)(2,1)S(1)}, u32[]{:S(2)}, u32[]{:S(2)}) collective-permute-start(bf16[528,512]{1,0:T(8,128)(2,1)S(1)} %collective-permute-done.6.refs_2_.refs_11_), channel_id=1, source_target_pairs={{0,1},{1,2},{2,3},{3,0},{4,5},{5,6},{6,7},{7,4},{8,9},{9,10},{10,1... | collective-permute-start | bytes 1622024 | tf_op jit(solution)/shard_map/ppermute | solution.py:37
  19.3 18.7 %collective-permute-start.8 = (bf16[528,512]{1,0:T(8,128)(2,1)S(1)}, bf16[528,512]{1,0:T(8,128)(2,1)S(1)}, u32[]{:S(2)}, u32[]{:S(2)}) collective-permute-start(bf16[528,512]{1,0:T(8,128)(2,1)S(1)} %collective-permute-done.6.refs_2_.refs_11_), channel_id=1, source_target_pairs={{0,3},{1,0},{2,1},{3,2},{4,7},{5,4},{6,5},{7,6},{8,11},{9,8},{10,9... | collective-permute-start | bytes 1622024 | tf_op jit(solution)/shard_map/ppermute | solution.py:37
  21.0 12.7 %collective-permute-start.1 = (bf16[528,512]{1,0:T(8,128)(2,1)S(1)}, bf16[528,512]{1,0:T(8,128)(2,1)S(1)}, u32[]{:S(2)}, u32[]{:S(2)}) collective-permute-start(bf16[528,512]{1,0:T(8,128)(2,1)S(1)} %collective-permute-done), channel_id=1, source_target_pairs={{12,8},{13,9},{14,10},{15,11},{0,12},{1,13},{2,14},{3,15},{4,16},{... | collective-permute-start | bytes 1622024 | tf_op jit(solution)/shard_map/ppermute | solution.py:57
  22.6 27.7 %collective-permute-start.9 = (bf16[528,512]{1,0:T(8,128)(2,1)S(1)}, bf16[528,512]{1,0:T(8,128)(2,1)S(1)}, u32[]{:S(2)}, u32[]{:S(2)}) collective-permute-start(bf16[528,512]{1,0:T(8,128)(2,1)S(1)} %collective-permute-done.2.refs_5_), channel_id=1, source_target_pairs={{0,4},{1,5},{2,6},{3,7},{4,8},{5,9},{6,10},{7,11},{8,12},{9,13},{1... | collective-permute-start | bytes 1622024 | tf_op jit(solution)/shard_map/ppermute | solution.py:61
  22.8 1.5 copy-start
  33.7 28.1 %collective-permute-start.5 = (bf16[528,512]{1,0:T(8,128)(2,1)S(1)}, bf16[528,512]{1,0:T(8,128)(2,1)S(1)}, u32[]{:S(2)}, u32[]{:S(2)}) collective-permute-start(bf16[528,512]{1,0:T(8,128)(2,1)S(1)} %collective-permute-done.2.refs_5_), channel_id=1, source_target_pairs={{0,8},{1,9},{2,10},{3,11},{4,12},{5,13},{6,14},{7,15},{8,16},{9,17... | collective-permute-start | bytes 1622024 | tf_op jit(solution)/shard_map/ppermute | solution.py:61
  34.1 25.0 %collective-permute-start.10 = (bf16[528,256]{1,0:T(8,128)(2,1)S(1)}, bf16[528,256]{1,0:T(8,128)(2,1)S(1)}, u32[]{:S(2)}, u32[]{:S(2)}) collective-permute-start(bf16[528,256]{1,0:T(8,128)(2,1)S(1)} %get-tuple-element.22), channel_id=1, source_target_pairs={{0,1},{1,2},{2,3},{3,0},{4,5},{5,6},{6,7},{7,4},{8,9},{9,10},{10,1... | collective-permute-start | bytes 811016 | tf_op jit(solution)/shard_map/ppermute | solution.py:37
  36.5 22.6 %collective-permute-start.11 = (bf16[528,256]{1,0:T(8,128)(2,1)S(1)}, bf16[528,256]{1,0:T(8,128)(2,1)S(1)}, u32[]{:S(2)}, u32[]{:S(2)}) collective-permute-start(bf16[528,256]{1,0:T(8,128)(2,1)S(1)} %get-tuple-element.21), channel_id=1, source_target_pairs={{0,3},{1,0},{2,1},{3,2},{4,7},{5,4},{6,5},{7,6},{8,11},{9,8},{10,9... | collective-permute-start | bytes 811016 | tf_op jit(solution)/shard_map/ppermute | solution.py:37
  38.1 23.7 %collective-permute-start.3 = (bf16[528,256]{1,0:T(8,128)(2,1)S(1)}, bf16[528,256]{1,0:T(8,128)(2,1)S(1)}, u32[]{:S(2)}, u32[]{:S(2)}) collective-permute-start(bf16[528,256]{1,0:T(8,128)(2,1)S(1)} %get-tuple-element.23), channel_id=1, source_target_pairs={{0,1},{1,2},{2,3},{3,0},{4,5},{5,6},{6,7},{7,4},{8,9},{9,10},{10,1... | collective-permute-start | bytes 811016 | tf_op jit(solution)/shard_map/ppermute | solution.py:37
  50.2 11.5 %collective-permute-start.4 = (bf16[528,256]{1,0:T(8,128)(2,1)S(1)}, bf16[528,256]{1,0:T(8,128)(2,1)S(1)}, u32[]{:S(2)}, u32[]{:S(2)}) collective-permute-start(bf16[528,256]{1,0:T(8,128)(2,1)S(1)} %get-tuple-element.24), channel_id=1, source_target_pairs={{0,3},{1,0},{2,1},{3,2},{4,7},{5,4},{6,5},{7,6},{8,11},{9,8},{10,9... | collective-permute-start | bytes 811016 | tf_op jit(solution)/shard_map/ppermute | solution.py:37

commit v9 on v7

--- a/solution.py
+++ b/solution.py
@@ -16,7 +16,7 @@
 AXES = ("dp", "seq")
 SCALE = 1.4426950408889634 / WIDTH**0.5
 LOW, HIGH = 1e-25, 1e30
-VMEM_LIMIT = 16 * 1024 * 1024
+VMEM_LIMIT = 20 * 1024 * 1024
 NT = (((1,), (1,)), ((), ()))
 NN = (((1,), (0,)), ((), ()))
 
@@ -139,90 +139,150 @@
     outs = take(1 if last else 3)
     mixed, picked, causal, rows_in = take(4)
     if last:
-        chosen, out, sems = take(3)
+        chosen, out, sems, total, narrow = take(5)
         latter = blocks.pop()
         chosen[...] = jnp.where(which[0] == 1, latter[...], blocks[-1][...])
         blocks[-1] = chosen
         prior -= 1
+    else:
+        total, narrow = outs[0], outs[1]
 
     ids = ids_of(own[:, 0:WIDTH])
     down = ids_down(ids)
     first = ids[0:1, 0:1]
     rows_in[...] = jnp.where(down == first, 1.0, 0.0)
+    lane = lax.broadcasted_iota(jnp.int32, (TOKENS, WIDTH), 1)
+    hits = [
+        jnp.where(ids_of(block[:, 0:WIDTH]) == first, 1.0, 0.0) for block in blocks
+    ]
+
+    def term(q, keys, values, mask=None):
+        s = lax.dot_general(q, keys, NT, preferred_element_type=jnp.float32)
+        p = jnp.exp2(s * SCALE)
+        if mask is not None:
+            p = p * mask
+        return lax.dot_general(
+            p.astype(jnp.bfloat16), values[...], NN, preferred_element_type=jnp.float32
+        )
+
+    def pick(b):
+        picked[b] = ids_down(hits[b]).astype(jnp.bfloat16)
+
+    def mix_in(b, keys):
+        mixed[b, :, 0:WIDTH] = blocks[b][TOKENS : 2 * TOKENS, keys] * picked[b]
+        mixed[b, :, WIDTH:] = picked[b]
+
+    def masked_term(b, q, keys):
+        t = term(q, blocks[b][0:TOKENS, keys], mixed.at[b])
+        inside = rows_in[...] > 0.5
+        return jnp.where(inside, t[:, :WIDTH], 0.0), jnp.where(inside, t[:, WIDTH:], 0.0)
+
+    def heads():
+        for head in range(KEY_VALUE_HEADS):
+            keys = slice(head * WIDTH, (head + 1) * WIDTH)
+            columns = [
+                slice((head * GROUP + g) * WIDTH, (head * GROUP + g + 1) * WIDTH)
+                for g in range(GROUP)
+            ]
+            yield head, keys, columns
+
+    def add(b, wide_from, narrow_from):
+        pick(b)
+        for head, keys, columns in heads():
+            mix_in(b, keys)
+            weights = narrow_from[:, keys]
+            for g in range(GROUP):
+                mix, weight = masked_term(b, q_ref[:, columns[g]], keys)
+                total[:, columns[g]] = wide_from[:, columns[g]] + mix
+                weights = weights + jnp.where(lane == g, weight, 0.0)
+            narrow[:, keys] = weights
+
+    def finish(b):
+        good = None
+        if b is not None:
+            pick(b)
+        for head, keys, columns in heads():
+            if b is not None:
+                mix_in(b, keys)
+            for g in range(GROUP):
+                mix = total[:, columns[g]]
+                weight = jnp.broadcast_to(
+                    narrow[:, head * WIDTH + g : head * WIDTH + g + 1], (TOKENS, WIDTH)
+                )
+                if b is not None:
+                    more, extra = masked_term(b, q_ref[:, columns[g]], keys)
+                    mix, weight = mix + more, weight + extra
+                out[:, columns[g]] = (mix / weight).astype(jnp.bfloat16)
+                fine = jnp.where((weight > LOW) & (weight < HIGH), 1.0, 0.0)
+                good = fine if good is None else jnp.minimum(good, fine)
+            at = slice(columns[0].start, columns[-1].stop)
+            pltpu.make_async_copy(out.at[:, at], outs[0].at[:, at], sems.at[head]).start()
+        rows_in[...] = good
+
     if has_own:
         down = jnp.concatenate([down, down], axis=1)
         row = lax.broadcasted_iota(jnp.int32, (TOKENS, TOKENS), 0)
         column = lax.broadcasted_iota(jnp.int32, (TOKENS, TOKENS), 1)
         same = down == ids_across(ids, TOKENS)
         causal[...] = jnp.where(same & (column <= row), 1.0, 0.0)
-    for b in range(prior):
-        theirs = ids_of(blocks[b][:, 0:WIDTH])
-        picked[b] = ids_down(jnp.where(theirs == first, 1.0, 0.0)).astype(jnp.bfloat16)
-
-    def term(q, keys, b, mask=None):
-        s = lax.dot_general(q, keys, NT, preferred_element_type=jnp.float32)
-        p = jnp.exp2(s * SCALE)
-        if mask is not None:
-            p = p * mask
-        return lax.dot_general(
-            p.astype(jnp.bfloat16), mixed[b], NN, preferred_element_type=jnp.float32
-        )
-
-    good = None
-    copies = []
-    lane = lax.broadcasted_iota(jnp.int32, (TOKENS, WIDTH), 1)
-    for head in range(KEY_VALUE_HEADS):
-        keys = slice(head * WIDTH, (head + 1) * WIDTH)
         for b in range(prior):
-            mixed[b, :, 0:WIDTH] = blocks[b][TOKENS : 2 * TOKENS, keys] * picked[b]
-            mixed[b, :, WIDTH:] = picked[b]
-        if has_own:
+            pick(b)
+        for head, keys, columns in heads():
             mixed[prior, :, 0:WIDTH] = own[TOKENS : 2 * TOKENS, keys]
             mixed[prior, :, WIDTH:] = jnp.ones((TOKENS, WIDTH), jnp.bfloat16)
-        weights = None
-        for g in range(GROUP):
-            columns = slice((head * GROUP + g) * WIDTH, (head * GROUP + g + 1) * WIDTH)
-            q = q_ref[:, columns]
-            mix, weight = 0.0, 0.0
-            if prior:
-                sums = term(q, blocks[0][0:TOKENS, keys], 0)
-                for b in range(1, prior):
-                    sums = sums + term(q, blocks[b][0:TOKENS, keys], b)
-                inside = rows_in[...] > 0.5
-                mix = jnp.where(inside, sums[:, :WIDTH], 0.0)
-                weight = jnp.where(inside, sums[:, WIDTH:], 0.0)
-            if has_own:
-                sums = term(q, own[0:TOKENS, keys], prior, causal[...])
-                mix = mix + sums[:, :WIDTH]
-                weight = weight + sums[:, WIDTH:]
-            if has_before:
-                mix = mix + before[0][:, columns]
-                weight = weight + before[1][:, head * WIDTH + g : head * WIDTH + g + 1]
-            if last:
-                out[:, columns] = (mix / weight).astype(jnp.bfloat16)
-                fine = jnp.where((weight > LOW) & (weight < HIGH), 1.0, 0.0)
-                good = fine if good is None else jnp.minimum(good, fine)
-            else:
-                outs[0][:, columns] = mix
-                weights = weight if weights is None else jnp.where(lane == g, weight, weights)
-        if last:
-            columns = slice(head * GROUP * WIDTH, (head + 1) * GROUP * WIDTH)
-            copy = pltpu.make_async_copy(
-                out.at[:, columns], outs[0].at[:, columns], sems.at[head]
-            )
-            copy.start()
-            copies.append(copy)
-        else:
-            outs[1][:, keys] = weights
-    if last:
-        for copy in copies:
-            copy.wait()
-
-        @pl.when(jnp.min(good) < 0.5)
-        def _():
-            general(whole, chosen, q_ref, outs[0], out, *refs, sems.at[0])
-    else:
+            for b in range(prior):
+                mix_in(b, keys)
+            weights = jnp.zeros((TOKENS, WIDTH), jnp.float32)
+            for g in range(GROUP):
+                q = q_ref[:, columns[g]]
+                t = term(q, own[0:TOKENS, keys], mixed.at[prior], causal[...])
+                mix, weight = t[:, :WIDTH], t[:, WIDTH:]
+                for b in range(prior):
+                    more, extra = masked_term(b, q, keys)
+                    mix, weight = mix + more, weight + extra
+                total[:, columns[g]] = mix
+                weights = jnp.where(lane == g, weight, weights)
+            narrow[:, keys] = weights
         outs[2][...] = jnp.zeros_like(outs[2])
+        return
+
+    needed = [jnp.max(hit) > 0.5 for hit in hits]
+
+    @pl.when(needed[0])
+    def _():
+        add(0, *before)
+
+    @pl.when(~needed[0])
+    def _():
+        total[...] = before[0][...]
+        narrow[...] = before[1][...]
+
+    for b in range(1, prior - last):
+
+        @pl.when(needed[b])
+        def _(b=b):
+            add(b, total, narrow)
+
+    if not last:
+        outs[2][...] = jnp.zeros_like(outs[2])
+        return
+
+    @pl.when(needed[-1])
+    def _():
+        finish(prior - 1)
+
+    @pl.when(~needed[-1])
+    def _():
+        finish(None)
+
+    bad = jnp.min(rows_in[...]) < 0.5
+    for head, keys, columns in heads():
+        at = slice(columns[0].start, columns[-1].stop)
+        pltpu.make_async_copy(out.at[:, at], outs[0].at[:, at], sems.at[head]).wait()
+
+    @pl.when(bad)
+    def _():
+        general(whole, chosen, q_ref, outs[0], out, *refs, sems.at[0])
 
 
 def attention(queries, own, blocks, has_own, before, whole, which):
@@ -250,6 +310,8 @@
             pltpu.VMEM((ROWS, KEY_VALUE_HEADS * WIDTH), jnp.bfloat16),
             pltpu.VMEM(queries.shape, jnp.bfloat16),
             pltpu.SemaphoreType.DMA((KEY_VALUE_HEADS,)),
+            pltpu.VMEM(queries.shape, jnp.float32),
+            pltpu.VMEM((TOKENS, KEY_VALUE_HEADS * WIDTH), jnp.float32),
             pltpu.VMEM((len(whole) + 1, ROWS, WIDTH), jnp.bfloat16),
             pltpu.VMEM((TOKENS, WIDTH), jnp.float32),
             pltpu.VMEM((TOKENS, WIDTH), jnp.float32),

time: 209 us -> 208 us (level)
  the two profiles are of different devices: /device:TPU:97 before, /device:TPU:199 now
where the time goes in v9:
time: 208 us; the launch traced here: 207 us
  Pallas kernels  163 us (78%)
  waiting for transfers between devices  30.5 us (15%)
  starting transfers between devices  10.6 us (5%)
    pallas_call x3, Pallas kernels, attention(): pl.pallas_call(functools.partial(attend, len(blocks), has_own, bool(befor...  163 us
    ppermute x5, waiting for transfers between devices, turned_along_x(): return lax.ppermute(value, AXES, pairs)  9.98 us
    ppermute x1, waiting for transfers between devices, turned_along_y(): return lax.ppermute(value, AXES, pairs)  9.81 us
    ppermute x3, waiting for transfers between devices, rows_on(): lax.ppermute(value, AXES, [(r, (r + 4 * rows) % 256) for r in range(256)])  7.6 us
  transfers between devices with their start and end apart: 10, of which 9 were waited for; matrix products, arithmetic and copies ran while one was open for 0% of the time, Pallas kernels for 3%

profile of v9, /device:TPU:199, one launch (start us, length us, event | category | flops | bytes accessed | tf_op | source)
XLA Modules:
  0.0 207.4 jit_solution(18261580094718940156)
XLA Ops:
  0.0 0.7 convert_bitcast_fusion
  0.7 1.1 fusion.1.refs_1_.refs_2_.refs_16_
  1.8 2.8 %collective-permute-start = (bf16[528,512]{1,0:T(8,128)(2,1)S(1)}, bf16[528,512]{1,0:T(8,128)(2,1)S(1)}, u32[]{:S(2)}, u32[]{:S(2)}) collective-permute-start(bf16[528,512]{1,0:T(8,128)(2,1)S(1)} %fusion.1.refs_1_.refs_2_.refs_16_), channel_id=1, source_target_pairs={{0,12},{1,13},{2,14},{3,15},{4,0},{5,1},{6,2},{7,3},{8,4},{9,5},{1... | collective-permute-start | bytes 1622024 | tf_op jit(solution)/shard_map/ppermute | solution.py:45
  4.6 0.0 collective-permute-start.6
  4.6 1.1 collective-permute-start.2
  5.7 9.8 %collective-permute-done = bf16[528,512]{1,0:T(8,128)(2,1)S(1)} collective-permute-done((bf16[528,512]{1,0:T(8,128)(2,1)S(1)}, bf16[528,512]{1,0:T(8,128)(2,1)S(1)}, u32[]{:S(2)}, u32[]{:S(2)}) %collective-permute-start) | collective-permute-done | bytes 540704 | tf_op jit(solution)/shard_map/ppermute | solution.py:45
  15.5 3.4 %collective-permute-start.1 = (bf16[528,512]{1,0:T(8,128)(2,1)S(1)}, bf16[528,512]{1,0:T(8,128)(2,1)S(1)}, u32[]{:S(2)}, u32[]{:S(2)}) collective-permute-start(bf16[528,512]{1,0:T(8,128)(2,1)S(1)} %collective-permute-done), channel_id=1, source_target_pairs={{12,8},{13,9},{14,10},{15,11},{0,12},{1,13},{2,14},{3,15},{4,16},{... | collective-permute-start | bytes 1622024 | tf_op jit(solution)/shard_map/ppermute | solution.py:55
  18.9 1.4 collective-permute-done.6.refs_2_.refs_9_
  20.4 0.2 collective-permute-start.7
  20.6 1.3 collective-permute-start.8
  21.9 0.0 collective-permute-done.2.refs_5_
  21.9 0.0 collective-permute-start.9
  21.9 0.0 copy-start
  21.9 1.5 copy-done
  23.4 4.4 %shard_map.46 = (f32[256,3584]{1,0:T(8,128)S(1)}, f32[256,512]{1,0:T(8,128)S(1)}, f32[8,128]{1,0:T(8,128)}) custom-call(bf16[256,3584]{1,0:T(8,128)(2,1)S(1)} %copy-done, bf16[528,512]{1,0:T(8,128)(2,1)S(1)} %fusion.1.refs_1_.refs_2_.refs_16_, bf16[528,512]{1,0:T(8,128)(2,1)S(1)} %collective-permute-done.6.refs_2_.refs_9_), custom_call_target="tpu_custom_call" | custom-call | flops 3758096384 | bytes 5080000 | tf_op jit(solution)/shard_map/pallas_call | solution.py:320
  27.7 3.1 %collective-permute-done.1.refs_5_.refs_13_ = bf16[528,512]{1,0:T(8,128)(2,1)S(1)} collective-permute-done((bf16[528,512]{1,0:T(8,128)(2,1)S(1)}, bf16[528,512]{1,0:T(8,128)(2,1)S(1)}, u32[]{:S(2)}, u32[]{:S(2)}) %collective-permute-start.1) | collective-permute-done | bytes 540704 | tf_op jit(solution)/shard_map/ppermute | solution.py:55
  30.8 0.1 broadcast_select_fusion
  30.9 0.3 collective-permute-start.3
  31.2 1.3 collective-permute-start.4
  32.5 1.4 collective-permute-done.7.refs_2_.refs_10_
  33.9 0.3 collective-permute-start.5
  34.1 0.8 collective-permute-done.8.refs_3_.refs_11_
  34.9 3.0 %collective-permute-done.9.refs_4_.refs_12_ = bf16[528,512]{1,0:T(8,128)(2,1)S(1)} collective-permute-done((bf16[528,512]{1,0:T(8,128)(2,1)S(1)}, bf16[528,512]{1,0:T(8,128)(2,1)S(1)}, u32[]{:S(2)}, u32[]{:S(2)}) %collective-permute-start.9) | collective-permute-done | bytes 540704 | tf_op jit(solution)/shard_map/ppermute | solution.py:59
  37.9 1.0 shard_map.47
  39.0 6.5 %collective-permute-done.3.refs_3_.refs_14_ = bf16[528,512]{1,0:T(8,128)(2,1)S(1)} collective-permute-done((bf16[528,512]{1,0:T(8,128)(2,1)S(1)}, bf16[528,512]{1,0:T(8,128)(2,1)S(1)}, u32[]{:S(2)}, u32[]{:S(2)}) %collective-permute-start.3) | collective-permute-done | bytes 540704 | tf_op jit(solution)/shard_map/ppermute | solution.py:35
  45.4 1.3 collective-permute-done.4.refs_4_.refs_15_
  46.8 3.2 %collective-permute-done.5.refs_6_ = bf16[528,512]{1,0:T(8,128)(2,1)S(1)} collective-permute-done((bf16[528,512]{1,0:T(8,128)(2,1)S(1)}, bf16[528,512]{1,0:T(8,128)(2,1)S(1)}, u32[]{:S(2)}, u32[]{:S(2)}) %collective-permute-start.5) | collective-permute-done | bytes 540704 | tf_op jit(solution)/shard_map/ppermute | solution.py:59
  49.9 157.3 %shard_map.48 = bf16[256,3584]{1,0:T(8,128)(2,1)} custom-call(s32[1]{0:T(128)} %bitcast.refs_0_, bf16[256,3584]{1,0:T(8,128)(2,1)S(1)} %copy-done, bf16[528,512]{1,0:T(8,128)(2,1)S(1)} %fusion.1.refs_1_.refs_2_.refs_16_, bf16[528,512]{1,0:T(8,128)(2,1)S(1)} %collective-permute-done.3.refs_3_.refs_14_, ...), custom_call_target="tpu_custom_call" | custom-call | flops 5637144576 | bytes 5620000 | tf_op jit(solution)/shard_map/pallas_call | solution.py:320
  (2 shorter events, 0.0 us)
Async XLA Ops:
  1.8 13.8 %collective-permute-start = (bf16[528,512]{1,0:T(8,128)(2,1)S(1)}, bf16[528,512]{1,0:T(8,128)(2,1)S(1)}, u32[]{:S(2)}, u32[]{:S(2)}) collective-permute-start(bf16[528,512]{1,0:T(8,128)(2,1)S(1)} %fusion.1.refs_1_.refs_2_.refs_16_), channel_id=1, source_target_pairs={{0,12},{1,13},{2,14},{3,15},{4,0},{5,1},{6,2},{7,3},{8,4},{9,5},{1... | collective-permute-start | bytes 1622024 | tf_op jit(solution)/shard_map/ppermute | solution.py:45
  4.6 15.8 %collective-permute-start.6 = (bf16[528,512]{1,0:T(8,128)(2,1)S(1)}, bf16[528,512]{1,0:T(8,128)(2,1)S(1)}, u32[]{:S(2)}, u32[]{:S(2)}) collective-permute-start(bf16[528,512]{1,0:T(8,128)(2,1)S(1)} %fusion.1.refs_1_.refs_2_.refs_16_), channel_id=1, source_target_pairs={{0,4},{1,5},{2,6},{3,7},{4,8},{5,9},{6,10},{7,11},{8,12},{9,13},{1... | collective-permute-start | bytes 1622024 | tf_op jit(solution)/shard_map/ppermute | solution.py:59
  4.6 17.3 %collective-permute-start.2 = (bf16[528,512]{1,0:T(8,128)(2,1)S(1)}, bf16[528,512]{1,0:T(8,128)(2,1)S(1)}, u32[]{:S(2)}, u32[]{:S(2)}) collective-permute-start(bf16[528,512]{1,0:T(8,128)(2,1)S(1)} %fusion.1.refs_1_.refs_2_.refs_16_), channel_id=1, source_target_pairs={{0,2},{1,3},{2,0},{3,1},{4,6},{5,7},{6,4},{7,5},{8,10},{9,11},{10,... | collective-permute-start | bytes 1622024 | tf_op jit(solution)/shard_map/ppermute | solution.py:35
  15.5 15.3 %collective-permute-start.1 = (bf16[528,512]{1,0:T(8,128)(2,1)S(1)}, bf16[528,512]{1,0:T(8,128)(2,1)S(1)}, u32[]{:S(2)}, u32[]{:S(2)}) collective-permute-start(bf16[528,512]{1,0:T(8,128)(2,1)S(1)} %collective-permute-done), channel_id=1, source_target_pairs={{12,8},{13,9},{14,10},{15,11},{0,12},{1,13},{2,14},{3,15},{4,16},{... | collective-permute-start | bytes 1622024 | tf_op jit(solution)/shard_map/ppermute | solution.py:55
  20.4 13.5 %collective-permute-start.7 = (bf16[528,512]{1,0:T(8,128)(2,1)S(1)}, bf16[528,512]{1,0:T(8,128)(2,1)S(1)}, u32[]{:S(2)}, u32[]{:S(2)}) collective-permute-start(bf16[528,512]{1,0:T(8,128)(2,1)S(1)} %collective-permute-done.6.refs_2_.refs_9_), channel_id=1, source_target_pairs={{0,1},{1,2},{2,3},{3,0},{4,5},{5,6},{6,7},{7,4},{8,9},{9,10},{10,1... | collective-permute-start | bytes 1622024 | tf_op jit(solution)/shard_map/ppermute | solution.py:35
  20.6 14.4 %collective-permute-start.8 = (bf16[528,512]{1,0:T(8,128)(2,1)S(1)}, bf16[528,512]{1,0:T(8,128)(2,1)S(1)}, u32[]{:S(2)}, u32[]{:S(2)}) collective-permute-start(bf16[528,512]{1,0:T(8,128)(2,1)S(1)} %collective-permute-done.6.refs_2_.refs_9_), channel_id=1, source_target_pairs={{0,3},{1,0},{2,1},{3,2},{4,7},{5,4},{6,5},{7,6},{8,11},{9,8},{10,9... | collective-permute-start | bytes 1622024 | tf_op jit(solution)/shard_map/ppermute | solution.py:35
  21.9 16.1 %collective-permute-start.9 = (bf16[528,512]{1,0:T(8,128)(2,1)S(1)}, bf16[528,512]{1,0:T(8,128)(2,1)S(1)}, u32[]{:S(2)}, u32[]{:S(2)}) collective-permute-start(bf16[528,512]{1,0:T(8,128)(2,1)S(1)} %collective-permute-done.2.refs_5_), channel_id=1, source_target_pairs={{0,4},{1,5},{2,6},{3,7},{4,8},{5,9},{6,10},{7,11},{8,12},{9,13},{1... | collective-permute-start | bytes 1622024 | tf_op jit(solution)/shard_map/ppermute | solution.py:59
  21.9 1.5 copy-start
  30.9 14.5 %collective-permute-start.3 = (bf16[528,512]{1,0:T(8,128)(2,1)S(1)}, bf16[528,512]{1,0:T(8,128)(2,1)S(1)}, u32[]{:S(2)}, u32[]{:S(2)}) collective-permute-start(bf16[528,512]{1,0:T(8,128)(2,1)S(1)} %get-tuple-element.18), channel_id=1, source_target_pairs={{0,1},{1,2},{2,3},{3,0},{4,5},{5,6},{6,7},{7,4},{8,9},{9,10},{10,1... | collective-permute-start | bytes 1622024 | tf_op jit(solution)/shard_map/ppermute | solution.py:35
  31.2 15.6 %collective-permute-start.4 = (bf16[528,512]{1,0:T(8,128)(2,1)S(1)}, bf16[528,512]{1,0:T(8,128)(2,1)S(1)}, u32[]{:S(2)}, u32[]{:S(2)}) collective-permute-start(bf16[528,512]{1,0:T(8,128)(2,1)S(1)} %get-tuple-element.17), channel_id=1, source_target_pairs={{0,3},{1,0},{2,1},{3,2},{4,7},{5,4},{6,5},{7,6},{8,11},{9,8},{10,9... | collective-permute-start | bytes 1622024 | tf_op jit(solution)/shard_map/ppermute | solution.py:35
  33.9 16.1 %collective-permute-start.5 = (bf16[528,512]{1,0:T(8,128)(2,1)S(1)}, bf16[528,512]{1,0:T(8,128)(2,1)S(1)}, u32[]{:S(2)}, u32[]{:S(2)}) collective-permute-start(bf16[528,512]{1,0:T(8,128)(2,1)S(1)} %collective-permute-done.2.refs_5_), channel_id=1, source_target_pairs={{0,8},{1,9},{2,10},{3,11},{4,12},{5,13},{6,14},{7,15},{8,16},{9,17... | collective-permute-start | bytes 1622024 | tf_op jit(solution)/shard_map/ppermute | solution.py:59
